TPU v7x, 256 devices: a whole 4x4x8 slice. The times are simulated.
256 devices in a mesh: role: 2 (over x_hi), grp: 8 (over z), blk: 16 (over y, x_lo, core).
Axes of the slice: x: 4 (x_hi: 2, x_lo: 2; x = x_hi * 2 + x_lo), y: 4, z: 8, core: 2. Of those that a mesh axis runs over, the one named last changes fastest.
Arguments:
- prompt_hidden: bfloat16 [16384, 8192], P(('grp', 'blk'), 'role'), parts along dimension 0, may hold values from -6 to 6
- prompt_qkv: bfloat16 [16384, 5120], P(('grp', 'blk')), parts along dimension 0, may hold values from -6 to 6
- block_tenant: int32 [128], P(('grp', 'blk')), parts along dimension 0, may hold values from 0 to 1
- row_hidden: bfloat16 [32, 8192], P('grp'), parts along dimension 0, may hold values from -6 to 6
- row_qkv: bfloat16 [32, 5120], P('grp'), parts along dimension 0, may hold values from -6 to 6
- row_tenant: int32 [32], P('grp'), parts along dimension 0, may hold values from 0 to 1, as said below
- row_cache: bfloat16 [24, 2048, 1024], P('grp', 'blk'), parts along dimension 0, may hold values from -6 to 6
- row_lengths: int32 [24], P('grp'), parts along dimension 0, may hold values from 1 to 2048, as said below
- qkv_down: bfloat16 [2, 8192, 192], P(None, ('role', 'blk')), may hold values from -0.0625 to 0.0625
- qkv_up: bfloat16 [2, 64, 5120], P(None, None, 'blk'), may hold values from -0.75 to 0.75
- out_down: bfloat16 [2, 4096, 64], P(None, 'blk'), may hold values from -0.09375 to 0.09375
- out_up: bfloat16 [2, 64, 8192], P(None, None, ('role', 'blk')), may hold values from -0.75 to 0.75
Outputs:
- prompt_out: bfloat16 [16384, 8192], P(('grp', 'blk'), 'role'), parts along dimension 0
- row_out: bfloat16 [32, 8192], P('grp', ('role', 'blk')), parts along dimension 0
There are 8 independent parts, one for each index of `grp`. A program takes and returns all parts, laid end to end along the dimension named above; an argument that names none is the same for every part. Nothing has to cross between parts.
Inputs may be any that keep to these rules, and one draw needn't show every extreme that they name: `row_lengths`: one of the rows has exactly 2048 valid positions. `row_tenant`: the rows name at least two different adapters.
All inputs are finite; a program needn't handle non-finite values.
Results may differ from a plain program's by a relative error of at most 0.03.
Values may be sent and summed in bfloat16 or wider, within the bound.
No kernel may reach another device: no remote copies, remote signals or barrier semaphores. Data moves between devices by JAX's collectives and lax.ppermute only.
A program may use at most 64 MiB of HBM per device.

v0:
```python
import jax
import jax.numpy as jnp
from jax import lax
from jax.sharding import PartitionSpec as P

D = 8192
QUERY_HEADS = 32
KEY_VALUE_HEADS = 4
HEAD_SIZE = 128
RANK = 64
BLOCK = 128


NEGATIVE_FILLER = -1e30


def swapped(value, axis, stride):
    return lax.ppermute(value, axis, [(i, i ^ 1 << stride) for i in range(lax.axis_size(axis))])


def joined(value, axis, join):
    pieces = jax.tree.map(lambda part: lax.all_gather(part, axis), value)
    head = jax.tree.map(lambda part: part[0], pieces)
    tail = jax.tree.map(lambda part: part[1:], pieces)
    running, _ = lax.scan(lambda running, piece: (join(running, piece), None), head, tail)
    return running


def combine_softmax(earlier, later):
    max_one, sum_one, acc_one = earlier
    max_two, sum_two, acc_two = later
    top_max = jnp.maximum(max_one, max_two)
    factor_one = jnp.exp(max_one - top_max)
    factor_two = jnp.exp(max_two - top_max)
    return (
        top_max,
        sum_one * factor_one + sum_two * factor_two,
        acc_one * factor_one[..., None] + acc_two * factor_two[..., None],
    )


def per_device(
    prompt_hidden,
    prompt_qkv,
    block_tenant,
    row_hidden,
    row_qkv,
    row_tenant,
    row_cache,
    row_lengths,
    qkv_down,
    qkv_up,
    out_down,
    out_up,
):
    shard_count = lax.axis_size("blk")
    shard_index = lax.axis_index("blk")
    role_index = lax.axis_index("role")
    is_prefill = role_index == 0
    token_rows = prompt_hidden.shape[0]
    num_blocks = token_rows // BLOCK
    decoding_rows = row_hidden.shape[0]
    query_columns = QUERY_HEADS * HEAD_SIZE
    key_value_columns = KEY_VALUE_HEADS * HEAD_SIZE
    group_width = QUERY_HEADS // KEY_VALUE_HEADS
    score_scale = HEAD_SIZE ** (-0.5)
    col_edges = (
        0,
        query_columns,
        query_columns + key_value_columns,
        query_columns + 2 * key_value_columns,
    )
    all_down, all_up, all_odown = (
        lax.all_gather(qkv_down, "blk", axis=1, tiled=True),
        lax.all_gather(qkv_up, "blk", axis=2, tiled=True),
        lax.all_gather(out_down, "blk", axis=1, tiled=True),
    )
    sel_down = jnp.take(all_down, block_tenant, axis=0)
    sel_up = jnp.take(all_up, block_tenant, axis=0)
    sel_odown = jnp.take(all_odown, block_tenant, axis=0)
    hidden_blocks = prompt_hidden.reshape(num_blocks, BLOCK, -1)
    half_low = jnp.einsum(
        "bnd,bdr->bnr", hidden_blocks, sel_down, preferred_element_type=jnp.float32
    )
    other_low = swapped(half_low.astype(jnp.bfloat16), "role", 0).astype(half_low.dtype)
    low_rank = (half_low + other_low).astype(jnp.bfloat16)
    base_blocks = prompt_qkv.reshape(num_blocks, BLOCK, -1)
    pieces_list = []
    for group_id in range(3):
        pieces_list.append(
            jnp.einsum(
                "bnr,brc->bnc",
                low_rank[:, :, group_id * RANK : (group_id + 1) * RANK],
                sel_up[:, :, col_edges[group_id] : col_edges[group_id + 1]],
                preferred_element_type=jnp.float32,
            )
        )
    adapted = base_blocks.astype(jnp.float32) + jnp.concatenate(pieces_list, axis=2)
    projected_input = adapted.astype(jnp.bfloat16).reshape(token_rows, -1)
    query_matrix = projected_input[:, :query_columns].reshape(
        token_rows, KEY_VALUE_HEADS, group_width, HEAD_SIZE
    )
    query_pos = shard_index * token_rows + jnp.arange(token_rows, dtype=jnp.int32)
    keys_values = projected_input[:, query_columns:]
    all_pairs = lax.all_gather(keys_values, "blk", axis=0, tiled=True)
    key_pos = jnp.arange(all_pairs.shape[0], dtype=jnp.int32)
    allowed = key_pos[None, :] <= query_pos[:, None]

    def attend_all(unused_value):
        head_results = []
        for head_id in range(KEY_VALUE_HEADS):
            query_rows = query_matrix[:, head_id]
            key_rows = all_pairs[:, head_id * HEAD_SIZE : (head_id + 1) * HEAD_SIZE]
            value_rows = all_pairs[
                :,
                key_value_columns
                + head_id * HEAD_SIZE : key_value_columns
                + (head_id + 1) * HEAD_SIZE,
            ]
            scores = (
                jnp.einsum("qgd,nd->gqn", query_rows, key_rows, preferred_element_type=jnp.float32)
                * score_scale
            )
            scores = jnp.where(allowed[None], scores, NEGATIVE_FILLER)
            row_max = jnp.max(scores, axis=-1, keepdims=True)
            weights = jnp.where(allowed[None], jnp.exp(scores - row_max), 0.0)
            weight_sum = jnp.sum(weights, axis=-1)
            numerator = jnp.einsum(
                "gqn,nd->gqd",
                weights.astype(jnp.bfloat16),
                value_rows,
                preferred_element_type=jnp.float32,
            )
            head_results.append(jnp.transpose(numerator / weight_sum[..., None], (1, 0, 2)))
        return (
            jnp.stack(head_results, axis=1).reshape(token_rows, query_columns).astype(jnp.bfloat16)
        )

    def skip_all(unused_value):
        return jnp.zeros((token_rows, query_columns), jnp.bfloat16)

    context = lax.cond(is_prefill, attend_all, skip_all, 0)
    prompt_factor = jnp.einsum(
        "bnh,bhr->bnr",
        context.reshape(num_blocks, BLOCK, query_columns),
        sel_odown,
        preferred_element_type=jnp.float32,
    ).astype(jnp.bfloat16)
    down_rows = qkv_down.shape[1]
    flat_index = role_index * shard_count + shard_index
    hidden_part = lax.dynamic_slice_in_dim(row_hidden, flat_index * down_rows, down_rows, 1)
    row_down_sel = jnp.take(qkv_down, row_tenant, axis=0)
    partial_low = jnp.einsum(
        "rd,rdk->rk", hidden_part, row_down_sel, preferred_element_type=jnp.float32
    )
    row_low = lax.psum(partial_low, ("role", "blk")).astype(jnp.bfloat16)
    up_width = qkv_up.shape[2]
    row_up_sel = jnp.take(qkv_up, row_tenant, axis=0)
    global_cols = shard_index * up_width + jnp.arange(up_width, dtype=jnp.int32)
    column_group = (global_cols >= query_columns).astype(jnp.int32) + (
        global_cols >= query_columns + key_value_columns
    ).astype(jnp.int32)
    local_delta = jnp.zeros((decoding_rows, up_width), jnp.float32)
    for group_id in range(3):
        group_term = jnp.einsum(
            "rk,rkc->rc",
            row_low[:, group_id * RANK : (group_id + 1) * RANK],
            row_up_sel,
            preferred_element_type=jnp.float32,
        )
        local_delta = local_delta + jnp.where(column_group[None, :] == group_id, group_term, 0.0)
    full_delta = lax.all_gather(local_delta, "blk", axis=1, tiled=True)
    row_projected = (row_qkv.astype(jnp.float32) + full_delta).astype(jnp.bfloat16)
    decode_queries = row_projected[:, :query_columns].reshape(
        decoding_rows, KEY_VALUE_HEADS, group_width, HEAD_SIZE
    )
    local_keys = row_projected[:, query_columns : query_columns + key_value_columns].reshape(
        decoding_rows, KEY_VALUE_HEADS, HEAD_SIZE
    )
    local_values = row_projected[:, query_columns + key_value_columns :].reshape(
        decoding_rows, KEY_VALUE_HEADS, HEAD_SIZE
    )
    cache_entries = jnp.concatenate([keys_values[None], row_cache], axis=0)
    cache_pos = shard_index * token_rows + jnp.arange(token_rows, dtype=jnp.int32)
    limits = jnp.concatenate([jnp.full((1,), token_rows * shard_count, jnp.int32), row_lengths])
    usable = cache_pos[None, :] < limits[:, None]
    stored_keys = cache_entries[:, :, :key_value_columns].reshape(
        decoding_rows, token_rows, KEY_VALUE_HEADS, HEAD_SIZE
    )
    stored_values = cache_entries[:, :, key_value_columns:].reshape(
        decoding_rows, token_rows, KEY_VALUE_HEADS, HEAD_SIZE
    )
    row_scores = (
        jnp.einsum(
            "rkgd,rnkd->rkgn", decode_queries, stored_keys, preferred_element_type=jnp.float32
        )
        * score_scale
    )
    row_scores = jnp.where(usable[:, None, None, :], row_scores, NEGATIVE_FILLER)
    local_max = jnp.max(row_scores, axis=-1)
    row_weights = jnp.where(
        usable[:, None, None, :], jnp.exp(row_scores - local_max[..., None]), 0.0
    )
    local_sum = jnp.sum(row_weights, axis=-1)
    local_acc = jnp.einsum(
        "rkgn,rnkd->rkgd",
        row_weights.astype(jnp.bfloat16),
        stored_values,
        preferred_element_type=jnp.float32,
    )
    merged_max, merged_sum, merged_acc = joined(
        (local_max, local_sum, local_acc), "blk", combine_softmax
    )
    own_score = (
        jnp.einsum("rkgd,rkd->rkg", decode_queries, local_keys, preferred_element_type=jnp.float32)
        * score_scale
    )
    top_max = jnp.maximum(merged_max, own_score)
    keep_factor = jnp.exp(merged_max - top_max)
    own_weight = jnp.exp(own_score - top_max)
    denominator = merged_sum * keep_factor + own_weight
    numerator = merged_acc * keep_factor[..., None] + jnp.einsum(
        "rkg,rkd->rkgd",
        own_weight.astype(jnp.bfloat16),
        local_values,
        preferred_element_type=jnp.float32,
    )
    row_context = (
        (numerator / denominator[..., None])
        .reshape(decoding_rows, query_columns)
        .astype(jnp.bfloat16)
    )
    odown_rows = out_down.shape[1]
    context_part = lax.dynamic_slice_in_dim(row_context, shard_index * odown_rows, odown_rows, 1)
    odown_sel = jnp.take(out_down, row_tenant, axis=0)
    partial_out = jnp.einsum(
        "rh,rhk->rk", context_part, odown_sel, preferred_element_type=jnp.float32
    )
    row_factor = lax.psum(partial_out, "blk").astype(jnp.bfloat16)
    half_cols = D // 2
    full_up = lax.all_gather(out_up, ("role", "blk"), axis=2, tiled=True)
    up_blocks = jnp.take(full_up, block_tenant, axis=0)
    prompt_full = jnp.einsum(
        "bnk,bkc->bnc", prompt_factor, up_blocks, preferred_element_type=jnp.float32
    ).astype(jnp.bfloat16)
    first_half = prompt_full[:, :, :half_cols].reshape(token_rows, half_cols)
    second_half = prompt_full[:, :, half_cols:].reshape(token_rows, half_cols)
    got_half, got_rows = swapped((second_half, row_factor), "role", 0)
    prompt_out = jnp.where(is_prefill, first_half, got_half)
    row_use = jnp.where(is_prefill, got_rows, row_factor)
    row_up_cols = jnp.take(out_up, row_tenant, axis=0)
    row_out = jnp.einsum(
        "rk,rkc->rc", row_use, row_up_cols, preferred_element_type=jnp.float32
    ).astype(jnp.bfloat16)
    return (prompt_out, row_out)


def solution(mesh):
    in_specs = (
        P(("grp", "blk"), "role"),
        P(("grp", "blk"), None),
        P(("grp", "blk")),
        P("grp", None),
        P("grp", None),
        P("grp"),
        P("grp", "blk", None),
        P("grp"),
        P(None, ("role", "blk"), None),
        P(None, None, "blk"),
        P(None, "blk", None),
        P(None, None, ("role", "blk")),
    )
    out_specs = (P(("grp", "blk"), "role"), P("grp", ("role", "blk")))
    return jax.shard_map(
        per_device, mesh=mesh, in_specs=in_specs, out_specs=out_specs, check_vma=False
    )
```

profile of v0, /device:TPU:24, one launch (start us, length us, event | category | flops | bytes accessed | tf_op | source)
XLA Modules:
  0.0 369.9 jit_solution(13023768228317722418)
XLA Ops:
  7.2 1.8 copy.69
  9.9 0.7 compare_select_fusion
  10.6 1.5 gather_fusion
  12.1 1.5 gather_fusion.1
  14.3 1.5 copy.74
  17.4 48.1 %psum.14 = bf16[4,192]{1,0:T(4,128)(2,1)S(1)} all-reduce(f32[4,192]{1,0:T(4,128)S(1)} %bitcast.359), channel_id=1, replica_groups=mesh['role'=2,'grp'=8,'blk'=16] {'role','blk'}, use_global_device_ids=true, to_apply=%region_10.11 | all-reduce | flops 768 | bytes 4608 | tf_op jit(solution)/shard_map/psum | solution.py:156
  66.3 32.5 %all-gather.3 = f32[16,320,4]{1,2,0:T(4,128)S(1)} all-gather(f32[1,320,4]{1,2,0:T(4,128)S(1)} %fusion.191), channel_id=1, replica_groups=mesh['role'=2,'grp'=8,'blk'=16] {'blk'}, dimensions={0}, use_global_device_ids=true | all-gather | bytes 87040 | tf_op jit(solution)/shard_map/all_gather | solution.py:172
  99.6 6.0 %constant_dynamic-slice_fusion = bf16[1,64,5120]{1,0,2:T(2,128)(2,1)} fusion(bf16[2,64,5120]{1,0,2:T(2,128)(2,1)} %all-gather.13.cloned.1.call-done, s32[]{:T(128)} %bitcast.35), kind=kLoop, calls=%fused_computation.216 | loop fusion | bytes 1310724 | tf_op jit(solution)/shard_map/jit(_take)/gather | solution.py:79
  105.7 4.8 %copy.101 = bf16[1,64,5120]{2,1,0:T(8,128)(2,1)S(1)} copy(bf16[1,64,5120]{1,0,2:T(2,128)(2,1)} %constant_dynamic-slice_fusion) | data formatting | bytes 1310720
  110.5 2.1 fusion.141
  112.7 5.5 %collective-permute-done = bf16[1,128,192]{1,2,0:T(8,128)(2,1)S(1)} collective-permute-done((bf16[1,128,192]{1,2,0:T(8,128)(2,1)S(1)}, bf16[1,128,192]{1,2,0:T(8,128)(2,1)S(1)}, u32[]{:S(2)}, u32[]{:S(2)}) %collective-permute-start) | collective-permute-done | bytes 49184 | tf_op jit(solution)/shard_map/ppermute | solution.py:18
  119.4 0.8 slice_bitcast_fusion.46
  120.2 0.8 copy.73
  121.0 1.0 pad_maximum_fusion.1
  122.1 1.1 fusion.238
  123.2 1.1 fusion.177
  126.0 1.2 gather_fusion.2
  127.2 0.9 fusion.179
  128.3 18.0 %all-gather.1 = f32[64,4,8]{2,1,0:T(4,128)S(1)} all-gather(f32[4,4,8]{2,1,0:T(4,128)S(1)} %fusion.175), channel_id=3, replica_groups=mesh['role'=2,'grp'=8,'blk'=16] {'blk'}, dimensions={0}, use_global_device_ids=true | all-gather | bytes 8704 | tf_op jit(solution)/shard_map/all_gather | solution.py:22
  147.0 17.0 %all-gather = f32[64,4,8]{2,1,0:T(4,128)S(1)} all-gather(f32[4,4,8]{2,1,0:T(4,128)S(1)} %get-tuple-element.166), channel_id=2, replica_groups=mesh['role'=2,'grp'=8,'blk'=16] {'blk'}, dimensions={0}, use_global_device_ids=true | all-gather | bytes 8704 | tf_op jit(solution)/shard_map/all_gather | solution.py:22
  164.7 1.3 slice.211
  165.9 0.8 slice.208
  166.8 13.2 %while.18 = (s32[]{:T(128)}, f32[4,4,8]{2,1,0:T(4,128)S(1)}, f32[4,4,8]{2,1,0:T(4,128)S(1)}, f32[4,4,8,128]{3,2,1,0:T(8,128)S(1)}, f32[15,4,4,8]{3,2,1,0:T(4,128...) while((s32[]{:T(128)}, f32[4,4,8]{2,1,0:T(4,128)S(1)}, ...), condition=%wide.region_14.15_spmd, body=%wide.region_13.14_spmd.sunk | while | flops 49922 | bytes 201821 | solution.py:25
  167.7 0.7 fusion.250
  168.5 0.7 fusion.250
  179.1 0.7 fusion.250
  180.0 23.0 %all-gather.15.cloned.1.call-done = bf16[2048,1024]{1,0:T(8,128)(2,1)} async-done(((bf16[128,1024]{1,0:T(8,128)(2,1)}), bf16[2048,1024]{1,0:T(8,128)(2,1)}) %all-gather.15.cloned.1.call-update) | async-done | bytes 4194320 | tf_op jit(solution)/shard_map/all_gather | solution.py:105
  203.1 49.7 %conditional.1 = (bf16[128,4096]{0,1:T(8,128)(2,1)S(1)}) conditional(s32[]{:T(128)} %convert_element_type.102, () %tuple.18, (s32[]{:T(128)}, s32[128,1]{0,1:T(1,128)S(1)}, s32[128,2048]{0,1:T(8,128)S(1)}, bf16[2048,1024]{1,0:T(8,128)(2,1)}, bf16[128,5120]{1,0:T(8,128)(2,1)S(1)}) %tuple.19), branch_computations={%region_0.1_spmd, %region_1.10_spmd} | conditional | flops 4348190720 | bytes 58492428 | solution.py:142
  203.1 1.5 copy.71
  204.6 1.3 slice.183
  206.1 6.8 %fusion.233 = (f32[8,128]{1,0:T(8,128)S(1)}, bf16[8,128,2048]{1,2,0:T(8,128)(2,1)}) fusion(pred[128,2048]{0,1:T(8,128)(4,1)S(1)} %broadcast_compare_fusion, bf16[2048,1024]{1,0:T(8,128)(2,1)} %get-tuple-element.51, bf16[128,4,8,128]{0,3,2,1:T(8,128)(2,1)S(1)} %bitcast.352), kind=kOutput, calls=%fused_computation.235 | convolution fusion | flops 549455872 | bytes 5509120 | tf_op jit(solution)/shard_map/cond/branch_1_fun/sub | solution.py:126
  212.9 6.5 %copy.58 = bf16[2048,1024]{0,1:T(8,128)(2,1)} copy(bf16[2048,1024]{1,0:T(8,128)(2,1)} %get-tuple-element.51) | data formatting | bytes 8388608 | tf_op jit(solution)/shard_map
  219.4 3.1 fusion.64
  222.5 6.8 %fusion.228 = (f32[8,128]{1,0:T(8,128)S(1)}, bf16[8,128,2048]{1,2,0:T(8,128)(2,1)}) fusion(pred[128,2048]{0,1:T(8,128)(4,1)S(1)} %broadcast_compare_fusion, bf16[2048,1024]{1,0:T(8,128)(2,1)} %get-tuple-element.51, bf16[128,4,8,128]{0,3,2,1:T(8,128)(2,1)S(1)} %bitcast.353), kind=kOutput, calls=%fused_computation.234 | convolution fusion | flops 549455872 | bytes 5509120 | tf_op jit(solution)/shard_map/cond/branch_1_fun/sub | solution.py:126
  229.3 3.1 fusion.67
  232.4 6.8 %fusion.223 = (f32[8,128]{1,0:T(8,128)S(1)}, bf16[8,128,2048]{1,2,0:T(8,128)(2,1)}) fusion(pred[128,2048]{0,1:T(8,128)(4,1)S(1)} %broadcast_compare_fusion, bf16[2048,1024]{1,0:T(8,128)(2,1)} %get-tuple-element.51, bf16[128,4,8,128]{0,3,2,1:T(8,128)(2,1)S(1)} %bitcast.354), kind=kOutput, calls=%fused_computation.233 | convolution fusion | flops 549455872 | bytes 5509120 | tf_op jit(solution)/shard_map/cond/branch_1_fun/sub | solution.py:126
  239.2 3.1 fusion.70
  242.3 7.0 %fusion.218 = (f32[8,128]{1,0:T(8,128)S(1)}, bf16[8,128,2048]{1,2,0:T(8,128)(2,1)}) fusion(pred[128,2048]{0,1:T(8,128)(4,1)S(1)} %broadcast_compare_fusion, bf16[2048,1024]{1,0:T(8,128)(2,1)} %get-tuple-element.51, bf16[128,4,8,128]{0,3,2,1:T(8,128)(2,1)S(1)} %bitcast.355), kind=kOutput, calls=%fused_computation.232 | convolution fusion | flops 549455872 | bytes 5509120 | tf_op jit(solution)/shard_map/cond/branch_1_fun/sub | solution.py:126
  249.4 3.1 fusion.73
  252.9 0.9 copy-done.1
  253.8 52.8 %all-gather.19.cloned.1.call-done = bf16[2,64,8192]{2,1,0:T(8,128)(2,1)} async-done(((bf16[2,64,256]{2,1,0:T(8,128)(2,1)}), bf16[2,64,8192]{2,1,0:T(8,128)(2,1)}) %all-gather.19.cloned.1.call-update) | async-done | bytes 2097168 | tf_op jit(solution)/shard_map/all_gather | solution.py:241
  306.6 2.8 fusion.139
  309.4 1.0 slice_bitcast_fusion.28
  310.5 2.2 collective-permute-start.1
  313.0 43.0 %psum.15 = bf16[4,64]{1,0:T(4,128)(2,1)S(1)} all-reduce(f32[4,64]{1,0:T(4,128)S(1)} %bitcast.362), channel_id=1, replica_groups=mesh['role'=2,'grp'=8,'blk'=16] {'blk'}, use_global_device_ids=true, to_apply=%region_15.16 | all-reduce | flops 256 | bytes 1536 | tf_op jit(solution)/shard_map/psum | solution.py:239
  356.0 1.5 collective-permute-start.2
  358.0 3.1 collective-permute-done.2
  361.9 1.1 fusion.145
  (105 shorter events, 21.5 us)
Async XLA Ops:
  7.2 103.3 %copy-start = (bf16[128,4096]{1,0:T(8,128)(2,1)S(1)}, bf16[128,4096]{1,0:T(8,128)(2,1)}, u32[]{:S(2)}) copy-start(bf16[128,4096]{1,0:T(8,128)(2,1)} %param.16) | copy-start | bytes 3145732
  7.2 91.8 %copy-start.6 = (bf16[4,5120]{1,0:T(4,128)(2,1)S(1)}, bf16[4,5120]{1,0:T(4,128)(2,1)}, u32[]{:S(2)}) copy-start(bf16[4,5120]{1,0:T(4,128)(2,1)} %param.20) | copy-start | bytes 122884
  7.2 92.5 %all-gather.13.cloned.1.call-start = ((), (), s32[]{:S(2)}) async-start(), calls=%async_computation.1 | async-start | bytes 2785280 | tf_op jit(solution)/shard_map/all_gather | solution.py:75
  9.1 101.4 %all-gather.11.cloned.1.call-start = ((), (), s32[]{:S(2)}) async-start(), calls=%async_computation | async-start | bytes 3342336 | tf_op jit(solution)/shard_map/all_gather | solution.py:74
  9.8 154.9 %all-gather.21.cloned.1.call-start = ((), (), s32[]{:S(2)}) async-start(), calls=%async_computation.5 | async-start | bytes 1114112 | tf_op jit(solution)/shard_map/all_gather | solution.py:22
  110.5 8.7 %copy-start.3 = (bf16[128,5120]{1,0:T(8,128)(2,1)S(1)}, bf16[128,5120]{1,0:T(8,128)(2,1)}, u32[]{:S(2)}) copy-start(bf16[128,5120]{1,0:T(8,128)(2,1)} %param.17) | copy-start | bytes 3932164
  112.6 5.7 %collective-permute-start = (bf16[1,128,192]{1,2,0:T(8,128)(2,1)S(1)}, bf16[1,128,192]{1,2,0:T(8,128)(2,1)S(1)}, u32[]{:S(2)}, u32[]{:S(2)}) collective-permute-start(bf16[1,128,192]{1,2,0:T(8,128)(2,1)S(1)} %fusion.176), channel_id=1, source_target_pairs={{0,128},{128,0},{1,129},{129,1},{2,130},{130,2},{3,131},{131,3},{4... | collective-permute-start | bytes 147464 | tf_op jit(solution)/shard_map/ppermute | solution.py:18
  119.2 6.9 %copy-start.2 = (bf16[2,256,64]{1,2,0:T(8,128)(2,1)S(1)}, bf16[2,256,64]{1,2,0:T(8,128)(2,1)}, u32[]{:S(2)}) copy-start(bf16[2,256,64]{1,2,0:T(8,128)(2,1)} %param.26) | copy-start | bytes 196612
  124.3 78.8 %all-gather.15.cloned.1.call-start = ((), (), s32[]{:S(2)}) async-start(), calls=%async_computation.2 | async-start | bytes 4456448 | tf_op jit(solution)/shard_map/all_gather | solution.py:105
  124.8 128.1 %all-gather.17.cloned.1.call-start = ((), (), s32[]{:S(2)}) async-start(), calls=%async_computation.3 | async-start | bytes 1114112 | tf_op jit(solution)/shard_map/all_gather | solution.py:76
  125.4 181.2 %all-gather.19.cloned.1.call-start = ((), (), s32[]{:S(2)}) async-start(), calls=%async_computation.4 | async-start | bytes 2162688 | tf_op jit(solution)/shard_map/all_gather | solution.py:241
  252.8 1.0 copy-start.1
  252.9 59.9 %copy-start.5 = (bf16[4,256,64]{1,2,0:T(8,128)(2,1)S(1)}, bf16[4,256,64]{1,2,0:T(8,128)(2,1)}, u32[]{:S(2)}) copy-start(bf16[4,256,64]{1,2,0:T(8,128)(2,1)} %gather_fusion.2) | copy-start | bytes 393220
  252.9 104.6 %copy-start.4 = (bf16[2,64,256]{2,1,0:T(8,128)(2,1)S(1)}, bf16[2,64,256]{2,1,0:T(8,128)(2,1)}, u32[]{:S(2)}) copy-start(bf16[2,64,256]{2,1,0:T(8,128)(2,1)} %param.27) | copy-start | bytes 196612
  310.5 51.5 %collective-permute-start.1 = (bf16[128,4096]{1,0:T(8,128)(2,1)}, bf16[128,4096]{1,0:T(8,128)(2,1)}, u32[]{:S(2)}, u32[]{:S(2)}) collective-permute-start(bf16[128,4096]{1,0:T(8,128)(2,1)} %slice_bitcast_fusion.28), channel_id=1, source_target_pairs={{0,128},{128,0},{1,129},{129,1},{2,130},{130,2},{3,131},{131,3},{4... | collective-permute-start | bytes 3145736 | tf_op jit(solution)/shard_map/ppermute | solution.py:18
  356.0 5.1 %collective-permute-start.2 = (bf16[4,64]{1,0:T(4,128)(2,1)S(1)}, bf16[4,64]{1,0:T(4,128)(2,1)S(1)}, u32[]{:S(2)}, u32[]{:S(2)}) collective-permute-start(bf16[4,64]{1,0:T(4,128)(2,1)S(1)} %psum.15), channel_id=1, source_target_pairs={{0,128},{128,0},{1,129},{129,1},{2,130},{130,2},{3,131},{131,3},{4... | collective-permute-start | bytes 1544 | tf_op jit(solution)/shard_map/ppermute | solution.py:18
Sparse Core Ops, SparseCore 0:
  10.4 39.1 all-gather.12
  51.4 43.8 all-gather.10
  124.4 36.1 all-gather.20
  162.8 40.1 all-gather.14
  204.6 36.7 all-gather.16
  243.0 63.5 all-gather.18
where the time goes:
time: 377 us; the launch traced here: 370 us
  blocking collectives  159 us (42%)
  waiting for transfers between devices  86.8 us (23%)
  matrix products  49.9 us (13%)
  local copies, waits for them, and re-layouts  37.4 us (10%)
  other arithmetic  17.5 us (5%)
  between operations  15.1 us (4%)
  starting transfers between devices  3.95 us (1%)
    all_gather x1, waiting for transfers between devices, per_device(): full_up = lax.all_gather(out_up, ('role', 'blk'), axis=2, tiled=True)  52.8 us
    psum x1, blocking collectives, per_device(): row_low = lax.psum(partial_low, ('role', 'blk')).astype(jnp.bfloat16)  48.1 us
    psum x1, blocking collectives, per_device(): row_factor = lax.psum(partial_out, 'blk').astype(jnp.bfloat16)  43 us
    all_gather x2, blocking collectives, joined(): pieces = jax.tree.map(lambda part: lax.all_gather(part, axis), value)  35 us
    all_gather x1, blocking collectives, per_device(): full_delta = lax.all_gather(local_delta, 'blk', axis=1, tiled=True)  32.5 us
    sub x4, matrix products, attend_all(): weights = jnp.where(allowed[None], jnp.exp(scores - row_max), 0.0)  27.5 us
    all_gather x1, waiting for transfers between devices, per_device(): all_pairs = lax.all_gather(keys_values, 'blk', axis=0, tiled=True)  23 us
    dot_general x4, matrix products, attend_all(): jnp.einsum('gqn,nd->gqd', weights.astype(jnp.bfloat16), value_rows, prefe...  12.4 us
  transfers between devices with their start and end apart: 9, of which 4 were waited for; matrix products, arithmetic and copies ran while one was open for 24% of the time, Pallas kernels for 0%

commit v1 on v0

v1 whole, which is shorter than its diff:
```python
import jax
import jax.numpy as jnp
from jax import lax
from jax.experimental import pallas as pl
from jax.experimental.pallas import tpu as pltpu
from jax.sharding import PartitionSpec as P

HEADS = 8
HEAD = 128
RANK = 64
BLOCK = 128
CHIPS = 8
CHUNK = 256
ROWS = 16
LIVE = 4
SCALE = HEAD ** -0.5
LOG2E = 1.4426950408889634
NEG = -1e30
F32 = jnp.float32
BF16 = jnp.bfloat16
MIB = 1 << 20

ROLE, CHIP, CORE, OWN, ROW_T, LENGTH, HEAD_ID, HEAD_OTHER, SCALARS = 0, 1, 2, 3, 4, 8, 11, 12, 13


def nt(a, b):
    return lax.dot_general(a, b, (((1,), (1,)), ((), ())), preferred_element_type=F32)


def nn(a, b):
    return jnp.dot(a, b, preferred_element_type=F32)


def aligned(index, size):
    return pl.ds(pl.multiple_of(index * size, size), size)


def call(body, scalars, args, in_specs, outs, scratch=(), limit=16):
    def whole(shape):
        zeros = (0,) * len(shape)
        return pl.BlockSpec(shape, lambda i, *s: zeros)

    specs = [whole(a.shape) if spec is None else spec for a, spec in zip(args, in_specs)]
    return pl.pallas_call(
        body,
        grid_spec=pltpu.PrefetchScalarGridSpec(
            num_scalar_prefetch=len(scalars),
            grid=(1,),
            in_specs=specs,
            out_specs=[whole(o.shape) for o in outs],
            scratch_shapes=list(scratch),
        ),
        out_shape=outs,
        compiler_params=pltpu.CompilerParams(vmem_limit_bytes=limit * MIB),
    )(*scalars, *args)


def spec(shape, place):
    return pl.BlockSpec(shape, lambda i, ids, *s: place(ids))


def shape(dims, dtype=BF16):
    return jax.ShapeDtypeStruct(dims, dtype)


STEPS = ((0, 0), (0, 1), (1, 0), (3, 0), (1, 1), (3, 1), (2, 0), (2, 1))


def source(chip, step):
    dy, dx = step
    return lax.rem(chip // 2 + dy, 4) * 2 + (lax.rem(chip, 2) ^ dx)


def gather_chips(value):
    def get(value, step):
        pairs = []
        for i in range(2 * CHIPS):
            y, x, core = i // 4, i // 2 % 2, i % 2
            pairs.append(((y + step[0]) % 4 * 4 + (x ^ step[1]) * 2 + core, i))
        return lax.ppermute(value, "blk", pairs)

    up = get(value, (1, 0))
    down_across = get(value, (3, 1))
    across = get(value, (0, 1))
    down = get(value, (3, 0))
    up_across = get(value, (1, 1))
    far = get(up, (1, 0))
    far_across = get(down_across, (3, 0))
    return [value, across, up, down, up_across, down_across, far, far_across]


def pack_body(ids, up, down, out_up, out):
    def columns(main, tail, at):
        for t in range(2):
            out[t] = up[t, :, main : main + CHUNK]
            out[2, :, t * HEAD : (t + 1) * HEAD] = jnp.zeros((RANK, HEAD), BF16)
            out[2, :, t * HEAD + at : t * HEAD + at + RANK] = up[t, :, tail : tail + RANK]

    pl.when(ids[CORE] == 0)(lambda: columns(0, CHUNK, 0))
    pl.when(ids[CORE] == 1)(lambda: columns(RANK, 0, RANK))
    for t in range(2):
        out[3 + t] = down[t]
        out[5 + t] = out_up[t]


def low_body(ids, oth, hid, hid_oth, row_hid, *rest):
    weights, out = rest[:CHIPS], rest[CHIPS]
    role, chip, core = ids[ROLE], ids[CHIP], ids[CORE]
    own_t, oth_t = ids[OWN], oth[0]
    sums = [jnp.zeros((n, 3 * RANK), F32) for n in (BLOCK, BLOCK, ROWS, ROWS)]
    for w, step in zip(weights, STEPS):
        src = source(chip, step)
        x_own = hid[:, aligned(2 * src + core, CHUNK)]
        x_oth = hid_oth[:, aligned(2 * src + core, CHUNK)]
        x_row = row_hid[:, aligned(role * 2 * CHIPS + 2 * src + core, CHUNK)]
        sums[0] += nt(x_own, w[own_t])
        sums[1] += nt(x_oth, w[oth_t])
        sums[2] += nt(x_row, w[0])
        sums[3] += nt(x_row, w[1])
    out[aligned(core, BLOCK), :] = sums[0].astype(BF16)
    out[aligned(1 - core, BLOCK), :] = sums[1].astype(BF16)
    out[2 * BLOCK :, :] = jnp.where(row_mask(ids, ROWS, 3 * RANK), sums[3], sums[2]).astype(BF16)


def row_mask(ids, rows, width):
    at = lax.broadcasted_iota(jnp.int32, (rows, width), 0)
    mask = jnp.zeros((rows, width), jnp.int32)
    for r in range(LIVE):
        mask = jnp.where(at == r, ids[ROW_T + r], mask)
    return mask == 1


def split3(x):
    hi = x.astype(BF16).astype(F32)
    mid = (x - hi).astype(BF16).astype(F32)
    return hi, mid, x - hi - mid


def proj_body(
    ids, oth, mine, theirs, q, k, v, oq, ok, ov, rq, rk, rv, ck, cv, ock, ocv, up0, up1, tail, q_out, kv_out, upb
):
    chip, core, head = ids[CHIP], ids[CORE], ids[HEAD_ID]
    for src in range(CHIPS):
        for t, up in enumerate((up0, up1)):
            lanes = slice(t * HEAD, (t + 1) * HEAD)
            upb[src, t, :, : 2 * HEAD] = up[2 * src, 0]
            upb[src, t, :, 2 * HEAD : 3 * HEAD] = tail[2 * src, 0, :, lanes] + tail[2 * src + 1, 0, :, lanes]
            upb[src, t, :, 3 * HEAD :] = up[2 * src + 1, 0]
    low = (mine[...].astype(F32) + theirs[...].astype(F32)).astype(BF16)
    own_rows, oth_rows = aligned(core, BLOCK), aligned(1 - core, BLOCK)
    low_own = (mine[own_rows, :].astype(F32) + theirs[own_rows, :].astype(F32)).astype(BF16)
    low_oth = (mine[oth_rows, :].astype(F32) + theirs[oth_rows, :].astype(F32)).astype(BF16)
    low_row = low[2 * BLOCK :]
    mask = row_mask(ids, ROWS, HEAD)
    row_q = []
    new_k = new_v = k_own = k_oth = v_own = v_oth = None
    for j in range(HEADS + 2):
        group = max(j - HEADS + 1, 0)
        tile = head * HEADS + j if j < HEADS else head + (32 if j == HEADS else 36)
        src, off = lax.div(tile, 5), lax.rem(tile, 5)
        columns = aligned(off, HEAD)
        part = slice(group * RANK, (group + 1) * RANK)
        here = slice(j * HEAD, (j + 1) * HEAD)
        base = (q[:, here] if j < HEADS else (k if j == HEADS else v)[...]).astype(F32)
        row_base = (rq[:, here] if j < HEADS else (rk if j == HEADS else rv)[...]).astype(F32)
        got_own = (base + nn(low_own[:, part], upb[src, ids[OWN], :, columns])).astype(BF16)
        oth_base = (oq[:, here] if j < HEADS else (ok if j == HEADS else ov)[...]).astype(F32)
        got_oth = (oth_base + nn(low_oth[:, part], upb[src, oth[0], :, columns])).astype(BF16)
        row_terms = [nn(low_row[:, part], upb[src, t, :, columns]) for t in range(2)]
        got_row = (row_base + jnp.where(mask, row_terms[1], row_terms[0])).astype(BF16)
        if j < HEADS:
            q_out[own_rows, here] = got_own
            q_out[oth_rows, here] = got_oth
            row_q.append(got_row)
        elif j == HEADS:
            kv_out[own_rows, :HEAD] = got_own
            kv_out[oth_rows, :HEAD] = got_oth
            k_own, k_oth, new_k = got_own, got_oth, got_row
        else:
            kv_out[own_rows, HEAD:] = got_own
            kv_out[oth_rows, HEAD:] = got_oth
            v_own, v_oth, new_v = got_own, got_oth, got_row

    count = HEADS * ROWS
    queries = jnp.concatenate(row_q, axis=0)
    row_id = lax.rem(lax.broadcasted_iota(jnp.int32, (count, BLOCK), 0), ROWS)
    lane = lax.broadcasted_iota(jnp.int32, (count, BLOCK), 1)
    halves = []
    for at, first in ((core, 0), (1 - core, 1)):
        scores = nt(queries, k_oth if first else k_own)
        valid = jnp.full((count, BLOCK), 1, jnp.int32)
        position = (2 * chip + at) * BLOCK + lane
        for r in range(LIVE - 1):
            keys = ock[r] if first else ck[r]
            this = row_id == r + 1
            scores = jnp.where(this, nt(queries, keys), scores)
            valid = jnp.where(this, (position < ids[LENGTH + r]).astype(jnp.int32), valid)
        halves.append((jnp.where(valid == 1, scores * SCALE, NEG), valid == 1))
    own_lane = lax.broadcasted_iota(jnp.int32, (count, ROWS), 1)
    own_row = lax.rem(lax.broadcasted_iota(jnp.int32, (count, ROWS), 0), ROWS)
    first_chip = chip == 0
    own_score = jnp.where((own_lane == own_row) & first_chip, nt(queries, new_k) * SCALE, NEG)
    top = jnp.max(jnp.maximum(halves[0][0], halves[1][0]), axis=1, keepdims=True)
    top = jnp.maximum(top, jnp.max(own_score, axis=1, keepdims=True))
    own_weight = jnp.where((own_lane == own_row) & first_chip, jnp.exp(own_score - top), 0.0)
    total = jnp.sum(own_weight, axis=1, keepdims=True)
    acc = nn(own_weight.astype(BF16), new_v)
    for first, (scores, valid) in enumerate(halves):
        weights = jnp.where(valid, jnp.exp(scores - top), 0.0)
        total = total + jnp.sum(weights, axis=1, keepdims=True)
        for r in range(LIVE):
            if r == 0:
                values = v_oth if first else v_own
            else:
                values = ocv[r - 1] if first else cv[r - 1]
            acc = acc + nn(jnp.where(row_id == r, weights, 0.0).astype(BF16), values)
    stats = jnp.zeros((count, HEAD), F32)
    for place, value in enumerate(split3(top) + split3(total)):
        stats = jnp.where(lane // 16 == place, value, stats)
    keep_row = lax.broadcasted_iota(jnp.int32, (HEADS * LIVE, count), 0)
    keep_from = lax.broadcasted_iota(jnp.int32, (HEADS * LIVE, count), 1)
    keep = jnp.where((keep_row // LIVE) * ROWS + keep_row % LIVE == keep_from, 1.0, 0.0).astype(BF16)
    kv_out[2 * BLOCK :, :HEAD] = nn(keep, acc.astype(BF16)).astype(BF16)
    kv_out[2 * BLOCK :, HEAD:] = nn(keep, stats.astype(BF16)).astype(BF16)


def attend_body(ids, q, *rest):
    kvs, (ctx, row_ctx), (keys, values) = rest[:CHIPS], rest[CHIPS : CHIPS + 2], rest[CHIPS + 2 :]
    chip = ids[CHIP]
    span = 2 * BLOCK
    values[:, HEAD:] = jnp.ones((CHIPS * span, HEAD), BF16)
    for k in range(CHIPS):
        keys[aligned(source(chip, STEPS[k]), span), :] = kvs[k][:span, :HEAD]
        values[aligned(source(chip, STEPS[k]), span), :HEAD] = kvs[k][:span, HEAD:]

    def branch(chips):
        below = (chips - 1) * span

        def one_head(j, carry):
            columns = aligned(j, HEAD)
            queries = q[:, columns]
            diagonal = nt(queries, keys[below : below + span, :])
            row = lax.broadcasted_iota(jnp.int32, (span, span), 0)
            col = lax.broadcasted_iota(jnp.int32, (span, span), 1)
            diagonal = jnp.where(col <= row, diagonal, NEG)
            top = jnp.max(diagonal, axis=1, keepdims=True)
            if chips > 1:
                scores = nt(queries, keys[:below, :])
                top = jnp.maximum(top, jnp.max(scores, axis=1, keepdims=True))
            weights = jnp.exp2((diagonal - top) * (SCALE * LOG2E)).astype(BF16)
            acc = nn(weights, values[below : below + span, :])
            if chips > 1:
                weights = jnp.exp2((scores - top) * (SCALE * LOG2E)).astype(BF16)
                acc = acc + nn(weights, values[:below, :])
            ctx[:, columns] = (acc[:, :HEAD] / acc[:, HEAD:]).astype(BF16)
            return carry

        lax.fori_loop(0, HEADS, one_head, 0)

    for chips in range(1, CHIPS + 1):
        pl.when(chip == chips - 1)(lambda chips=chips: branch(chips))

    tops, totals, accs = [], [], []
    for k in range(CHIPS):
        stats = kvs[k][span:, HEAD:].astype(F32)
        tops.append(stats[:, 0:1] + stats[:, 16:17] + stats[:, 32:33])
        totals.append(stats[:, 48:49] + stats[:, 64:65] + stats[:, 80:81])
        accs.append(kvs[k][span:, :HEAD].astype(F32))
    top = tops[0]
    for value in tops[1:]:
        top = jnp.maximum(top, value)
    total, acc = 0.0, 0.0
    for k in range(CHIPS):
        factor = jnp.exp(tops[k] - top)
        total = total + totals[k] * factor
        acc = acc + accs[k] * factor
    merged = acc / total
    row_ctx[...] = jnp.zeros((ROWS, HEADS * HEAD), F32)
    for j in range(HEADS):
        row_ctx[:LIVE, j * HEAD : (j + 1) * HEAD] = merged[j * LIVE : (j + 1) * LIVE]


def factor_body(ids, oth, ctx, row_ctx, down0, down1, own_out, oth_out):
    core = ids[CORE]
    parts = HEADS * HEAD // CHUNK
    rows = row_ctx[...].astype(BF16)

    def block(at, t):
        total = jnp.zeros((RANK, BLOCK), F32)
        for i in range(parts):
            total += nt(jnp.where(t == 1, down1[i, 0], down0[i, 0]), ctx[aligned(at, BLOCK), i * CHUNK : (i + 1) * CHUNK])
        return total.astype(BF16)

    row_terms = []
    for t in range(2):
        total = jnp.zeros((ROWS, RANK), F32)
        for i in range(parts):
            total += nt(rows[:, i * CHUNK : (i + 1) * CHUNK], (down0, down1)[t][i, 0])
        row_terms.append(total)
    row_part = jnp.where(row_mask(ids, ROWS, RANK), row_terms[1], row_terms[0]).astype(BF16)
    for out, at, t in ((own_out, core, ids[OWN]), (oth_out, 1 - core, oth[0])):
        out[:RANK, :] = block(at, t)
        out[RANK:, :] = jnp.zeros((ROWS, BLOCK), BF16)
        out[RANK:, :RANK] = row_part


def out_body(ids, a, b, up, own_up, out, row_out):
    total = a[...].astype(F32) + b[...].astype(F32)
    factor = jnp.transpose(total[:RANK]).astype(BF16)
    for i in range(2 * CHIPS):
        out[:, i * CHUNK : (i + 1) * CHUNK] = nn(factor, up[i, 0]).astype(BF16)
    rows = total[RANK:, :RANK].astype(BF16)
    terms = [nn(rows, own_up[t]) for t in range(2)]
    row_out[...] = jnp.where(row_mask(ids, ROWS, CHUNK), terms[1], terms[0])[:LIVE].astype(BF16)


def per_device(
    prompt_hidden,
    prompt_qkv,
    block_tenant,
    row_hidden,
    row_qkv,
    row_tenant,
    row_cache,
    row_lengths,
    qkv_down,
    qkv_up,
    out_down,
    out_up,
):
    blk = lax.axis_index("blk")
    role = lax.axis_index("role")
    chip, core = blk // 2, blk % 2
    head = 2 * role + core
    ids = jnp.concatenate(
        [
            jnp.stack([role, chip, core]).astype(jnp.int32),
            block_tenant,
            row_tenant,
            row_lengths,
            jnp.stack([head, 2 * role + 1 - core]).astype(jnp.int32),
        ]
    )

    def to_core(value):
        return lax.ppermute(value, "blk", [(i, i ^ 1) for i in range(2 * CHIPS)])

    def to_role(value):
        return lax.ppermute(value, "role", [(0, 1), (1, 0)])

    down = jnp.transpose(qkv_down, (0, 2, 1))
    downs = gather_chips(down)
    (mixed,) = call(
        pack_body,
        [ids],
        [qkv_up, jnp.transpose(out_down, (0, 2, 1)), out_up],
        [None] * 3,
        [shape((7, RANK, CHUNK))],
    )
    weights = lax.all_gather(mixed, "blk")
    oth = to_core(block_tenant)
    hid_oth, qkv_oth, cache_oth = to_core(prompt_hidden), to_core(prompt_qkv), to_core(row_cache)
    row_hid = jnp.pad(row_hidden, ((0, ROWS - LIVE), (0, 0)))
    row_base = jnp.pad(row_qkv, ((0, ROWS - LIVE), (0, 0)))

    (part,) = call(
        low_body,
        [ids, oth],
        [prompt_hidden, hid_oth, row_hid, *downs],
        [None] * (3 + CHIPS),
        [shape((2 * BLOCK + ROWS, 3 * RANK))],
    )
    mine = (part.astype(F32) + to_core(part).astype(F32)).astype(BF16)
    theirs = to_role(mine)

    columns = [
        spec((BLOCK, HEADS * HEAD), lambda s: (0, s[HEAD_ID])),
        spec((BLOCK, HEAD), lambda s: (0, 32 + s[HEAD_ID])),
        spec((BLOCK, HEAD), lambda s: (0, 36 + s[HEAD_ID])),
    ]
    row_columns = [
        spec((ROWS, HEADS * HEAD), lambda s: (0, s[HEAD_ID])),
        spec((ROWS, HEAD), lambda s: (0, 32 + s[HEAD_ID])),
        spec((ROWS, HEAD), lambda s: (0, 36 + s[HEAD_ID])),
    ]
    cached = [
        spec((LIVE - 1, BLOCK, HEAD), lambda s: (0, 0, s[HEAD_ID])),
        spec((LIVE - 1, BLOCK, HEAD), lambda s: (0, 0, 4 + s[HEAD_ID])),
    ]
    q, kv = call(
        proj_body,
        [ids, oth],
        [mine, theirs]
        + [prompt_qkv] * 3
        + [qkv_oth] * 3
        + [row_base] * 3
        + [row_cache] * 2
        + [cache_oth] * 2
        + [weights] * 3,
        [None, None]
        + columns
        + columns
        + row_columns
        + cached
        + cached
        + [spec((2 * CHIPS, 1, RANK, CHUNK), lambda s, i=i: (0, i, 0, 0)) for i in range(3)],
        [shape((2 * BLOCK, HEADS * HEAD)), shape((2 * BLOCK + HEADS * LIVE, 2 * HEAD))],
        [pltpu.VMEM((CHIPS, 2, RANK, 5 * HEAD), BF16)],
        48,
    )
    kvs = gather_chips(kv)
    ctx, row_ctx = call(
        attend_body,
        [ids],
        [q, *kvs],
        [None] * (1 + CHIPS),
        [shape((2 * BLOCK, HEADS * HEAD)), shape((ROWS, HEADS * HEAD), F32)],
        [pltpu.VMEM((CHIPS * 2 * BLOCK, HEAD), BF16), pltpu.VMEM((CHIPS * 2 * BLOCK, 2 * HEAD), BF16)],
        32,
    )
    own, other = call(
        factor_body,
        [ids, oth],
        [ctx, row_ctx, weights, weights],
        [None, None]
        + [spec((4, 1, RANK, CHUNK), lambda s, t=t: (s[HEAD_ID], 3 + t, 0, 0)) for t in range(2)],
        [shape((RANK + ROWS, BLOCK)), shape((RANK + ROWS, BLOCK))],
        limit=48,
    )
    mine = (own.astype(F32) + to_core(other).astype(F32)).astype(BF16)
    return tuple(
        call(
            out_body,
            [ids],
            [mine, to_role(mine), weights, out_up],
            [None, None, spec((2 * CHIPS, 1, RANK, CHUNK), lambda s: (0, 5 + s[OWN], 0, 0)), None],
            [shape(prompt_hidden.shape), shape((LIVE, CHUNK))],
            limit=48,
        )
    )


def solution(mesh):
    in_specs = (
        P(("grp", "blk"), "role"),
        P(("grp", "blk"), None),
        P(("grp", "blk")),
        P("grp", None),
        P("grp", None),
        P("grp"),
        P("grp", "blk", None),
        P("grp"),
        P(None, ("role", "blk"), None),
        P(None, None, "blk"),
        P(None, "blk", None),
        P(None, None, ("role", "blk")),
    )
    out_specs = (P(("grp", "blk"), "role"), P("grp", ("role", "blk")))
    return jax.shard_map(
        per_device, mesh=mesh, in_specs=in_specs, out_specs=out_specs, check_vma=False
    )
```

time: 377 us -> 113 us (0.30); the launches traced: 370 us -> 112 us
  blocking collectives: 159 us -> 0 us
  matrix products: 49.9 us -> 0 us
  waiting for transfers between devices: 86.8 us -> 39.9 us
  local copies, waits for them, and re-layouts: 37.4 us -> 11.6 us
  Pallas kernels: 0 us -> 22.2 us
  starting transfers between devices: 3.95 us -> 23.7 us
  other arithmetic: 17.5 us -> 0.05 us
    psum x2 -> x0, blocking collectives: 91.1 us -> none  [the longest x1 48.1 us: per_device(): row_low = lax.psum(partial_low, ('role', 'blk')).astype(jnp.bfloat16)]
    all_gather x6 -> x1, waiting for transfers between devices: 75.9 us -> 0.27 us  [per_device(): weights = lax.all_gather(mixed, 'blk')]
    all_gather x3 -> x0, blocking collectives: 67.4 us -> none  [the longest x2 35 us: joined(): pieces = jax.tree.map(lambda part: lax.all_gather(part, axis), value)]
    ppermute x3 -> x22, waiting for transfers between devices: 8.62 us -> 39.6 us  [the longest x14 26.2 us: get(): return lax.ppermute(value, 'blk', pairs)]
    sub x4 -> x0, matrix products: 27.5 us -> none  [attend_all(): weights = jnp.where(allowed[None], jnp.exp(scores - row_max), 0.0)]
    dot_general x18 -> x0, matrix products: 22.5 us -> none  [the longest x4 12.4 us: attend_all(): jnp.einsum('gqn,nd->gqd', weights.astype(jnp.bfloat16), value_rows, prefe...]
    pallas_call x0 -> x6, Pallas kernels: none -> 22.2 us  [call(): pl.pallas_call(body, grid_spec=pltpu.PrefetchScalarGridSpec(num_scalar_pr...]
    ppermute x3 -> x22, starting transfers between devices: 3.71 us -> 23.6 us  [the longest x14 18 us: get(): return lax.ppermute(value, 'blk', pairs)]
  transfers between devices with their start and end apart: 9 -> 23, of which waited for: 4 -> 17; matrix products, arithmetic and copies ran while one was open for 24% -> 1% of each run, Pallas kernels for 0% -> 2%
where the time goes in v1:
time: 113 us; the launch traced here: 112 us
  waiting for transfers between devices  39.9 us (35%)
  starting transfers between devices  23.7 us (21%)
  Pallas kernels  22.2 us (20%)
  between operations  14.8 us (13%)
  local copies, waits for them, and re-layouts  11.6 us (10%)
    ppermute x14, waiting for transfers between devices, get(): return lax.ppermute(value, 'blk', pairs)  26.2 us
    pallas_call x6, Pallas kernels, call(): pl.pallas_call(body, grid_spec=pltpu.PrefetchScalarGridSpec(num_scalar_pr...  22.2 us
    ppermute x14, starting transfers between devices, get(): return lax.ppermute(value, 'blk', pairs)  18 us
    ppermute x2, waiting for transfers between devices, to_role(): return lax.ppermute(value, 'role', [(0, 1), (1, 0)])  9.49 us
    unnamed x30, local copies, waits for them, and re-layouts  9.24 us
    ppermute x2, starting transfers between devices, to_role(): return lax.ppermute(value, 'role', [(0, 1), (1, 0)])  4.87 us
    ppermute x6, waiting for transfers between devices, to_core(): return lax.ppermute(value, 'blk', [(i, i ^ 1) for i in range(2 * CHIPS)])  3.91 us
  transfers between devices with their start and end apart: 23, of which 17 were waited for; matrix products, arithmetic and copies ran while one was open for 1% of the time, Pallas kernels for 2%

profile of v1, /device:TPU:24, one launch (start us, length us, event | category | flops | bytes accessed | tf_op | source)
XLA Modules:
  0.0 112.1 jit_solution(1550364245537346711)
XLA Ops:
  7.9 0.8 concatenate.3.ids
  8.6 0.8 copy-done.7
  9.5 0.9 copy-done.12
  10.4 0.8 copy-done.13
  11.2 1.3 %shard_map.132 = bf16[7,64,256]{2,1,0:T(8,128)(2,1)} custom-call(s32[13]{0:T(128)S(1)} %concatenate.3.ids, bf16[2,64,320]{2,1,0:T(8,128)(2,1)S(1)} %copy-done.12, bf16[2,64,256]{2,1,0:T(8,128)(2,1)S(1)} %bitcast.20, bf16[2,64,256]{2,1,0:T(8,128)(2,1)S(1)} %copy-done.7), custom_call_target="tpu_custom_call" | custom-call | tf_op jit(solution)/shard_map/pallas_call | solution.py:44
  12.6 0.5 collective-permute-start.11
  13.1 0.7 collective-permute-start.3
  13.8 3.4 %collective-permute-start.6 = (bf16[2,192,256]{2,1,0:T(8,128)(2,1)}, bf16[2,192,256]{2,1,0:T(8,128)(2,1)S(1)}, u32[]{:S(2)}, u32[]{:S(2)}) collective-permute-start(bf16[2,192,256]{2,1,0:T(8,128)(2,1)} %bitcast.15), channel_id=1, source_target_pairs={{14,0},{15,1},{12,2},{13,3},{2,4},{3,5},{0,6},{1,7},{6,8},{7,9},{4... | collective-permute-start | bytes 589832 | tf_op jit(solution)/shard_map/ppermute | solution.py:80
  17.3 1.4 %collective-permute-done.oth = s32[1]{0:T(128)} collective-permute-done((s32[1]{0:T(128)}, s32[1]{0:T(128)}, u32[]{:S(2)}, u32[]{:S(2)}) %collective-permute-start) | collective-permute-done | bytes 36 | tf_op jit(solution)/shard_map/ppermute | solution.py:346
  18.6 0.5 collective-permute-start.2
  19.2 2.2 %collective-permute-done.3.rest_2_ = bf16[2,192,256]{2,1,0:T(8,128)(2,1)S(1)} collective-permute-done((bf16[2,192,256]{2,1,0:T(8,128)(2,1)}, bf16[2,192,256]{2,1,0:T(8,128)(2,1)S(1)}, u32[]{:S(2)}, u32[]{:S(2)}) %collective-permute-start.3) | collective-permute-done | bytes 196640 | tf_op jit(solution)/shard_map/ppermute | solution.py:80
  21.4 0.7 collective-permute-start.4
  22.2 0.7 collective-permute-done.6.rest_5_
  22.9 1.5 %collective-permute-start.5 = (bf16[2,192,256]{2,1,0:T(8,128)(2,1)}, bf16[2,192,256]{2,1,0:T(8,128)(2,1)S(1)}, u32[]{:S(2)}, u32[]{:S(2)}) collective-permute-start(bf16[2,192,256]{2,1,0:T(8,128)(2,1)} %bitcast.18), channel_id=1, source_target_pairs={{6,0},{7,1},{4,2},{5,3},{10,4},{11,5},{8,6},{9,7},{14,8},{15,9},{1... | collective-permute-start | bytes 589832 | tf_op jit(solution)/shard_map/ppermute | solution.py:80
  24.4 3.3 %collective-permute-done.2.rest_1_ = bf16[2,192,256]{2,1,0:T(8,128)(2,1)S(1)} collective-permute-done((bf16[2,192,256]{2,1,0:T(8,128)(2,1)}, bf16[2,192,256]{2,1,0:T(8,128)(2,1)S(1)}, u32[]{:S(2)}, u32[]{:S(2)}) %collective-permute-start.2) | collective-permute-done | bytes 196640 | tf_op jit(solution)/shard_map/ppermute | solution.py:80
  27.7 6.6 %collective-permute-done.5.rest_4_ = bf16[2,192,256]{2,1,0:T(8,128)(2,1)S(1)} collective-permute-done((bf16[2,192,256]{2,1,0:T(8,128)(2,1)}, bf16[2,192,256]{2,1,0:T(8,128)(2,1)S(1)}, u32[]{:S(2)}, u32[]{:S(2)}) %collective-permute-start.5) | collective-permute-done | bytes 196640 | tf_op jit(solution)/shard_map/ppermute | solution.py:80
  34.3 0.9 pad.8.row_hid
  35.2 3.4 %collective-permute-done.7.rest_6_ = bf16[2,192,256]{2,1,0:T(8,128)(2,1)S(1)} collective-permute-done((bf16[2,192,256]{2,1,0:T(8,128)(2,1)S(1)}, bf16[2,192,256]{2,1,0:T(8,128)(2,1)S(1)}, u32[]{:S(2)}, u32[]{:S(2)}) %collective-permute-start.7) | collective-permute-done | bytes 196640 | tf_op jit(solution)/shard_map/ppermute | solution.py:80
  38.6 3.5 %collective-permute-done.8.rest_7_ = bf16[2,192,256]{2,1,0:T(8,128)(2,1)S(1)} collective-permute-done((bf16[2,192,256]{2,1,0:T(8,128)(2,1)S(1)}, bf16[2,192,256]{2,1,0:T(8,128)(2,1)S(1)}, u32[]{:S(2)}, u32[]{:S(2)}) %collective-permute-start.8) | collective-permute-done | bytes 196640 | tf_op jit(solution)/shard_map/ppermute | solution.py:80
  42.1 1.2 %copy-done.6 = bf16[128,4096]{1,0:T(8,128)(2,1)S(1)} copy-done((bf16[128,4096]{1,0:T(8,128)(2,1)S(1)}, bf16[128,4096]{1,0:T(8,128)(2,1)}, u32[]{:S(2)}) %copy-start.6) | copy-done | bytes 1048600
  43.4 0.9 copy-done.9
  44.3 2.2 %shard_map.131 = bf16[272,192]{1,0:T(8,128)(2,1)S(1)} custom-call(s32[13]{0:T(128)S(1)} %concatenate.3.ids, s32[1]{0:T(128)} %collective-permute-done.oth, bf16[128,4096]{1,0:T(8,128)(2,1)S(1)} %copy-done.6, bf16[128,4096]{1,0:T(8,128)(2,1)S(1)} %collective-permute-done.1.hid_oth, bf16[16,8192]{1,0:T(8,128)(2,1)S(1)} %pad.8.row_hid, ...), custom_call_target="tpu_custom_call" | custom-call | tf_op jit(solution)/shard_map/pallas_call | solution.py:44
  46.6 1.3 %collective-permute-done.9 = bf16[272,192]{1,0:T(8,128)(2,1)S(1)} collective-permute-done((bf16[272,192]{1,0:T(8,128)(2,1)S(1)}, bf16[272,192]{1,0:T(8,128)(2,1)S(1)}, u32[]{:S(2)}, u32[]{:S(2)}) %collective-permute-start.9) | collective-permute-done | bytes 104480 | tf_op jit(solution)/shard_map/ppermute | solution.py:346
  48.0 2.4 %collective-permute-start.10 = (bf16[272,192]{1,0:T(8,128)(2,1)S(1)}, bf16[272,192]{1,0:T(8,128)(2,1)S(1)}, u32[]{:S(2)}, u32[]{:S(2)}) collective-permute-start(bf16[272,192]{1,0:T(8,128)(2,1)S(1)} %add_convert_fusion.mine), channel_id=1, source_target_pairs={{0,128},{128,0},{1,129},{129,1},{2,130},{130,2},{3,131},{131,3},{4... | collective-permute-start | bytes 313352 | tf_op jit(solution)/shard_map/ppermute | solution.py:349
  50.4 0.7 pad.9.rq.rk.rv
  51.1 0.9 copy-done.3
  52.0 6.6 %collective-permute-done.10.theirs = bf16[272,192]{1,0:T(8,128)(2,1)S(1)} collective-permute-done((bf16[272,192]{1,0:T(8,128)(2,1)S(1)}, bf16[272,192]{1,0:T(8,128)(2,1)S(1)}, u32[]{:S(2)}, u32[]{:S(2)}) %collective-permute-start.10) | collective-permute-done | bytes 104480 | tf_op jit(solution)/shard_map/ppermute | solution.py:349
  58.5 0.7 copy-done.10
  59.5 1.1 %copy-done.4 = bf16[3,128,1024]{2,1,0:T(8,128)(2,1)S(1)} copy-done((bf16[3,128,1024]{2,1,0:T(8,128)(2,1)S(1)}, bf16[3,128,1024]{2,1,0:T(8,128)(2,1)}, u32[]{:S(2)}) %copy-start.4) | copy-done | bytes 786456
  60.6 0.9 copy-done.5
  61.5 0.9 copy-done.11
  62.4 4.1 %shard_map.133 = (bf16[256,1024]{1,0:T(8,128)(2,1)S(1)}, bf16[288,256]{1,0:T(8,128)(2,1)S(1)}) custom-call(s32[13]{0:T(128)S(1)} %concatenate.3.ids, s32[1]{0:T(128)} %collective-permute-done.oth, bf16[272,192]{1,0:T(8,128)(2,1)S(1)} %add_convert_fusion.mine, bf16[272,192]{1,0:T(8,128)(2,1)S(1)} %copy-done.11, bf16[128,5120]{1,0:T(8,128)(2,1)S(1)} %copy-done.1, ...), custom_call_target="tpu_custom_call" | custom-call | tf_op jit(solution)/shard_map/pallas_call | solution.py:44
  66.5 1.4 %collective-permute-start.14 = (bf16[288,256]{1,0:T(8,128)(2,1)S(1)}, bf16[288,256]{1,0:T(8,128)(2,1)S(1)}, u32[]{:S(2)}, u32[]{:S(2)}) collective-permute-start(bf16[288,256]{1,0:T(8,128)(2,1)S(1)} %get-tuple-element.9.rest_0_), channel_id=1, source_target_pairs={{4,0},{5,1},{6,2},{7,3},{8,4},{9,5},{10,6},{11,7},{12,8},{13,9},{1... | collective-permute-start | bytes 442376 | tf_op jit(solution)/shard_map/ppermute | solution.py:80
  67.9 2.6 %collective-permute-start.17 = (bf16[288,256]{1,0:T(8,128)(2,1)S(1)}, bf16[288,256]{1,0:T(8,128)(2,1)S(1)}, u32[]{:S(2)}, u32[]{:S(2)}) collective-permute-start(bf16[288,256]{1,0:T(8,128)(2,1)S(1)} %get-tuple-element.9.rest_0_), channel_id=1, source_target_pairs={{14,0},{15,1},{12,2},{13,3},{2,4},{3,5},{0,6},{1,7},{6,8},{7,9},{4... | collective-permute-start | bytes 442376 | tf_op jit(solution)/shard_map/ppermute | solution.py:80
  70.5 1.1 collective-permute-start.13
  71.6 1.8 %collective-permute-start.15 = (bf16[288,256]{1,0:T(8,128)(2,1)S(1)}, bf16[288,256]{1,0:T(8,128)(2,1)S(1)}, u32[]{:S(2)}, u32[]{:S(2)}) collective-permute-start(bf16[288,256]{1,0:T(8,128)(2,1)S(1)} %get-tuple-element.9.rest_0_), channel_id=1, source_target_pairs={{12,0},{13,1},{14,2},{15,3},{0,4},{1,5},{2,6},{3,7},{4,8},{5,9},{6... | collective-permute-start | bytes 442376 | tf_op jit(solution)/shard_map/ppermute | solution.py:80
  73.3 0.6 collective-permute-start.16
  74.3 1.2 %collective-permute-done.17.rest_5_ = bf16[288,256]{1,0:T(8,128)(2,1)S(1)} collective-permute-done((bf16[288,256]{1,0:T(8,128)(2,1)S(1)}, bf16[288,256]{1,0:T(8,128)(2,1)S(1)}, u32[]{:S(2)}, u32[]{:S(2)}) %collective-permute-start.17) | collective-permute-done | bytes 147488 | tf_op jit(solution)/shard_map/ppermute | solution.py:80
  75.5 3.4 %collective-permute-start.19 = (bf16[288,256]{1,0:T(8,128)(2,1)S(1)}, bf16[288,256]{1,0:T(8,128)(2,1)S(1)}, u32[]{:S(2)}, u32[]{:S(2)}) collective-permute-start(bf16[288,256]{1,0:T(8,128)(2,1)S(1)} %collective-permute-done.17.rest_5_), channel_id=1, source_target_pairs={{12,0},{13,1},{14,2},{15,3},{0,4},{1,5},{2,6},{3,7},{4,8},{5,9},{6... | collective-permute-start | bytes 442376 | tf_op jit(solution)/shard_map/ppermute | solution.py:80
  78.9 0.5 collective-permute-done.13.rest_1_
  79.4 3.5 %collective-permute-done.16.rest_4_ = bf16[288,256]{1,0:T(8,128)(2,1)S(1)} collective-permute-done((bf16[288,256]{1,0:T(8,128)(2,1)S(1)}, bf16[288,256]{1,0:T(8,128)(2,1)S(1)}, u32[]{:S(2)}, u32[]{:S(2)}) %collective-permute-start.16) | collective-permute-done | bytes 147488 | tf_op jit(solution)/shard_map/ppermute | solution.py:80
  82.9 1.1 collective-permute-done.18.rest_6_
  83.9 11.1 %shard_map.134 = (bf16[256,1024]{1,0:T(8,128)(2,1)S(1)}, f32[16,1024]{1,0:T(8,128)S(1)}) custom-call(s32[13]{0:T(128)S(1)} %concatenate.3.ids, bf16[256,1024]{1,0:T(8,128)(2,1)S(1)} %get-tuple-element.8.q, bf16[288,256]{1,0:T(8,128)(2,1)S(1)} %get-tuple-element.9.rest_0_, bf16[288,256]{1,0:T(8,128)(2,1)S(1)} %collective-permute-done.13.rest_1_, ...), custom_call_target="tpu_custom_call" | custom-call | tf_op jit(solution)/shard_map/pallas_call | solution.py:44
  95.1 1.5 %shard_map.135 = (bf16[80,128]{1,0:T(8,128)(2,1)S(1)}, bf16[80,128]{1,0:T(8,128)(2,1)S(1)}) custom-call(s32[13]{0:T(128)S(1)} %concatenate.3.ids, s32[1]{0:T(128)} %collective-permute-done.oth, bf16[256,1024]{1,0:T(8,128)(2,1)S(1)} %get-tuple-element.10.ctx, f32[16,1024]{1,0:T(8,128)S(1)} %get-tuple-element.11.row_ctx, ...), custom_call_target="tpu_custom_call" | custom-call | tf_op jit(solution)/shard_map/pallas_call | solution.py:44
  96.7 1.2 %collective-permute-done.20 = bf16[80,128]{1,0:T(8,128)(2,1)S(1)} collective-permute-done((bf16[80,128]{1,0:T(8,128)(2,1)S(1)}, bf16[80,128]{1,0:T(8,128)(2,1)S(1)}, u32[]{:S(2)}, u32[]{:S(2)}) %collective-permute-start.20) | collective-permute-done | bytes 20512 | tf_op jit(solution)/shard_map/ppermute | solution.py:346
  97.9 2.5 %collective-permute-start.21 = (bf16[80,128]{1,0:T(8,128)(2,1)S(1)}, bf16[80,128]{1,0:T(8,128)(2,1)S(1)}, u32[]{:S(2)}, u32[]{:S(2)}) collective-permute-start(bf16[80,128]{1,0:T(8,128)(2,1)S(1)} %add_convert_fusion.1.a), channel_id=1, source_target_pairs={{0,128},{128,0},{1,129},{129,1},{2,130},{130,2},{3,131},{131,3},{4... | collective-permute-start | bytes 61448 | tf_op jit(solution)/shard_map/ppermute | solution.py:349
  100.3 2.9 %collective-permute-done.21.b = bf16[80,128]{1,0:T(8,128)(2,1)S(1)} collective-permute-done((bf16[80,128]{1,0:T(8,128)(2,1)S(1)}, bf16[80,128]{1,0:T(8,128)(2,1)S(1)}, u32[]{:S(2)}, u32[]{:S(2)}) %collective-permute-start.21) | collective-permute-done | bytes 20512 | tf_op jit(solution)/shard_map/ppermute | solution.py:349
  103.2 2.0 %shard_map.136 = (bf16[128,4096]{1,0:T(8,128)(2,1)}, bf16[4,256]{1,0:T(4,128)(2,1)}) custom-call(s32[13]{0:T(128)S(1)} %concatenate.3.ids, bf16[80,128]{1,0:T(8,128)(2,1)S(1)} %add_convert_fusion.1.a, bf16[80,128]{1,0:T(8,128)(2,1)S(1)} %collective-permute-done.21.b, bf16[16,7,64,256]{3,2,1,0:T(8,128)(2,1)S(1)} %bitcast.13, bf16[2,64,256]{2,1,0:T(8,128)(2,1)S(1)} %copy-done.8), custom_call_target="tpu_custom_call" | custom-call | tf_op jit(solution)/shard_map/pallas_call | solution.py:44
  (40 shorter events, 1.0 us)
Async XLA Ops:
  7.2 52.3 %all-gather.3.cloned.1.call-start = ((), (), s32[]{:S(2)}) async-start(), calls=%async_computation | async-start | bytes 3899392 | tf_op jit(solution)/shard_map/all_gather | solution.py:360
  8.6 0.8 copy-start.7
  9.5 0.9 copy-start.12
  10.4 0.8 copy-start.13
  12.5 29.6 %collective-permute-start.1 = (bf16[128,4096]{1,0:T(8,128)(2,1)}, bf16[128,4096]{1,0:T(8,128)(2,1)S(1)}, u32[]{:S(2)}, u32[]{:S(2)}) collective-permute-start(bf16[128,4096]{1,0:T(8,128)(2,1)} %hid.1), channel_id=1, source_target_pairs={{0,1},{1,0},{2,3},{3,2},{4,5},{5,4},{6,7},{7,6},{8,9},{9,8},{10,11... | collective-permute-start | bytes 3145736 | tf_op jit(solution)/shard_map/ppermute | solution.py:346
  12.6 46.6 %collective-permute-start.11 = (bf16[128,5120]{1,0:T(8,128)(2,1)}, bf16[128,5120]{1,0:T(8,128)(2,1)S(1)}, u32[]{:S(2)}, u32[]{:S(2)}) collective-permute-start(bf16[128,5120]{1,0:T(8,128)(2,1)} %v.1), channel_id=1, source_target_pairs={{0,1},{1,0},{2,3},{3,2},{4,5},{5,4},{6,7},{7,6},{8,9},{9,8},{10,11... | collective-permute-start | bytes 3932168 | tf_op jit(solution)/shard_map/ppermute | solution.py:346
  13.1 8.3 %collective-permute-start.3 = (bf16[2,192,256]{2,1,0:T(8,128)(2,1)}, bf16[2,192,256]{2,1,0:T(8,128)(2,1)S(1)}, u32[]{:S(2)}, u32[]{:S(2)}) collective-permute-start(bf16[2,192,256]{2,1,0:T(8,128)(2,1)} %bitcast.14), channel_id=1, source_target_pairs={{4,0},{5,1},{6,2},{7,3},{8,4},{9,5},{10,6},{11,7},{12,8},{13,9},{1... | collective-permute-start | bytes 589832 | tf_op jit(solution)/shard_map/ppermute | solution.py:80
  13.8 9.0 %collective-permute-start.6 = (bf16[2,192,256]{2,1,0:T(8,128)(2,1)}, bf16[2,192,256]{2,1,0:T(8,128)(2,1)S(1)}, u32[]{:S(2)}, u32[]{:S(2)}) collective-permute-start(bf16[2,192,256]{2,1,0:T(8,128)(2,1)} %bitcast.15), channel_id=1, source_target_pairs={{14,0},{15,1},{12,2},{13,3},{2,4},{3,5},{0,6},{1,7},{6,8},{7,9},{4... | collective-permute-start | bytes 589832 | tf_op jit(solution)/shard_map/ppermute | solution.py:80
  17.3 1.4 %collective-permute-start = (s32[1]{0:T(128)}, s32[1]{0:T(128)}, u32[]{:S(2)}, u32[]{:S(2)}) collective-permute-start(s32[1]{0:T(128)} %param.14), channel_id=1, source_target_pairs={{0,1},{1,0},{2,3},{3,2},{4,5},{5,4},{6,7},{7,6},{8,9},{9,8},{10,11... | collective-permute-start | bytes 20 | tf_op jit(solution)/shard_map/ppermute | solution.py:346
  18.6 9.1 %collective-permute-start.2 = (bf16[2,192,256]{2,1,0:T(8,128)(2,1)}, bf16[2,192,256]{2,1,0:T(8,128)(2,1)S(1)}, u32[]{:S(2)}, u32[]{:S(2)}) collective-permute-start(bf16[2,192,256]{2,1,0:T(8,128)(2,1)} %bitcast.16), channel_id=1, source_target_pairs={{2,0},{3,1},{0,2},{1,3},{6,4},{7,5},{4,6},{5,7},{10,8},{11,9},{8,1... | collective-permute-start | bytes 589832 | tf_op jit(solution)/shard_map/ppermute | solution.py:80
  21.4 6.3 %collective-permute-start.4 = (bf16[2,192,256]{2,1,0:T(8,128)(2,1)}, bf16[2,192,256]{2,1,0:T(8,128)(2,1)S(1)}, u32[]{:S(2)}, u32[]{:S(2)}) collective-permute-start(bf16[2,192,256]{2,1,0:T(8,128)(2,1)} %bitcast.17), channel_id=1, source_target_pairs={{12,0},{13,1},{14,2},{15,3},{0,4},{1,5},{2,6},{3,7},{4,8},{5,9},{6... | collective-permute-start | bytes 589832 | tf_op jit(solution)/shard_map/ppermute | solution.py:80
  22.9 11.4 %collective-permute-start.5 = (bf16[2,192,256]{2,1,0:T(8,128)(2,1)}, bf16[2,192,256]{2,1,0:T(8,128)(2,1)S(1)}, u32[]{:S(2)}, u32[]{:S(2)}) collective-permute-start(bf16[2,192,256]{2,1,0:T(8,128)(2,1)} %bitcast.18), channel_id=1, source_target_pairs={{6,0},{7,1},{4,2},{5,3},{10,4},{11,5},{8,6},{9,7},{14,8},{15,9},{1... | collective-permute-start | bytes 589832 | tf_op jit(solution)/shard_map/ppermute | solution.py:80
  27.7 23.4 %collective-permute-start.12 = (bf16[3,128,1024]{2,1,0:T(8,128)(2,1)}, bf16[3,128,1024]{2,1,0:T(8,128)(2,1)S(1)}, u32[]{:S(2)}, u32[]{:S(2)}) collective-permute-start(bf16[3,128,1024]{2,1,0:T(8,128)(2,1)} %cv.1), channel_id=1, source_target_pairs={{0,1},{1,0},{2,3},{3,2},{4,5},{5,4},{6,7},{7,6},{8,9},{9,8},{10,11... | collective-permute-start | bytes 2359304 | tf_op jit(solution)/shard_map/ppermute | solution.py:346
  27.7 10.9 %collective-permute-start.7 = (bf16[2,192,256]{2,1,0:T(8,128)(2,1)S(1)}, bf16[2,192,256]{2,1,0:T(8,128)(2,1)S(1)}, u32[]{:S(2)}, u32[]{:S(2)}) collective-permute-start(bf16[2,192,256]{2,1,0:T(8,128)(2,1)S(1)} %collective-permute-done.3.rest_2_), channel_id=1, source_target_pairs={{4,0},{5,1},{6,2},{7,3},{8,4},{9,5},{10,6},{11,7},{12,8},{13,9},{1... | collective-permute-start | bytes 589832 | tf_op jit(solution)/shard_map/ppermute | solution.py:80
  34.3 7.8 %collective-permute-start.8 = (bf16[2,192,256]{2,1,0:T(8,128)(2,1)S(1)}, bf16[2,192,256]{2,1,0:T(8,128)(2,1)S(1)}, u32[]{:S(2)}, u32[]{:S(2)}) collective-permute-start(bf16[2,192,256]{2,1,0:T(8,128)(2,1)S(1)} %collective-permute-done.6.rest_5_), channel_id=1, source_target_pairs={{12,0},{13,1},{14,2},{15,3},{0,4},{1,5},{2,6},{3,7},{4,8},{5,9},{6... | collective-permute-start | bytes 589832 | tf_op jit(solution)/shard_map/ppermute | solution.py:80
  34.3 16.1 %copy-start.14 = (bf16[4,5120]{1,0:T(4,128)(2,1)S(1)}, bf16[4,5120]{1,0:T(4,128)(2,1)}, u32[]{:S(2)}) copy-start(bf16[4,5120]{1,0:T(4,128)(2,1)} %param.16) | copy-start | bytes 122884
  35.2 24.3 %copy-start.2 = (bf16[3,128,1024]{2,1,0:T(8,128)(2,1)S(1)}, bf16[3,128,1024]{2,1,0:T(8,128)(2,1)}, u32[]{:S(2)}) copy-start(bf16[3,128,1024]{2,1,0:T(8,128)(2,1)} %cv.1) | copy-start | bytes 2359300
  42.1 1.2 %copy-start.6 = (bf16[128,4096]{1,0:T(8,128)(2,1)S(1)}, bf16[128,4096]{1,0:T(8,128)(2,1)}, u32[]{:S(2)}) copy-start(bf16[128,4096]{1,0:T(8,128)(2,1)} %hid.1) | copy-start | bytes 3145732
  43.4 0.9 copy-start.9
  44.3 15.2 %copy-start.1 = (bf16[128,5120]{1,0:T(8,128)(2,1)S(1)}, bf16[128,5120]{1,0:T(8,128)(2,1)}, u32[]{:S(2)}) copy-start(bf16[128,5120]{1,0:T(8,128)(2,1)} %v.1) | copy-start | bytes 3932164
  46.5 1.4 %collective-permute-start.9 = (bf16[272,192]{1,0:T(8,128)(2,1)S(1)}, bf16[272,192]{1,0:T(8,128)(2,1)S(1)}, u32[]{:S(2)}, u32[]{:S(2)}) collective-permute-start(bf16[272,192]{1,0:T(8,128)(2,1)S(1)} %shard_map.131), channel_id=1, source_target_pairs={{0,1},{1,0},{2,3},{3,2},{4,5},{5,4},{6,7},{7,6},{8,9},{9,8},{10,11... | collective-permute-start | bytes 313352 | tf_op jit(solution)/shard_map/ppermute | solution.py:346
  48.0 10.6 %collective-permute-start.10 = (bf16[272,192]{1,0:T(8,128)(2,1)S(1)}, bf16[272,192]{1,0:T(8,128)(2,1)S(1)}, u32[]{:S(2)}, u32[]{:S(2)}) collective-permute-start(bf16[272,192]{1,0:T(8,128)(2,1)S(1)} %add_convert_fusion.mine), channel_id=1, source_target_pairs={{0,128},{128,0},{1,129},{129,1},{2,130},{130,2},{3,131},{131,3},{4... | collective-permute-start | bytes 313352 | tf_op jit(solution)/shard_map/ppermute | solution.py:349
  51.1 0.9 copy-start.3
  58.5 0.7 copy-start.10
  59.5 1.1 %copy-start.4 = (bf16[3,128,1024]{2,1,0:T(8,128)(2,1)S(1)}, bf16[3,128,1024]{2,1,0:T(8,128)(2,1)}, u32[]{:S(2)}) copy-start(bf16[3,128,1024]{2,1,0:T(8,128)(2,1)} %copy-done.3) | copy-start | bytes 2359300
  60.6 0.9 copy-start.5
  61.5 0.9 copy-start.11
  62.4 32.6 %copy-start = (bf16[112,64,256]{2,1,0:T(8,128)(2,1)S(1)}, bf16[112,64,256]{2,1,0:T(8,128)(2,1)}, u32[]{:S(2)}) copy-start(bf16[112,64,256]{2,1,0:T(8,128)(2,1)} %all-gather.3.cloned.1.call-done) | copy-start | bytes 11010052
  66.5 7.5 %collective-permute-start.14 = (bf16[288,256]{1,0:T(8,128)(2,1)S(1)}, bf16[288,256]{1,0:T(8,128)(2,1)S(1)}, u32[]{:S(2)}, u32[]{:S(2)}) collective-permute-start(bf16[288,256]{1,0:T(8,128)(2,1)S(1)} %get-tuple-element.9.rest_0_), channel_id=1, source_target_pairs={{4,0},{5,1},{6,2},{7,3},{8,4},{9,5},{10,6},{11,7},{12,8},{13,9},{1... | collective-permute-start | bytes 442376 | tf_op jit(solution)/shard_map/ppermute | solution.py:80
  67.9 7.6 %collective-permute-start.17 = (bf16[288,256]{1,0:T(8,128)(2,1)S(1)}, bf16[288,256]{1,0:T(8,128)(2,1)S(1)}, u32[]{:S(2)}, u32[]{:S(2)}) collective-permute-start(bf16[288,256]{1,0:T(8,128)(2,1)S(1)} %get-tuple-element.9.rest_0_), channel_id=1, source_target_pairs={{14,0},{15,1},{12,2},{13,3},{2,4},{3,5},{0,6},{1,7},{6,8},{7,9},{4... | collective-permute-start | bytes 442376 | tf_op jit(solution)/shard_map/ppermute | solution.py:80
  70.5 8.9 %collective-permute-start.13 = (bf16[288,256]{1,0:T(8,128)(2,1)S(1)}, bf16[288,256]{1,0:T(8,128)(2,1)S(1)}, u32[]{:S(2)}, u32[]{:S(2)}) collective-permute-start(bf16[288,256]{1,0:T(8,128)(2,1)S(1)} %get-tuple-element.9.rest_0_), channel_id=1, source_target_pairs={{2,0},{3,1},{0,2},{1,3},{6,4},{7,5},{4,6},{5,7},{10,8},{11,9},{8,1... | collective-permute-start | bytes 442376 | tf_op jit(solution)/shard_map/ppermute | solution.py:80
  71.6 7.8 %collective-permute-start.15 = (bf16[288,256]{1,0:T(8,128)(2,1)S(1)}, bf16[288,256]{1,0:T(8,128)(2,1)S(1)}, u32[]{:S(2)}, u32[]{:S(2)}) collective-permute-start(bf16[288,256]{1,0:T(8,128)(2,1)S(1)} %get-tuple-element.9.rest_0_), channel_id=1, source_target_pairs={{12,0},{13,1},{14,2},{15,3},{0,4},{1,5},{2,6},{3,7},{4,8},{5,9},{6... | collective-permute-start | bytes 442376 | tf_op jit(solution)/shard_map/ppermute | solution.py:80
  73.3 9.5 %collective-permute-start.16 = (bf16[288,256]{1,0:T(8,128)(2,1)S(1)}, bf16[288,256]{1,0:T(8,128)(2,1)S(1)}, u32[]{:S(2)}, u32[]{:S(2)}) collective-permute-start(bf16[288,256]{1,0:T(8,128)(2,1)S(1)} %get-tuple-element.9.rest_0_), channel_id=1, source_target_pairs={{6,0},{7,1},{4,2},{5,3},{10,4},{11,5},{8,6},{9,7},{14,8},{15,9},{1... | collective-permute-start | bytes 442376 | tf_op jit(solution)/shard_map/ppermute | solution.py:80
  74.1 9.9 %collective-permute-start.18 = (bf16[288,256]{1,0:T(8,128)(2,1)S(1)}, bf16[288,256]{1,0:T(8,128)(2,1)S(1)}, u32[]{:S(2)}, u32[]{:S(2)}) collective-permute-start(bf16[288,256]{1,0:T(8,128)(2,1)S(1)} %collective-permute-done.14.rest_2_), channel_id=1, source_target_pairs={{4,0},{5,1},{6,2},{7,3},{8,4},{9,5},{10,6},{11,7},{12,8},{13,9},{1... | collective-permute-start | bytes 442376 | tf_op jit(solution)/shard_map/ppermute | solution.py:80
  75.5 8.4 %collective-permute-start.19 = (bf16[288,256]{1,0:T(8,128)(2,1)S(1)}, bf16[288,256]{1,0:T(8,128)(2,1)S(1)}, u32[]{:S(2)}, u32[]{:S(2)}) collective-permute-start(bf16[288,256]{1,0:T(8,128)(2,1)S(1)} %collective-permute-done.17.rest_5_), channel_id=1, source_target_pairs={{12,0},{13,1},{14,2},{15,3},{0,4},{1,5},{2,6},{3,7},{4,8},{5,9},{6... | collective-permute-start | bytes 442376 | tf_op jit(solution)/shard_map/ppermute | solution.py:80
  95.1 8.2 %copy-start.8 = (bf16[2,64,256]{2,1,0:T(8,128)(2,1)S(1)}, bf16[2,64,256]{2,1,0:T(8,128)(2,1)}, u32[]{:S(2)}) copy-start(bf16[2,64,256]{2,1,0:T(8,128)(2,1)} %own_up.1) | copy-start | bytes 196612
  96.6 1.3 %collective-permute-start.20 = (bf16[80,128]{1,0:T(8,128)(2,1)S(1)}, bf16[80,128]{1,0:T(8,128)(2,1)S(1)}, u32[]{:S(2)}, u32[]{:S(2)}) collective-permute-start(bf16[80,128]{1,0:T(8,128)(2,1)S(1)} %get-tuple-element.13), channel_id=1, source_target_pairs={{0,1},{1,0},{2,3},{3,2},{4,5},{5,4},{6,7},{7,6},{8,9},{9,8},{10,11... | collective-permute-start | bytes 61448 | tf_op jit(solution)/shard_map/ppermute | solution.py:346
  97.9 5.4 %collective-permute-start.21 = (bf16[80,128]{1,0:T(8,128)(2,1)S(1)}, bf16[80,128]{1,0:T(8,128)(2,1)S(1)}, u32[]{:S(2)}, u32[]{:S(2)}) collective-permute-start(bf16[80,128]{1,0:T(8,128)(2,1)S(1)} %add_convert_fusion.1.a), channel_id=1, source_target_pairs={{0,128},{128,0},{1,129},{129,1},{2,130},{130,2},{3,131},{131,3},{4... | collective-permute-start | bytes 61448 | tf_op jit(solution)/shard_map/ppermute | solution.py:349
Sparse Core Ops, SparseCore 0:
  12.6 46.8 all-gather.2

commit v2 on v1

--- a/solution.py
+++ b/solution.py
@@ -35,7 +35,7 @@
     return pl.ds(pl.multiple_of(index * size, size), size)
 
 
-def call(body, scalars, args, in_specs, outs, scratch=(), limit=16):
+def call(body, scalars, args, in_specs, outs, scratch=(), limit=16, out_specs=None):
     def whole(shape):
         zeros = (0,) * len(shape)
         return pl.BlockSpec(shape, lambda i, *s: zeros)
@@ -47,7 +47,7 @@
             num_scalar_prefetch=len(scalars),
             grid=(1,),
             in_specs=specs,
-            out_specs=[whole(o.shape) for o in outs],
+            out_specs=out_specs or [whole(o.shape) for o in outs],
             scratch_shapes=list(scratch),
         ),
         out_shape=outs,
@@ -89,37 +89,94 @@
     return [value, across, up, down, up_across, down_across, far, far_across]
 
 
-def pack_body(ids, up, down, out_up, out):
+def pack_body(place, up, down, out_up, out):
     def columns(main, tail, at):
         for t in range(2):
             out[t] = up[t, :, main : main + CHUNK]
             out[2, :, t * HEAD : (t + 1) * HEAD] = jnp.zeros((RANK, HEAD), BF16)
             out[2, :, t * HEAD + at : t * HEAD + at + RANK] = up[t, :, tail : tail + RANK]
 
-    pl.when(ids[CORE] == 0)(lambda: columns(0, CHUNK, 0))
-    pl.when(ids[CORE] == 1)(lambda: columns(RANK, 0, RANK))
+    pl.when(lax.rem(place[0], 2) == 0)(lambda: columns(0, CHUNK, 0))
+    pl.when(lax.rem(place[0], 2) == 1)(lambda: columns(RANK, 0, RANK))
     for t in range(2):
         out[3 + t] = down[t]
         out[5 + t] = out_up[t]
 
 
-def low_body(ids, oth, hid, hid_oth, row_hid, *rest):
-    weights, out = rest[:CHIPS], rest[CHIPS]
-    role, chip, core = ids[ROLE], ids[CHIP], ids[CORE]
-    own_t, oth_t = ids[OWN], oth[0]
-    sums = [jnp.zeros((n, 3 * RANK), F32) for n in (BLOCK, BLOCK, ROWS, ROWS)]
-    for w, step in zip(weights, STEPS):
-        src = source(chip, step)
-        x_own = hid[:, aligned(2 * src + core, CHUNK)]
-        x_oth = hid_oth[:, aligned(2 * src + core, CHUNK)]
-        x_row = row_hid[:, aligned(role * 2 * CHIPS + 2 * src + core, CHUNK)]
-        sums[0] += nt(x_own, w[own_t])
-        sums[1] += nt(x_oth, w[oth_t])
-        sums[2] += nt(x_row, w[0])
-        sums[3] += nt(x_row, w[1])
-    out[aligned(core, BLOCK), :] = sums[0].astype(BF16)
-    out[aligned(1 - core, BLOCK), :] = sums[1].astype(BF16)
-    out[2 * BLOCK :, :] = jnp.where(row_mask(ids, ROWS, 3 * RANK), sums[3], sums[2]).astype(BF16)
+def hidden_body(place, adapter, hid, own, to_core, to_x, to_cross, tenant, sems):
+    x, core = lax.rem(place[0] // 2, 2), lax.rem(place[0], 2)
+    tenant[...] = jnp.full((ROWS, 4 * CHUNK), adapter[0].astype(F32)).astype(BF16)
+    copies = []
+
+    def move(src, dst):
+        copies.append(pltpu.make_async_copy(src, dst, sems.at[len(copies)]))
+
+    for out, dx, dc in ((own, 0, 0), (to_core, 0, 1), (to_x, 1, 0), (to_cross, 1, 1)):
+        for y in range(4):
+            chunk = 4 * y + 2 * (x ^ dx) + (core ^ dc)
+            move(hid.at[:, aligned(chunk, CHUNK)], out.at[:BLOCK, y * CHUNK : (y + 1) * CHUNK])
+        move(tenant, out.at[BLOCK:, :])
+    for copy in copies:
+        copy.start()
+    for copy in copies:
+        copy.wait()
+
+
+CACHE_AT = (HEADS + 2) * HEAD
+PACKED = CACHE_AT + (LIVE - 1) * 2 * HEAD
+
+
+def base_body(ids, qkv, cache, own, other, sems):
+    copies = []
+
+    def move(src, out, at, width):
+        copies.append(pltpu.make_async_copy(src, out.at[:, at : at + width], sems.at[len(copies)]))
+
+    for out, head in ((own, ids[HEAD_ID]), (other, ids[HEAD_OTHER])):
+        move(qkv.at[:, aligned(head, HEADS * HEAD)], out, 0, HEADS * HEAD)
+        move(qkv.at[:, aligned(32 + head, HEAD)], out, HEADS * HEAD, HEAD)
+        move(qkv.at[:, aligned(36 + head, HEAD)], out, (HEADS + 1) * HEAD, HEAD)
+        for r in range(LIVE - 1):
+            for half in range(2):
+                at = CACHE_AT + (2 * r + half) * HEAD
+                move(cache.at[r, :, aligned(4 * half + head, HEAD)], out, at, HEAD)
+    for copy in copies:
+        copy.start()
+    for copy in copies:
+        copy.wait()
+
+
+LOW_ROWS = 3 * BLOCK + 2 * ROWS
+
+
+def low_body(ids, own, by_core, by_x, by_cross, row_hid, w0, w1, w3, w2, mine, theirs):
+    role, y, x, core = ids[ROLE], ids[CHIP] // 2, lax.rem(ids[CHIP], 2), ids[CORE]
+    sums = [[jnp.zeros((n, 3 * RANK), F32) for _ in range(2)] for n in (BLOCK, BLOCK, BLOCK, BLOCK, ROWS)]
+    for dy, w in ((0, w0), (1, w1), (3, w3), (2, w2)):
+        src = lax.rem(y + dy, 4)
+        parts = [hid[:BLOCK, aligned(src, CHUNK)] for hid in (own, by_core, by_x, by_cross)]
+        parts.append(row_hid[:, aligned(role * 2 * CHIPS + 4 * src + 2 * x + core, CHUNK)])
+        for total, part in zip(sums, parts):
+            for t in range(2):
+                total[t] += nt(part, w[t])
+
+    def chosen(at, hid):
+        adapter = jnp.broadcast_to(hid[BLOCK : BLOCK + 1, : 3 * RANK].astype(F32), (BLOCK, 3 * RANK))
+        return jnp.where(adapter > 0.5, sums[at][1], sums[at][0])
+
+    rows = jnp.where(row_mask(ids, ROWS, 3 * RANK), sums[4][1], sums[4][0]).astype(BF16)
+    for out, (first, one), (second, two) in (
+        (mine, (0, own), (1, by_core)),
+        (theirs, (2, by_x), (3, by_cross)),
+    ):
+        first, second = chosen(first, one), chosen(second, two)
+        even, odd = jnp.where(core == 0, first, second), jnp.where(core == 0, second, first)
+        out[:BLOCK, :] = even[:, :HEAD].astype(BF16)
+        out[BLOCK : 2 * BLOCK, :] = odd[:, :HEAD].astype(BF16)
+        out[2 * BLOCK : 3 * BLOCK, :] = jnp.concatenate([even[:, HEAD:], odd[:, HEAD:]], axis=1).astype(BF16)
+        out[3 * BLOCK : 3 * BLOCK + ROWS, :] = rows[:, :HEAD]
+        out[3 * BLOCK + ROWS :, :RANK] = rows[:, HEAD:]
+        out[3 * BLOCK + ROWS :, RANK:] = jnp.zeros((ROWS, RANK), BF16)
 
 
 def row_mask(ids, rows, width):
@@ -136,8 +193,13 @@
     return hi, mid, x - hi - mid
 
 
+def cached(r, half):
+    at = CACHE_AT + (2 * r + half) * HEAD
+    return slice(at, at + HEAD)
+
+
 def proj_body(
-    ids, oth, mine, theirs, q, k, v, oq, ok, ov, rq, rk, rv, ck, cv, ock, ocv, up0, up1, tail, q_out, kv_out, upb
+    ids, oth, mine, theirs, base, base_oth, rq, rk, rv, up0, up1, tail, q_out, kv_out, upb
 ):
     chip, core, head = ids[CHIP], ids[CORE], ids[HEAD_ID]
     for src in range(CHIPS):
@@ -146,11 +208,18 @@
             upb[src, t, :, : 2 * HEAD] = up[2 * src, 0]
             upb[src, t, :, 2 * HEAD : 3 * HEAD] = tail[2 * src, 0, :, lanes] + tail[2 * src + 1, 0, :, lanes]
             upb[src, t, :, 3 * HEAD :] = up[2 * src + 1, 0]
-    low = (mine[...].astype(F32) + theirs[...].astype(F32)).astype(BF16)
     own_rows, oth_rows = aligned(core, BLOCK), aligned(1 - core, BLOCK)
-    low_own = (mine[own_rows, :].astype(F32) + theirs[own_rows, :].astype(F32)).astype(BF16)
-    low_oth = (mine[oth_rows, :].astype(F32) + theirs[oth_rows, :].astype(F32)).astype(BF16)
-    low_row = low[2 * BLOCK :]
+
+    def low(rows):
+        return (mine[rows, :].astype(F32) + theirs[rows, :].astype(F32)).astype(BF16)
+
+    third = low(slice(2 * BLOCK, 3 * BLOCK))
+    thirds = third[:, :RANK], third[:, RANK:]
+    low_own = jnp.concatenate([low(own_rows), jnp.where(core == 0, *thirds)], axis=1)
+    low_oth = jnp.concatenate([low(oth_rows), jnp.where(core == 1, *thirds)], axis=1)
+    low_row = jnp.concatenate(
+        [low(slice(3 * BLOCK, 3 * BLOCK + ROWS)), low(slice(3 * BLOCK + ROWS, LOW_ROWS))[:, :RANK]], axis=1
+    )
     mask = row_mask(ids, ROWS, HEAD)
     row_q = []
     new_k = new_v = k_own = k_oth = v_own = v_oth = None
@@ -161,11 +230,9 @@
         columns = aligned(off, HEAD)
         part = slice(group * RANK, (group + 1) * RANK)
         here = slice(j * HEAD, (j + 1) * HEAD)
-        base = (q[:, here] if j < HEADS else (k if j == HEADS else v)[...]).astype(F32)
         row_base = (rq[:, here] if j < HEADS else (rk if j == HEADS else rv)[...]).astype(F32)
-        got_own = (base + nn(low_own[:, part], upb[src, ids[OWN], :, columns])).astype(BF16)
-        oth_base = (oq[:, here] if j < HEADS else (ok if j == HEADS else ov)[...]).astype(F32)
-        got_oth = (oth_base + nn(low_oth[:, part], upb[src, oth[0], :, columns])).astype(BF16)
+        got_own = (base[:, here].astype(F32) + nn(low_own[:, part], upb[src, ids[OWN], :, columns])).astype(BF16)
+        got_oth = (base_oth[:, here].astype(F32) + nn(low_oth[:, part], upb[src, oth[0], :, columns])).astype(BF16)
         row_terms = [nn(low_row[:, part], upb[src, t, :, columns]) for t in range(2)]
         got_row = (row_base + jnp.where(mask, row_terms[1], row_terms[0])).astype(BF16)
         if j < HEADS:
@@ -191,7 +258,7 @@
         valid = jnp.full((count, BLOCK), 1, jnp.int32)
         position = (2 * chip + at) * BLOCK + lane
         for r in range(LIVE - 1):
-            keys = ock[r] if first else ck[r]
+            keys = (base_oth if first else base)[:, cached(r, 0)]
             this = row_id == r + 1
             scores = jnp.where(this, nt(queries, keys), scores)
             valid = jnp.where(this, (position < ids[LENGTH + r]).astype(jnp.int32), valid)
@@ -212,7 +279,7 @@
             if r == 0:
                 values = v_oth if first else v_own
             else:
-                values = ocv[r - 1] if first else cv[r - 1]
+                values = (base_oth if first else base)[:, cached(r - 1, 1)]
             acc = acc + nn(jnp.where(row_id == r, weights, 0.0).astype(BF16), values)
     stats = jnp.zeros((count, HEAD), F32)
     for place, value in enumerate(split3(top) + split3(total)):
@@ -234,31 +301,38 @@
         values[aligned(source(chip, STEPS[k]), span), :HEAD] = kvs[k][:span, HEAD:]
 
     def branch(chips):
-        below = (chips - 1) * span
-
-        def one_head(j, carry):
-            columns = aligned(j, HEAD)
-            queries = q[:, columns]
-            diagonal = nt(queries, keys[below : below + span, :])
-            row = lax.broadcasted_iota(jnp.int32, (span, span), 0)
-            col = lax.broadcasted_iota(jnp.int32, (span, span), 1)
-            diagonal = jnp.where(col <= row, diagonal, NEG)
-            top = jnp.max(diagonal, axis=1, keepdims=True)
-            if chips > 1:
-                scores = nt(queries, keys[:below, :])
-                top = jnp.maximum(top, jnp.max(scores, axis=1, keepdims=True))
-            weights = jnp.exp2((diagonal - top) * (SCALE * LOG2E)).astype(BF16)
-            acc = nn(weights, values[below : below + span, :])
-            if chips > 1:
-                weights = jnp.exp2((scores - top) * (SCALE * LOG2E)).astype(BF16)
-                acc = acc + nn(weights, values[:below, :])
-            ctx[:, columns] = (acc[:, :HEAD] / acc[:, HEAD:]).astype(BF16)
+        below, tail = (chips - 2) * span, 2 * span
+
+        def head_scores(j):
+            queries = q[:, aligned(j, HEAD)]
+            last = nt(queries, keys[below : below + tail, :])
+            row = lax.broadcasted_iota(jnp.int32, (span, tail), 0) + (chip - (chips - 2)) * span
+            col = lax.broadcasted_iota(jnp.int32, (span, tail), 1)
+            scores = [jnp.where(col <= row, last, NEG)]
+            if below:
+                scores.append(nt(queries, keys[:below, :]))
+            return scores
+
+        def head_context(j, scores):
+            top = jnp.max(scores[0], axis=1, keepdims=True)
+            if below:
+                top = jnp.maximum(top, jnp.max(scores[1], axis=1, keepdims=True))
+            acc = 0.0
+            for score, rows in zip(scores, (slice(below, below + tail), slice(0, below))):
+                weights = jnp.exp2((score - top) * (SCALE * LOG2E)).astype(BF16)
+                acc = acc + nn(weights, values[rows, :])
+            ctx[:, aligned(j, HEAD)] = (acc[:, :HEAD] / acc[:, HEAD:]).astype(BF16)
+
+        def two_heads(i, carry):
+            scores = [head_scores(2 * i + e) for e in range(2)]
+            for e in range(2):
+                head_context(2 * i + e, scores[e])
             return carry
 
-        lax.fori_loop(0, HEADS, one_head, 0)
-
-    for chips in range(1, CHIPS + 1):
-        pl.when(chip == chips - 1)(lambda chips=chips: branch(chips))
+        lax.fori_loop(0, HEADS // 2, two_heads, 0)
+
+    for chips in range(2, CHIPS + 1, 2):
+        pl.when(chip // 2 == chips // 2 - 1)(lambda chips=chips: branch(chips))
 
     tops, totals, accs = [], [], []
     for k in range(CHIPS):
@@ -349,60 +423,73 @@
         return lax.ppermute(value, "role", [(0, 1), (1, 0)])
 
     down = jnp.transpose(qkv_down, (0, 2, 1))
-    downs = gather_chips(down)
-    (mixed,) = call(
+    def to_x(value):
+        return lax.ppermute(value, "blk", [(i, i ^ 2) for i in range(2 * CHIPS)])
+
+    def from_row(value, dy):
+        pairs = [((i + 4 * dy) % (2 * CHIPS), i) for i in range(2 * CHIPS)]
+        return lax.ppermute(value, "blk", pairs)
+
+    place = jnp.reshape(blk, (1,))
+    (weights,) = call(
         pack_body,
-        [ids],
+        [place],
         [qkv_up, jnp.transpose(out_down, (0, 2, 1)), out_up],
         [None] * 3,
         [shape((7, RANK, CHUNK))],
-    )
-    weights = lax.all_gather(mixed, "blk")
+        limit=48,
+    )
+    weights = lax.all_gather(weights, "blk")
+    arrived = from_row(down, 1)
+    downs = [down, arrived, from_row(down, 3), from_row(down, 2)]
+    hid, core_hid, x_hid, cross_hid = call(
+        hidden_body,
+        [place, block_tenant],
+        [prompt_hidden],
+        [pl.BlockSpec(memory_space=pl.ANY)],
+        [shape((BLOCK + ROWS, 4 * CHUNK))] * 4,
+        [pltpu.VMEM((ROWS, 4 * CHUNK), BF16), pltpu.SemaphoreType.DMA((20,))],
+        48,
+        out_specs=[pl.BlockSpec(memory_space=pl.ANY)] * 4,
+    )
+    cross_hid = lax.ppermute(cross_hid, "blk", [(i, i ^ 3) for i in range(2 * CHIPS)])
+    x_hid, core_hid = to_x(x_hid), to_core(core_hid)
+    base, base_send = call(
+        base_body,
+        [lax.optimization_barrier((ids, arrived))[0]],
+        [prompt_qkv, row_cache],
+        [pl.BlockSpec(memory_space=pl.ANY)] * 2,
+        [shape((BLOCK, PACKED))] * 2,
+        [pltpu.SemaphoreType.DMA((2 * (3 + 2 * (LIVE - 1)),))],
+        48,
+        out_specs=[pl.BlockSpec(memory_space=pl.ANY)] * 2,
+    )
+    base_oth = to_core(base_send)
     oth = to_core(block_tenant)
-    hid_oth, qkv_oth, cache_oth = to_core(prompt_hidden), to_core(prompt_qkv), to_core(row_cache)
     row_hid = jnp.pad(row_hidden, ((0, ROWS - LIVE), (0, 0)))
     row_base = jnp.pad(row_qkv, ((0, ROWS - LIVE), (0, 0)))
 
-    (part,) = call(
+    part, part_x = call(
         low_body,
-        [ids, oth],
-        [prompt_hidden, hid_oth, row_hid, *downs],
-        [None] * (3 + CHIPS),
-        [shape((2 * BLOCK + ROWS, 3 * RANK))],
-    )
-    mine = (part.astype(F32) + to_core(part).astype(F32)).astype(BF16)
+        [ids],
+        [hid, core_hid, x_hid, cross_hid, row_hid, *downs],
+        [None] * 9,
+        [shape((LOW_ROWS, HEAD))] * 2,
+    )
+    mine = (part.astype(F32) + to_x(part_x).astype(F32)).astype(BF16)
+    mine = (mine.astype(F32) + to_core(mine).astype(F32)).astype(BF16)
     theirs = to_role(mine)
-
-    columns = [
-        spec((BLOCK, HEADS * HEAD), lambda s: (0, s[HEAD_ID])),
-        spec((BLOCK, HEAD), lambda s: (0, 32 + s[HEAD_ID])),
-        spec((BLOCK, HEAD), lambda s: (0, 36 + s[HEAD_ID])),
-    ]
     row_columns = [
         spec((ROWS, HEADS * HEAD), lambda s: (0, s[HEAD_ID])),
         spec((ROWS, HEAD), lambda s: (0, 32 + s[HEAD_ID])),
         spec((ROWS, HEAD), lambda s: (0, 36 + s[HEAD_ID])),
     ]
-    cached = [
-        spec((LIVE - 1, BLOCK, HEAD), lambda s: (0, 0, s[HEAD_ID])),
-        spec((LIVE - 1, BLOCK, HEAD), lambda s: (0, 0, 4 + s[HEAD_ID])),
-    ]
     q, kv = call(
         proj_body,
         [ids, oth],
-        [mine, theirs]
-        + [prompt_qkv] * 3
-        + [qkv_oth] * 3
-        + [row_base] * 3
-        + [row_cache] * 2
-        + [cache_oth] * 2
-        + [weights] * 3,
-        [None, None]
-        + columns
-        + columns
+        [mine, theirs, base, base_oth] + [row_base] * 3 + [weights] * 3,
+        [None] * 4
         + row_columns
-        + cached
-        + cached
         + [spec((2 * CHIPS, 1, RANK, CHUNK), lambda s, i=i: (0, i, 0, 0)) for i in range(3)],
         [shape((2 * BLOCK, HEADS * HEAD)), shape((2 * BLOCK + HEADS * LIVE, 2 * HEAD))],
         [pltpu.VMEM((CHIPS, 2, RANK, 5 * HEAD), BF16)],

time: 113 us -> 104 us (0.920)
  the two profiles are of different devices: /device:TPU:24 before, /device:TPU:248 now
where the time goes in v2:
time: 104 us; the launch traced here: 103 us
  waiting for transfers between devices  33.1 us (32%)
  starting transfers between devices  26.4 us (25%)
  Pallas kernels  18.9 us (18%)
  between operations  14.8 us (14%)
  local copies, waits for them, and re-layouts  10.1 us (10%)
    pallas_call x8, Pallas kernels, call(): pl.pallas_call(body, grid_spec=pltpu.PrefetchScalarGridSpec(num_scalar_pr...  18.9 us
    ppermute x7, starting transfers between devices, get(): return lax.ppermute(value, 'blk', pairs)  12.6 us
    ppermute x3, waiting for transfers between devices, from_row(): return lax.ppermute(value, 'blk', pairs)  11.1 us
    unnamed x26, local copies, waits for them, and re-layouts  8.5 us
    ppermute x2, starting transfers between devices, to_role(): return lax.ppermute(value, 'role', [(0, 1), (1, 0)])  5.57 us
    ppermute x2, waiting for transfers between devices, to_role(): return lax.ppermute(value, 'role', [(0, 1), (1, 0)])  5.09 us
    ppermute x1, waiting for transfers between devices, per_device(): lax.ppermute(cross_hid, 'blk', [(i, i ^ 3) for i in range(2 * CHIPS)])  4.54 us
    ppermute x2, waiting for transfers between devices, to_x(): return lax.ppermute(value, 'blk', [(i, i ^ 2) for i in range(2 * CHIPS)])  4.38 us
  transfers between devices with their start and end apart: 21, of which 13 were waited for; matrix products, arithmetic and copies ran while one was open for 2% of the time, Pallas kernels for 5%

profile of v2, /device:TPU:248, one launch (start us, length us, event | category | flops | bytes accessed | tf_op | source)
XLA Modules:
  0.0 103.5 jit_solution(14548689138261978528)
XLA Ops:
  7.2 0.0 all-gather.3.cloned.1.call-start
  7.2 0.9 copy-done.5
  8.2 0.9 copy-done.10
  9.1 0.8 copy-done.11
  9.9 0.7 shard_map.134
  10.6 0.8 collective-permute-start.4
  12.1 1.2 %copy-done.3 = bf16[128,4096]{1,0:T(8,128)(2,1)S(1)} copy-done((bf16[128,4096]{1,0:T(8,128)(2,1)S(1)}, bf16[128,4096]{1,0:T(8,128)(2,1)}, u32[]{:S(2)}) %copy-start.3) | copy-done | bytes 1048600
  13.3 1.2 %shard_map.131 = (bf16[144,1024]{1,0:T(8,128)(2,1)S(1)}, bf16[144,1024]{1,0:T(8,128)(2,1)}, bf16[144,1024]{1,0:T(8,128)(2,1)}, bf16[144,1024]{1,0:T(8,128)(2,1)}) custom-call(s32[1]{0:T(128)} %bitcast.5.place, s32[1]{0:T(128)S(6)} %copy.14.adapter, bf16[128,4096]{1,0:T(8,128)(2,1)S(1)} %copy-done.3), custom_call_target="tpu_custom_call" | custom-call | tf_op jit(solution)/shard_map/pallas_call | solution.py:44
  14.5 0.1 collective-permute-start.1
  14.6 1.6 %collective-permute-start.2 = (bf16[144,1024]{1,0:T(8,128)(2,1)}, bf16[144,1024]{1,0:T(8,128)(2,1)S(1)}, u32[]{:S(2)}, u32[]{:S(2)}) collective-permute-start(bf16[144,1024]{1,0:T(8,128)(2,1)} %get-tuple-element.19), channel_id=1, source_target_pairs={{0,2},{1,3},{2,0},{3,1},{4,6},{5,7},{6,4},{7,5},{8,10},{9,11},{10,... | collective-permute-start | bytes 884744 | tf_op jit(solution)/shard_map/ppermute | solution.py:427
  16.2 0.3 collective-permute-start.3
  16.5 2.5 %collective-permute-start.5 = (bf16[2,192,256]{2,1,0:T(8,128)(2,1)}, bf16[2,192,256]{2,1,0:T(8,128)(2,1)}, u32[]{:S(2)}, u32[]{:S(2)}) collective-permute-start(bf16[2,192,256]{2,1,0:T(8,128)(2,1)} %bitcast.16), channel_id=1, source_target_pairs={{12,0},{13,1},{14,2},{15,3},{0,4},{1,5},{2,6},{3,7},{4,8},{5,9},{6... | collective-permute-start | bytes 589832 | tf_op jit(solution)/shard_map/ppermute | solution.py:431
  19.0 0.7 copy-done.8
  19.7 0.9 pad.8.row_hid
  20.6 0.8 concatenate.3.ids
  21.3 3.7 %collective-permute-done.5.w3 = bf16[2,192,256]{2,1,0:T(8,128)(2,1)} collective-permute-done((bf16[2,192,256]{2,1,0:T(8,128)(2,1)}, bf16[2,192,256]{2,1,0:T(8,128)(2,1)}, u32[]{:S(2)}, u32[]{:S(2)}) %collective-permute-start.5) | collective-permute-done | bytes 196640 | tf_op jit(solution)/shard_map/ppermute | solution.py:431
  25.0 7.4 %collective-permute-done.6.w2 = bf16[2,192,256]{2,1,0:T(8,128)(2,1)} collective-permute-done((bf16[2,192,256]{2,1,0:T(8,128)(2,1)}, bf16[2,192,256]{2,1,0:T(8,128)(2,1)}, u32[]{:S(2)}, u32[]{:S(2)}) %collective-permute-start.6) | collective-permute-done | bytes 196640 | tf_op jit(solution)/shard_map/ppermute | solution.py:431
  32.5 4.5 %collective-permute-done.3.by_cross = bf16[144,1024]{1,0:T(8,128)(2,1)S(1)} collective-permute-done((bf16[144,1024]{1,0:T(8,128)(2,1)}, bf16[144,1024]{1,0:T(8,128)(2,1)S(1)}, u32[]{:S(2)}, u32[]{:S(2)}) %collective-permute-start.3) | collective-permute-done | bytes 294944 | tf_op jit(solution)/shard_map/ppermute | solution.py:455
  37.0 0.9 copy-done.7
  37.9 0.9 copy-done.9
  38.9 2.9 %shard_map.132 = (bf16[416,128]{1,0:T(8,128)(2,1)S(1)}, bf16[416,128]{1,0:T(8,128)(2,1)S(1)}) custom-call(s32[13]{0:T(128)S(1)} %concatenate.3.ids, bf16[144,1024]{1,0:T(8,128)(2,1)S(1)} %get-tuple-element.17.own, bf16[144,1024]{1,0:T(8,128)(2,1)S(1)} %collective-permute-done.1.by_core, bf16[144,1024]{1,0:T(8,128)(2,1)S(1)} %collective-permute-done.2.by_x, ...), custom_call_target="tpu_custom_call" | custom-call | tf_op jit(solution)/shard_map/pallas_call | solution.py:44
  41.8 1.0 collective-permute-start.7
  42.9 0.9 shard_map.133
  43.8 1.5 %collective-permute-start.10 = (bf16[128,2048]{1,0:T(8,128)(2,1)S(1)}, bf16[128,2048]{1,0:T(8,128)(2,1)S(1)}, u32[]{:S(2)}, u32[]{:S(2)}) collective-permute-start(bf16[128,2048]{1,0:T(8,128)(2,1)S(1)} %get-tuple-element.25), channel_id=1, source_target_pairs={{0,1},{1,0},{2,3},{3,2},{4,5},{5,4},{6,7},{7,6},{8,9},{9,8},{10,11... | collective-permute-start | bytes 1572872 | tf_op jit(solution)/shard_map/ppermute | solution.py:420
  45.2 4.4 %collective-permute-done.7 = bf16[416,128]{1,0:T(8,128)(2,1)S(1)} collective-permute-done((bf16[416,128]{1,0:T(8,128)(2,1)S(1)}, bf16[416,128]{1,0:T(8,128)(2,1)S(1)}, u32[]{:S(2)}, u32[]{:S(2)}) %collective-permute-start.7) | collective-permute-done | bytes 106528 | tf_op jit(solution)/shard_map/ppermute | solution.py:427
  49.7 0.3 collective-permute-start.8
  50.0 1.1 %collective-permute-done.8 = bf16[416,128]{1,0:T(8,128)(2,1)S(1)} collective-permute-done((bf16[416,128]{1,0:T(8,128)(2,1)S(1)}, bf16[416,128]{1,0:T(8,128)(2,1)S(1)}, u32[]{:S(2)}, u32[]{:S(2)}) %collective-permute-start.8) | collective-permute-done | bytes 106528 | tf_op jit(solution)/shard_map/ppermute | solution.py:420
  51.1 2.6 %collective-permute-start.9 = (bf16[416,128]{1,0:T(8,128)(2,1)S(1)}, bf16[416,128]{1,0:T(8,128)(2,1)S(1)}, u32[]{:S(2)}, u32[]{:S(2)}) collective-permute-start(bf16[416,128]{1,0:T(8,128)(2,1)S(1)} %add_convert_fusion.mine), channel_id=1, source_target_pairs={{0,128},{128,0},{1,129},{129,1},{2,130},{130,2},{3,131},{131,3},{4... | collective-permute-start | bytes 319496 | tf_op jit(solution)/shard_map/ppermute | solution.py:423
  53.7 1.4 %collective-permute-done.oth = s32[1]{0:T(128)} collective-permute-done((s32[1]{0:T(128)}, s32[1]{0:T(128)}, u32[]{:S(2)}, u32[]{:S(2)}) %collective-permute-start) | collective-permute-done | bytes 36 | tf_op jit(solution)/shard_map/ppermute | solution.py:420
  55.1 2.7 %collective-permute-done.9.theirs = bf16[416,128]{1,0:T(8,128)(2,1)S(1)} collective-permute-done((bf16[416,128]{1,0:T(8,128)(2,1)S(1)}, bf16[416,128]{1,0:T(8,128)(2,1)S(1)}, u32[]{:S(2)}, u32[]{:S(2)}) %collective-permute-start.9) | collective-permute-done | bytes 106528 | tf_op jit(solution)/shard_map/ppermute | solution.py:423
  57.8 2.0 %copy-done = bf16[112,64,256]{2,1,0:T(8,128)(2,1)S(1)} copy-done((bf16[112,64,256]{2,1,0:T(8,128)(2,1)S(1)}, bf16[112,64,256]{2,1,0:T(8,128)(2,1)}, u32[]{:S(2)}) %copy-start) | copy-done | bytes 3670040
  59.8 2.7 %shard_map.135 = (bf16[256,1024]{1,0:T(8,128)(2,1)S(1)}, bf16[288,256]{1,0:T(8,128)(2,1)S(1)}) custom-call(s32[13]{0:T(128)S(1)} %concatenate.3.ids, s32[1]{0:T(128)} %collective-permute-done.oth, bf16[416,128]{1,0:T(8,128)(2,1)S(1)} %add_convert_fusion.mine, bf16[416,128]{1,0:T(8,128)(2,1)S(1)} %collective-permute-done.9.theirs, ...), custom_call_target="tpu_custom_call" | custom-call | tf_op jit(solution)/shard_map/pallas_call | solution.py:44
  62.5 4.8 %collective-permute-start.15 = (bf16[288,256]{1,0:T(8,128)(2,1)S(1)}, bf16[288,256]{1,0:T(8,128)(2,1)S(1)}, u32[]{:S(2)}, u32[]{:S(2)}) collective-permute-start(bf16[288,256]{1,0:T(8,128)(2,1)S(1)} %get-tuple-element.27.rest_0_), channel_id=1, source_target_pairs={{14,0},{15,1},{12,2},{13,3},{2,4},{3,5},{0,6},{1,7},{6,8},{7,9},{4... | collective-permute-start | bytes 442376 | tf_op jit(solution)/shard_map/ppermute | solution.py:80
  67.3 1.2 %collective-permute-start.11 = (bf16[288,256]{1,0:T(8,128)(2,1)S(1)}, bf16[288,256]{1,0:T(8,128)(2,1)S(1)}, u32[]{:S(2)}, u32[]{:S(2)}) collective-permute-start(bf16[288,256]{1,0:T(8,128)(2,1)S(1)} %get-tuple-element.27.rest_0_), channel_id=1, source_target_pairs={{2,0},{3,1},{0,2},{1,3},{6,4},{7,5},{4,6},{5,7},{10,8},{11,9},{8,1... | collective-permute-start | bytes 442376 | tf_op jit(solution)/shard_map/ppermute | solution.py:80
  68.5 2.0 %collective-permute-start.13 = (bf16[288,256]{1,0:T(8,128)(2,1)S(1)}, bf16[288,256]{1,0:T(8,128)(2,1)S(1)}, u32[]{:S(2)}, u32[]{:S(2)}) collective-permute-start(bf16[288,256]{1,0:T(8,128)(2,1)S(1)} %get-tuple-element.27.rest_0_), channel_id=1, source_target_pairs={{12,0},{13,1},{14,2},{15,3},{0,4},{1,5},{2,6},{3,7},{4,8},{5,9},{6... | collective-permute-start | bytes 442376 | tf_op jit(solution)/shard_map/ppermute | solution.py:80
  70.4 0.3 collective-permute-start.14
  70.8 0.8 collective-permute-done.15.rest_5_
  71.6 4.3 %collective-permute-start.17 = (bf16[288,256]{1,0:T(8,128)(2,1)S(1)}, bf16[288,256]{1,0:T(8,128)(2,1)S(1)}, u32[]{:S(2)}, u32[]{:S(2)}) collective-permute-start(bf16[288,256]{1,0:T(8,128)(2,1)S(1)} %collective-permute-done.15.rest_5_), channel_id=1, source_target_pairs={{12,0},{13,1},{14,2},{15,3},{0,4},{1,5},{2,6},{3,7},{4,8},{5,9},{6... | collective-permute-start | bytes 442376 | tf_op jit(solution)/shard_map/ppermute | solution.py:80
  75.9 0.4 collective-permute-done.11.rest_1_
  76.3 2.8 %collective-permute-done.14.rest_4_ = bf16[288,256]{1,0:T(8,128)(2,1)S(1)} collective-permute-done((bf16[288,256]{1,0:T(8,128)(2,1)S(1)}, bf16[288,256]{1,0:T(8,128)(2,1)S(1)}, u32[]{:S(2)}, u32[]{:S(2)}) %collective-permute-start.14) | collective-permute-done | bytes 147488 | tf_op jit(solution)/shard_map/ppermute | solution.py:80
  79.1 0.4 collective-permute-done.16.rest_6_
  79.4 7.0 %shard_map.136 = (bf16[256,1024]{1,0:T(8,128)(2,1)S(1)}, f32[16,1024]{1,0:T(8,128)S(1)}) custom-call(s32[13]{0:T(128)S(1)} %concatenate.3.ids, bf16[256,1024]{1,0:T(8,128)(2,1)S(1)} %get-tuple-element.26.q, bf16[288,256]{1,0:T(8,128)(2,1)S(1)} %get-tuple-element.27.rest_0_, bf16[288,256]{1,0:T(8,128)(2,1)S(1)} %collective-permute-done.11.rest_1_, ...), custom_call_target="tpu_custom_call" | custom-call | tf_op jit(solution)/shard_map/pallas_call | solution.py:44
  86.5 1.5 %shard_map.137 = (bf16[80,128]{1,0:T(8,128)(2,1)S(1)}, bf16[80,128]{1,0:T(8,128)(2,1)S(1)}) custom-call(s32[13]{0:T(128)S(1)} %concatenate.3.ids, s32[1]{0:T(128)} %collective-permute-done.oth, bf16[256,1024]{1,0:T(8,128)(2,1)S(1)} %get-tuple-element.28.ctx, f32[16,1024]{1,0:T(8,128)S(1)} %get-tuple-element.29.row_ctx, ...), custom_call_target="tpu_custom_call" | custom-call | tf_op jit(solution)/shard_map/pallas_call | solution.py:44
  88.0 0.1 collective-permute-start.18
  88.1 1.2 %collective-permute-done.18 = bf16[80,128]{1,0:T(8,128)(2,1)S(1)} collective-permute-done((bf16[80,128]{1,0:T(8,128)(2,1)S(1)}, bf16[80,128]{1,0:T(8,128)(2,1)S(1)}, u32[]{:S(2)}, u32[]{:S(2)}) %collective-permute-start.18) | collective-permute-done | bytes 20512 | tf_op jit(solution)/shard_map/ppermute | solution.py:420
  89.3 3.0 %collective-permute-start.19 = (bf16[80,128]{1,0:T(8,128)(2,1)S(1)}, bf16[80,128]{1,0:T(8,128)(2,1)S(1)}, u32[]{:S(2)}, u32[]{:S(2)}) collective-permute-start(bf16[80,128]{1,0:T(8,128)(2,1)S(1)} %add_convert_fusion.2.a), channel_id=1, source_target_pairs={{0,128},{128,0},{1,129},{129,1},{2,130},{130,2},{3,131},{131,3},{4... | collective-permute-start | bytes 61448 | tf_op jit(solution)/shard_map/ppermute | solution.py:423
  92.2 2.4 %collective-permute-done.19.b = bf16[80,128]{1,0:T(8,128)(2,1)S(1)} collective-permute-done((bf16[80,128]{1,0:T(8,128)(2,1)S(1)}, bf16[80,128]{1,0:T(8,128)(2,1)S(1)}, u32[]{:S(2)}, u32[]{:S(2)}) %collective-permute-start.19) | collective-permute-done | bytes 20512 | tf_op jit(solution)/shard_map/ppermute | solution.py:423
  94.6 2.0 %shard_map.138 = (bf16[128,4096]{1,0:T(8,128)(2,1)}, bf16[4,256]{1,0:T(4,128)(2,1)}) custom-call(s32[13]{0:T(128)S(1)} %concatenate.3.ids, bf16[80,128]{1,0:T(8,128)(2,1)S(1)} %add_convert_fusion.2.a, bf16[80,128]{1,0:T(8,128)(2,1)S(1)} %collective-permute-done.19.b, bf16[16,7,64,256]{3,2,1,0:T(8,128)(2,1)S(1)} %bitcast.14, bf16[2,64,256]{2,1,0:T(8,128)(2,1)S(1)} %copy-done.6), custom_call_target="tpu_custom_call" | custom-call | tf_op jit(solution)/shard_map/pallas_call | solution.py:44
  (35 shorter events, 0.2 us)
Async XLA Ops:
  7.2 35.7 %copy-start.2 = (bf16[128,5120]{1,0:T(8,128)(2,1)S(1)}, bf16[128,5120]{1,0:T(8,128)(2,1)}, u32[]{:S(2)}) copy-start(bf16[128,5120]{1,0:T(8,128)(2,1)} %qkv.1) | copy-start | bytes 3932164
  7.2 50.6 %all-gather.3.cloned.1.call-start = ((), (), s32[]{:S(2)}) async-start(), calls=%async_computation | async-start | bytes 3899392 | tf_op jit(solution)/shard_map/all_gather | solution.py:442
  7.2 0.9 copy-start.5
  8.2 0.9 copy-start.10
  9.1 0.8 copy-start.11
  10.6 8.4 %collective-permute-start.4 = (bf16[2,192,256]{2,1,0:T(8,128)(2,1)}, bf16[2,192,256]{2,1,0:T(8,128)(2,1)S(1)}, u32[]{:S(2)}, u32[]{:S(2)}) collective-permute-start(bf16[2,192,256]{2,1,0:T(8,128)(2,1)} %bitcast.15), channel_id=1, source_target_pairs={{4,0},{5,1},{6,2},{7,3},{8,4},{9,5},{10,6},{11,7},{12,8},{13,9},{1... | collective-permute-start | bytes 589832 | tf_op jit(solution)/shard_map/ppermute | solution.py:431
  12.1 1.2 %copy-start.3 = (bf16[128,4096]{1,0:T(8,128)(2,1)S(1)}, bf16[128,4096]{1,0:T(8,128)(2,1)}, u32[]{:S(2)}) copy-start(bf16[128,4096]{1,0:T(8,128)(2,1)} %hid.1) | copy-start | bytes 3145732
  13.3 29.5 %copy-start.4 = (bf16[3,128,1024]{2,1,0:T(8,128)(2,1)S(1)}, bf16[3,128,1024]{2,1,0:T(8,128)(2,1)}, u32[]{:S(2)}) copy-start(bf16[3,128,1024]{2,1,0:T(8,128)(2,1)} %cache.1) | copy-start | bytes 2359300
  14.5 17.9 %collective-permute-start.1 = (bf16[144,1024]{1,0:T(8,128)(2,1)}, bf16[144,1024]{1,0:T(8,128)(2,1)S(1)}, u32[]{:S(2)}, u32[]{:S(2)}) collective-permute-start(bf16[144,1024]{1,0:T(8,128)(2,1)} %get-tuple-element.18), channel_id=1, source_target_pairs={{0,1},{1,0},{2,3},{3,2},{4,5},{5,4},{6,7},{7,6},{8,9},{9,8},{10,11... | collective-permute-start | bytes 884744 | tf_op jit(solution)/shard_map/ppermute | solution.py:420
  14.6 17.8 %collective-permute-start.2 = (bf16[144,1024]{1,0:T(8,128)(2,1)}, bf16[144,1024]{1,0:T(8,128)(2,1)S(1)}, u32[]{:S(2)}, u32[]{:S(2)}) collective-permute-start(bf16[144,1024]{1,0:T(8,128)(2,1)} %get-tuple-element.19), channel_id=1, source_target_pairs={{0,2},{1,3},{2,0},{3,1},{4,6},{5,7},{6,4},{7,5},{8,10},{9,11},{10,... | collective-permute-start | bytes 884744 | tf_op jit(solution)/shard_map/ppermute | solution.py:427
  16.2 20.8 %collective-permute-start.3 = (bf16[144,1024]{1,0:T(8,128)(2,1)}, bf16[144,1024]{1,0:T(8,128)(2,1)S(1)}, u32[]{:S(2)}, u32[]{:S(2)}) collective-permute-start(bf16[144,1024]{1,0:T(8,128)(2,1)} %get-tuple-element.20), channel_id=1, source_target_pairs={{0,3},{1,2},{2,1},{3,0},{4,7},{5,6},{6,5},{7,4},{8,11},{9,10},{10,... | collective-permute-start | bytes 884744 | tf_op jit(solution)/shard_map/ppermute | solution.py:455
  16.5 8.6 %collective-permute-start.5 = (bf16[2,192,256]{2,1,0:T(8,128)(2,1)}, bf16[2,192,256]{2,1,0:T(8,128)(2,1)}, u32[]{:S(2)}, u32[]{:S(2)}) collective-permute-start(bf16[2,192,256]{2,1,0:T(8,128)(2,1)} %bitcast.16), channel_id=1, source_target_pairs={{12,0},{13,1},{14,2},{15,3},{0,4},{1,5},{2,6},{3,7},{4,8},{5,9},{6... | collective-permute-start | bytes 589832 | tf_op jit(solution)/shard_map/ppermute | solution.py:431
  19.0 0.7 copy-start.8
  19.7 12.8 %collective-permute-start.6 = (bf16[2,192,256]{2,1,0:T(8,128)(2,1)}, bf16[2,192,256]{2,1,0:T(8,128)(2,1)}, u32[]{:S(2)}, u32[]{:S(2)}) collective-permute-start(bf16[2,192,256]{2,1,0:T(8,128)(2,1)} %bitcast.17), channel_id=1, source_target_pairs={{8,0},{9,1},{10,2},{11,3},{12,4},{13,5},{14,6},{15,7},{0,8},{1,9},... | collective-permute-start | bytes 589832 | tf_op jit(solution)/shard_map/ppermute | solution.py:431
  37.0 0.9 copy-start.7
  37.9 0.9 copy-start.9
  38.9 14.8 %copy-start.12 = (bf16[4,5120]{1,0:T(4,128)(2,1)S(1)}, bf16[4,5120]{1,0:T(4,128)(2,1)}, u32[]{:S(2)}) copy-start(bf16[4,5120]{1,0:T(4,128)(2,1)} %param.16) | copy-start | bytes 122884
  41.8 7.8 %collective-permute-start.7 = (bf16[416,128]{1,0:T(8,128)(2,1)S(1)}, bf16[416,128]{1,0:T(8,128)(2,1)S(1)}, u32[]{:S(2)}, u32[]{:S(2)}) collective-permute-start(bf16[416,128]{1,0:T(8,128)(2,1)S(1)} %get-tuple-element.22), channel_id=1, source_target_pairs={{0,2},{1,3},{2,0},{3,1},{4,6},{5,7},{6,4},{7,5},{8,10},{9,11},{10,... | collective-permute-start | bytes 319496 | tf_op jit(solution)/shard_map/ppermute | solution.py:427
  43.8 14.0 %collective-permute-start.10 = (bf16[128,2048]{1,0:T(8,128)(2,1)S(1)}, bf16[128,2048]{1,0:T(8,128)(2,1)S(1)}, u32[]{:S(2)}, u32[]{:S(2)}) collective-permute-start(bf16[128,2048]{1,0:T(8,128)(2,1)S(1)} %get-tuple-element.25), channel_id=1, source_target_pairs={{0,1},{1,0},{2,3},{3,2},{4,5},{5,4},{6,7},{7,6},{8,9},{9,8},{10,11... | collective-permute-start | bytes 1572872 | tf_op jit(solution)/shard_map/ppermute | solution.py:420
  49.7 1.4 %collective-permute-start.8 = (bf16[416,128]{1,0:T(8,128)(2,1)S(1)}, bf16[416,128]{1,0:T(8,128)(2,1)S(1)}, u32[]{:S(2)}, u32[]{:S(2)}) collective-permute-start(bf16[416,128]{1,0:T(8,128)(2,1)S(1)} %add_convert_fusion.1), channel_id=1, source_target_pairs={{0,1},{1,0},{2,3},{3,2},{4,5},{5,4},{6,7},{7,6},{8,9},{9,8},{10,11... | collective-permute-start | bytes 319496 | tf_op jit(solution)/shard_map/ppermute | solution.py:420
  51.1 6.7 %collective-permute-start.9 = (bf16[416,128]{1,0:T(8,128)(2,1)S(1)}, bf16[416,128]{1,0:T(8,128)(2,1)S(1)}, u32[]{:S(2)}, u32[]{:S(2)}) collective-permute-start(bf16[416,128]{1,0:T(8,128)(2,1)S(1)} %add_convert_fusion.mine), channel_id=1, source_target_pairs={{0,128},{128,0},{1,129},{129,1},{2,130},{130,2},{3,131},{131,3},{4... | collective-permute-start | bytes 319496 | tf_op jit(solution)/shard_map/ppermute | solution.py:423
  53.7 1.4 %collective-permute-start = (s32[1]{0:T(128)}, s32[1]{0:T(128)}, u32[]{:S(2)}, u32[]{:S(2)}) collective-permute-start(s32[1]{0:T(128)} %param.14), channel_id=1, source_target_pairs={{0,1},{1,0},{2,3},{3,2},{4,5},{5,4},{6,7},{7,6},{8,9},{9,8},{10,11... | collective-permute-start | bytes 20 | tf_op jit(solution)/shard_map/ppermute | solution.py:420
  57.8 2.0 %copy-start = (bf16[112,64,256]{2,1,0:T(8,128)(2,1)S(1)}, bf16[112,64,256]{2,1,0:T(8,128)(2,1)}, u32[]{:S(2)}) copy-start(bf16[112,64,256]{2,1,0:T(8,128)(2,1)} %all-gather.3.cloned.1.call-done) | copy-start | bytes 11010052
  59.8 26.6 %copy-start.1 = (bf16[112,64,256]{2,1,0:T(8,128)(2,1)S(1)}, bf16[112,64,256]{2,1,0:T(8,128)(2,1)}, u32[]{:S(2)}) copy-start(bf16[112,64,256]{2,1,0:T(8,128)(2,1)} %all-gather.3.cloned.1.call-done) | copy-start | bytes 11010052
  62.5 8.3 %collective-permute-start.12 = (bf16[288,256]{1,0:T(8,128)(2,1)S(1)}, bf16[288,256]{1,0:T(8,128)(2,1)S(1)}, u32[]{:S(2)}, u32[]{:S(2)}) collective-permute-start(bf16[288,256]{1,0:T(8,128)(2,1)S(1)} %get-tuple-element.27.rest_0_), channel_id=1, source_target_pairs={{4,0},{5,1},{6,2},{7,3},{8,4},{9,5},{10,6},{11,7},{12,8},{13,9},{1... | collective-permute-start | bytes 442376 | tf_op jit(solution)/shard_map/ppermute | solution.py:80
  62.5 9.1 %collective-permute-start.15 = (bf16[288,256]{1,0:T(8,128)(2,1)S(1)}, bf16[288,256]{1,0:T(8,128)(2,1)S(1)}, u32[]{:S(2)}, u32[]{:S(2)}) collective-permute-start(bf16[288,256]{1,0:T(8,128)(2,1)S(1)} %get-tuple-element.27.rest_0_), channel_id=1, source_target_pairs={{14,0},{15,1},{12,2},{13,3},{2,4},{3,5},{0,6},{1,7},{6,8},{7,9},{4... | collective-permute-start | bytes 442376 | tf_op jit(solution)/shard_map/ppermute | solution.py:80
  67.3 9.0 %collective-permute-start.11 = (bf16[288,256]{1,0:T(8,128)(2,1)S(1)}, bf16[288,256]{1,0:T(8,128)(2,1)S(1)}, u32[]{:S(2)}, u32[]{:S(2)}) collective-permute-start(bf16[288,256]{1,0:T(8,128)(2,1)S(1)} %get-tuple-element.27.rest_0_), channel_id=1, source_target_pairs={{2,0},{3,1},{0,2},{1,3},{6,4},{7,5},{4,6},{5,7},{10,8},{11,9},{8,1... | collective-permute-start | bytes 442376 | tf_op jit(solution)/shard_map/ppermute | solution.py:80
  68.5 7.8 %collective-permute-start.13 = (bf16[288,256]{1,0:T(8,128)(2,1)S(1)}, bf16[288,256]{1,0:T(8,128)(2,1)S(1)}, u32[]{:S(2)}, u32[]{:S(2)}) collective-permute-start(bf16[288,256]{1,0:T(8,128)(2,1)S(1)} %get-tuple-element.27.rest_0_), channel_id=1, source_target_pairs={{12,0},{13,1},{14,2},{15,3},{0,4},{1,5},{2,6},{3,7},{4,8},{5,9},{6... | collective-permute-start | bytes 442376 | tf_op jit(solution)/shard_map/ppermute | solution.py:80
  70.4 8.7 %collective-permute-start.14 = (bf16[288,256]{1,0:T(8,128)(2,1)S(1)}, bf16[288,256]{1,0:T(8,128)(2,1)S(1)}, u32[]{:S(2)}, u32[]{:S(2)}) collective-permute-start(bf16[288,256]{1,0:T(8,128)(2,1)S(1)} %get-tuple-element.27.rest_0_), channel_id=1, source_target_pairs={{6,0},{7,1},{4,2},{5,3},{10,4},{11,5},{8,6},{9,7},{14,8},{15,9},{1... | collective-permute-start | bytes 442376 | tf_op jit(solution)/shard_map/ppermute | solution.py:80
  70.8 8.7 %collective-permute-start.16 = (bf16[288,256]{1,0:T(8,128)(2,1)S(1)}, bf16[288,256]{1,0:T(8,128)(2,1)S(1)}, u32[]{:S(2)}, u32[]{:S(2)}) collective-permute-start(bf16[288,256]{1,0:T(8,128)(2,1)S(1)} %collective-permute-done.12.rest_2_), channel_id=1, source_target_pairs={{4,0},{5,1},{6,2},{7,3},{8,4},{9,5},{10,6},{11,7},{12,8},{13,9},{1... | collective-permute-start | bytes 442376 | tf_op jit(solution)/shard_map/ppermute | solution.py:80
  71.6 7.9 %collective-permute-start.17 = (bf16[288,256]{1,0:T(8,128)(2,1)S(1)}, bf16[288,256]{1,0:T(8,128)(2,1)S(1)}, u32[]{:S(2)}, u32[]{:S(2)}) collective-permute-start(bf16[288,256]{1,0:T(8,128)(2,1)S(1)} %collective-permute-done.15.rest_5_), channel_id=1, source_target_pairs={{12,0},{13,1},{14,2},{15,3},{0,4},{1,5},{2,6},{3,7},{4,8},{5,9},{6... | collective-permute-start | bytes 442376 | tf_op jit(solution)/shard_map/ppermute | solution.py:80
  86.5 8.2 %copy-start.6 = (bf16[2,64,256]{2,1,0:T(8,128)(2,1)S(1)}, bf16[2,64,256]{2,1,0:T(8,128)(2,1)}, u32[]{:S(2)}) copy-start(bf16[2,64,256]{2,1,0:T(8,128)(2,1)} %own_up.1) | copy-start | bytes 196612
  88.0 1.3 %collective-permute-start.18 = (bf16[80,128]{1,0:T(8,128)(2,1)S(1)}, bf16[80,128]{1,0:T(8,128)(2,1)S(1)}, u32[]{:S(2)}, u32[]{:S(2)}) collective-permute-start(bf16[80,128]{1,0:T(8,128)(2,1)S(1)} %get-tuple-element.31), channel_id=1, source_target_pairs={{0,1},{1,0},{2,3},{3,2},{4,5},{5,4},{6,7},{7,6},{8,9},{9,8},{10,11... | collective-permute-start | bytes 61448 | tf_op jit(solution)/shard_map/ppermute | solution.py:420
  89.3 5.4 %collective-permute-start.19 = (bf16[80,128]{1,0:T(8,128)(2,1)S(1)}, bf16[80,128]{1,0:T(8,128)(2,1)S(1)}, u32[]{:S(2)}, u32[]{:S(2)}) collective-permute-start(bf16[80,128]{1,0:T(8,128)(2,1)S(1)} %add_convert_fusion.2.a), channel_id=1, source_target_pairs={{0,128},{128,0},{1,129},{129,1},{2,130},{130,2},{3,131},{131,3},{4... | collective-permute-start | bytes 61448 | tf_op jit(solution)/shard_map/ppermute | solution.py:423
Sparse Core Ops, SparseCore 0:
  10.8 42.4 all-gather.2

commit v3 on v2

--- a/solution.py
+++ b/solution.py
@@ -89,6 +89,9 @@
     return [value, across, up, down, up_across, down_across, far, far_across]
 
 
+SNAKE = [4 * y + 2 * (i ^ (y % 2)) + core for y in range(4) for i in range(2) for core in range(2)]
+
+
 def pack_body(place, up, down, out_up, out):
     def columns(main, tail, at):
         for t in range(2):
@@ -203,11 +206,12 @@
 ):
     chip, core, head = ids[CHIP], ids[CORE], ids[HEAD_ID]
     for src in range(CHIPS):
+        even, odd = SNAKE.index(2 * src), SNAKE.index(2 * src + 1)
         for t, up in enumerate((up0, up1)):
             lanes = slice(t * HEAD, (t + 1) * HEAD)
-            upb[src, t, :, : 2 * HEAD] = up[2 * src, 0]
-            upb[src, t, :, 2 * HEAD : 3 * HEAD] = tail[2 * src, 0, :, lanes] + tail[2 * src + 1, 0, :, lanes]
-            upb[src, t, :, 3 * HEAD :] = up[2 * src + 1, 0]
+            upb[src, t, :, : 2 * HEAD] = up[even, 0]
+            upb[src, t, :, 2 * HEAD : 3 * HEAD] = tail[even, 0, :, lanes] + tail[odd, 0, :, lanes]
+            upb[src, t, :, 3 * HEAD :] = up[odd, 0]
     own_rows, oth_rows = aligned(core, BLOCK), aligned(1 - core, BLOCK)
 
     def low(rows):
@@ -323,13 +327,13 @@
                 acc = acc + nn(weights, values[rows, :])
             ctx[:, aligned(j, HEAD)] = (acc[:, :HEAD] / acc[:, HEAD:]).astype(BF16)
 
-        def two_heads(i, carry):
-            scores = [head_scores(2 * i + e) for e in range(2)]
-            for e in range(2):
-                head_context(2 * i + e, scores[e])
+        def some_heads(i, carry):
+            scores = [head_scores(4 * i + e) for e in range(4)]
+            for e in range(4):
+                head_context(4 * i + e, scores[e])
             return carry
 
-        lax.fori_loop(0, HEADS // 2, two_heads, 0)
+        lax.fori_loop(0, HEADS // 4, some_heads, 0)
 
     for chips in range(2, CHIPS + 1, 2):
         pl.when(chip // 2 == chips // 2 - 1)(lambda chips=chips: branch(chips))
@@ -359,17 +363,20 @@
     parts = HEADS * HEAD // CHUNK
     rows = row_ctx[...].astype(BF16)
 
+    def place(i):
+        return i ^ (2 * core)
+
     def block(at, t):
         total = jnp.zeros((RANK, BLOCK), F32)
         for i in range(parts):
-            total += nt(jnp.where(t == 1, down1[i, 0], down0[i, 0]), ctx[aligned(at, BLOCK), i * CHUNK : (i + 1) * CHUNK])
+            total += nt(jnp.where(t == 1, down1[place(i), 0], down0[place(i), 0]), ctx[aligned(at, BLOCK), i * CHUNK : (i + 1) * CHUNK])
         return total.astype(BF16)
 
     row_terms = []
     for t in range(2):
         total = jnp.zeros((ROWS, RANK), F32)
         for i in range(parts):
-            total += nt(rows[:, i * CHUNK : (i + 1) * CHUNK], (down0, down1)[t][i, 0])
+            total += nt(rows[:, i * CHUNK : (i + 1) * CHUNK], (down0, down1)[t][place(i), 0])
         row_terms.append(total)
     row_part = jnp.where(row_mask(ids, ROWS, RANK), row_terms[1], row_terms[0]).astype(BF16)
     for out, at, t in ((own_out, core, ids[OWN]), (oth_out, 1 - core, oth[0])):
@@ -382,7 +389,7 @@
     total = a[...].astype(F32) + b[...].astype(F32)
     factor = jnp.transpose(total[:RANK]).astype(BF16)
     for i in range(2 * CHIPS):
-        out[:, i * CHUNK : (i + 1) * CHUNK] = nn(factor, up[i, 0]).astype(BF16)
+        out[:, i * CHUNK : (i + 1) * CHUNK] = nn(factor, up[SNAKE.index(i), 0]).astype(BF16)
     rows = total[RANK:, :RANK].astype(BF16)
     terms = [nn(rows, own_up[t]) for t in range(2)]
     row_out[...] = jnp.where(row_mask(ids, ROWS, CHUNK), terms[1], terms[0])[:LIVE].astype(BF16)
@@ -439,7 +446,7 @@
         [shape((7, RANK, CHUNK))],
         limit=48,
     )
-    weights = lax.all_gather(weights, "blk")
+    weights = lax.all_gather(weights, "blk", axis_index_groups=[SNAKE])
     arrived = from_row(down, 1)
     downs = [down, arrived, from_row(down, 3), from_row(down, 2)]
     hid, core_hid, x_hid, cross_hid = call(
@@ -493,7 +500,7 @@
         + [spec((2 * CHIPS, 1, RANK, CHUNK), lambda s, i=i: (0, i, 0, 0)) for i in range(3)],
         [shape((2 * BLOCK, HEADS * HEAD)), shape((2 * BLOCK + HEADS * LIVE, 2 * HEAD))],
         [pltpu.VMEM((CHIPS, 2, RANK, 5 * HEAD), BF16)],
-        48,
+        58,
     )
     kvs = gather_chips(kv)
     ctx, row_ctx = call(

time: 104 us -> 108 us (1.038)
  local copies, waits for them, and re-layouts: 10.1 us -> 13.6 us
  Pallas kernels: 18.9 us -> 21.2 us
  waiting for transfers between devices: 33.1 us -> 32 us
    unnamed x26 -> x42, local copies, waits for them, and re-layouts: 8.5 us -> 11.3 us
    pallas_call x8, Pallas kernels: 18.9 us -> 21.2 us  [call(): pl.pallas_call(body, grid_spec=pltpu.PrefetchScalarGridSpec(num_scalar_pr...]
where the time goes in v3:
time: 108 us
  waiting for transfers between devices  32 us (30%)
  starting transfers between devices  26.1 us (24%)
  Pallas kernels  21.2 us (20%)
  between operations  14.9 us (14%)
  local copies, waits for them, and re-layouts  13.6 us (13%)
    pallas_call x8, Pallas kernels, call(): pl.pallas_call(body, grid_spec=pltpu.PrefetchScalarGridSpec(num_scalar_pr...  21.2 us
    ppermute x7, starting transfers between devices, get(): return lax.ppermute(value, 'blk', pairs)  12.4 us
    unnamed x42, local copies, waits for them, and re-layouts  11.3 us
    ppermute x3, waiting for transfers between devices, from_row(): return lax.ppermute(value, 'blk', pairs)  11.1 us
    ppermute x2, starting transfers between devices, to_role(): return lax.ppermute(value, 'role', [(0, 1), (1, 0)])  5.6 us
    ppermute x2, waiting for transfers between devices, to_role(): return lax.ppermute(value, 'role', [(0, 1), (1, 0)])  5.22 us
    ppermute x7, waiting for transfers between devices, get(): return lax.ppermute(value, 'blk', pairs)  4.63 us
    ppermute x1, waiting for transfers between devices, per_device(): lax.ppermute(cross_hid, 'blk', [(i, i ^ 3) for i in range(2 * CHIPS)])  4.55 us
  transfers between devices with their start and end apart: 21, of which 13 were waited for; matrix products, arithmetic and copies ran while one was open for 2% of the time, Pallas kernels for 5%

profile of v3, /device:TPU:248, one launch (start us, length us, event | category | flops | bytes accessed | tf_op | source)
XLA Modules:
  0.0 107.9 jit_solution(14222699526356586798)
XLA Ops:
  7.2 0.9 copy-done.6
  8.2 0.9 copy-done.12
  9.1 0.8 copy-done.13
  9.9 0.7 shard_map.134
  10.6 0.8 collective-permute-start.4
  12.1 1.2 %copy-done.2 = bf16[128,4096]{1,0:T(8,128)(2,1)S(1)} copy-done((bf16[128,4096]{1,0:T(8,128)(2,1)S(1)}, bf16[128,4096]{1,0:T(8,128)(2,1)}, u32[]{:S(2)}) %copy-start.2) | copy-done | bytes 1048600
  13.3 1.2 %shard_map.131 = (bf16[144,1024]{1,0:T(8,128)(2,1)S(1)}, bf16[144,1024]{1,0:T(8,128)(2,1)}, bf16[144,1024]{1,0:T(8,128)(2,1)}, bf16[144,1024]{1,0:T(8,128)(2,1)}) custom-call(s32[1]{0:T(128)} %bitcast.5.place, s32[1]{0:T(128)S(6)} %copy.14.adapter, bf16[128,4096]{1,0:T(8,128)(2,1)S(1)} %copy-done.2), custom_call_target="tpu_custom_call" | custom-call | tf_op jit(solution)/shard_map/pallas_call | solution.py:44
  14.6 1.6 %collective-permute-start.2 = (bf16[144,1024]{1,0:T(8,128)(2,1)}, bf16[144,1024]{1,0:T(8,128)(2,1)S(1)}, u32[]{:S(2)}, u32[]{:S(2)}) collective-permute-start(bf16[144,1024]{1,0:T(8,128)(2,1)} %get-tuple-element.19), channel_id=1, source_target_pairs={{0,2},{1,3},{2,0},{3,1},{4,6},{5,7},{6,4},{7,5},{8,10},{9,11},{10,... | collective-permute-start | bytes 884744 | tf_op jit(solution)/shard_map/ppermute | solution.py:434
  16.5 2.5 %collective-permute-start.5 = (bf16[2,192,256]{2,1,0:T(8,128)(2,1)}, bf16[2,192,256]{2,1,0:T(8,128)(2,1)}, u32[]{:S(2)}, u32[]{:S(2)}) collective-permute-start(bf16[2,192,256]{2,1,0:T(8,128)(2,1)} %bitcast.16), channel_id=1, source_target_pairs={{12,0},{13,1},{14,2},{15,3},{0,4},{1,5},{2,6},{3,7},{4,8},{5,9},{6... | collective-permute-start | bytes 589832 | tf_op jit(solution)/shard_map/ppermute | solution.py:438
  19.0 0.7 copy-done.9
  19.7 0.9 pad.8.row_hid
  20.6 0.8 concatenate.3.ids
  21.3 3.7 %collective-permute-done.5.w3 = bf16[2,192,256]{2,1,0:T(8,128)(2,1)} collective-permute-done((bf16[2,192,256]{2,1,0:T(8,128)(2,1)}, bf16[2,192,256]{2,1,0:T(8,128)(2,1)}, u32[]{:S(2)}, u32[]{:S(2)}) %collective-permute-start.5) | collective-permute-done | bytes 196640 | tf_op jit(solution)/shard_map/ppermute | solution.py:438
  25.0 7.4 %collective-permute-done.6.w2 = bf16[2,192,256]{2,1,0:T(8,128)(2,1)} collective-permute-done((bf16[2,192,256]{2,1,0:T(8,128)(2,1)}, bf16[2,192,256]{2,1,0:T(8,128)(2,1)}, u32[]{:S(2)}, u32[]{:S(2)}) %collective-permute-start.6) | collective-permute-done | bytes 196640 | tf_op jit(solution)/shard_map/ppermute | solution.py:438
  32.4 4.5 %collective-permute-done.3.by_cross = bf16[144,1024]{1,0:T(8,128)(2,1)S(1)} collective-permute-done((bf16[144,1024]{1,0:T(8,128)(2,1)}, bf16[144,1024]{1,0:T(8,128)(2,1)S(1)}, u32[]{:S(2)}, u32[]{:S(2)}) %collective-permute-start.3) | collective-permute-done | bytes 294944 | tf_op jit(solution)/shard_map/ppermute | solution.py:462
  37.0 0.9 copy-done.8
  37.9 0.9 copy-done.10
  38.9 2.9 %shard_map.132 = (bf16[416,128]{1,0:T(8,128)(2,1)S(1)}, bf16[416,128]{1,0:T(8,128)(2,1)S(1)}) custom-call(s32[13]{0:T(128)S(1)} %concatenate.3.ids, bf16[144,1024]{1,0:T(8,128)(2,1)S(1)} %get-tuple-element.17.own, bf16[144,1024]{1,0:T(8,128)(2,1)S(1)} %collective-permute-done.1.by_core, bf16[144,1024]{1,0:T(8,128)(2,1)S(1)} %collective-permute-done.2.by_x, ...), custom_call_target="tpu_custom_call" | custom-call | tf_op jit(solution)/shard_map/pallas_call | solution.py:44
  41.8 1.1 collective-permute-start.7
  42.9 0.9 shard_map.133
  43.8 0.8 copy-done.4
  44.6 1.3 %collective-permute-start.10 = (bf16[128,2048]{1,0:T(8,128)(2,1)S(1)}, bf16[128,2048]{1,0:T(8,128)(2,1)S(1)}, u32[]{:S(2)}, u32[]{:S(2)}) collective-permute-start(bf16[128,2048]{1,0:T(8,128)(2,1)S(1)} %get-tuple-element.25), channel_id=1, source_target_pairs={{0,1},{1,0},{2,3},{3,2},{4,5},{5,4},{6,7},{7,6},{8,9},{9,8},{10,11... | collective-permute-start | bytes 1572872 | tf_op jit(solution)/shard_map/ppermute | solution.py:427
  45.9 3.7 %collective-permute-done.7 = bf16[416,128]{1,0:T(8,128)(2,1)S(1)} collective-permute-done((bf16[416,128]{1,0:T(8,128)(2,1)S(1)}, bf16[416,128]{1,0:T(8,128)(2,1)S(1)}, u32[]{:S(2)}, u32[]{:S(2)}) %collective-permute-start.7) | collective-permute-done | bytes 106528 | tf_op jit(solution)/shard_map/ppermute | solution.py:434
  49.7 0.3 collective-permute-start.8
  50.0 1.1 %collective-permute-done.8 = bf16[416,128]{1,0:T(8,128)(2,1)S(1)} collective-permute-done((bf16[416,128]{1,0:T(8,128)(2,1)S(1)}, bf16[416,128]{1,0:T(8,128)(2,1)S(1)}, u32[]{:S(2)}, u32[]{:S(2)}) %collective-permute-start.8) | collective-permute-done | bytes 106528 | tf_op jit(solution)/shard_map/ppermute | solution.py:427
  51.1 2.6 %collective-permute-start.9 = (bf16[416,128]{1,0:T(8,128)(2,1)S(1)}, bf16[416,128]{1,0:T(8,128)(2,1)S(1)}, u32[]{:S(2)}, u32[]{:S(2)}) collective-permute-start(bf16[416,128]{1,0:T(8,128)(2,1)S(1)} %add_convert_fusion.mine), channel_id=1, source_target_pairs={{0,128},{128,0},{1,129},{129,1},{2,130},{130,2},{3,131},{131,3},{4... | collective-permute-start | bytes 319496 | tf_op jit(solution)/shard_map/ppermute | solution.py:430
  53.7 0.7 pad.9.rq.rk.rv
  54.4 0.5 collective-permute-done.oth
  54.9 2.8 %collective-permute-done.9.theirs = bf16[416,128]{1,0:T(8,128)(2,1)S(1)} collective-permute-done((bf16[416,128]{1,0:T(8,128)(2,1)S(1)}, bf16[416,128]{1,0:T(8,128)(2,1)S(1)}, u32[]{:S(2)}, u32[]{:S(2)}) %collective-permute-start.9) | collective-permute-done | bytes 106528 | tf_op jit(solution)/shard_map/ppermute | solution.py:430
  57.8 0.6 copy-done.19
  58.6 5.5 %shard_map.135 = (bf16[256,1024]{1,0:T(8,128)(2,1)}, bf16[288,256]{1,0:T(8,128)(2,1)}) custom-call(s32[13]{0:T(128)} %copy-done.14, s32[1]{0:T(128)} %collective-permute-done.oth, bf16[416,128]{1,0:T(8,128)(2,1)} %copy-done.18, bf16[416,128]{1,0:T(8,128)(2,1)} %copy-done.19, bf16[128,2048]{1,0:T(8,128)(2,1)} %copy-done.4, bf16[128,2048]{1,0:T(8,128)(2,1)} %copy-done.17, ...), custom_call_target="tpu_custom_call" | custom-call | tf_op jit(solution)/shard_map/pallas_call | solution.py:44
  64.1 4.7 %collective-permute-start.15 = (bf16[288,256]{1,0:T(8,128)(2,1)}, bf16[288,256]{1,0:T(8,128)(2,1)S(1)}, u32[]{:S(2)}, u32[]{:S(2)}) collective-permute-start(bf16[288,256]{1,0:T(8,128)(2,1)} %get-tuple-element.27.rest_0_), channel_id=1, source_target_pairs={{14,0},{15,1},{12,2},{13,3},{2,4},{3,5},{0,6},{1,7},{6,8},{7,9},{4... | collective-permute-start | bytes 442376 | tf_op jit(solution)/shard_map/ppermute | solution.py:80
  68.8 1.2 %collective-permute-start.11 = (bf16[288,256]{1,0:T(8,128)(2,1)}, bf16[288,256]{1,0:T(8,128)(2,1)S(1)}, u32[]{:S(2)}, u32[]{:S(2)}) collective-permute-start(bf16[288,256]{1,0:T(8,128)(2,1)} %get-tuple-element.27.rest_0_), channel_id=1, source_target_pairs={{2,0},{3,1},{0,2},{1,3},{6,4},{7,5},{4,6},{5,7},{10,8},{11,9},{8,1... | collective-permute-start | bytes 442376 | tf_op jit(solution)/shard_map/ppermute | solution.py:80
  70.0 2.0 %collective-permute-start.13 = (bf16[288,256]{1,0:T(8,128)(2,1)}, bf16[288,256]{1,0:T(8,128)(2,1)S(1)}, u32[]{:S(2)}, u32[]{:S(2)}) collective-permute-start(bf16[288,256]{1,0:T(8,128)(2,1)} %get-tuple-element.27.rest_0_), channel_id=1, source_target_pairs={{12,0},{13,1},{14,2},{15,3},{0,4},{1,5},{2,6},{3,7},{4,8},{5,9},{6... | collective-permute-start | bytes 442376 | tf_op jit(solution)/shard_map/ppermute | solution.py:80
  72.3 1.1 %collective-permute-done.15.rest_5_ = bf16[288,256]{1,0:T(8,128)(2,1)S(1)} collective-permute-done((bf16[288,256]{1,0:T(8,128)(2,1)}, bf16[288,256]{1,0:T(8,128)(2,1)S(1)}, u32[]{:S(2)}, u32[]{:S(2)}) %collective-permute-start.15) | collective-permute-done | bytes 147488 | tf_op jit(solution)/shard_map/ppermute | solution.py:80
  73.4 4.2 %collective-permute-start.17 = (bf16[288,256]{1,0:T(8,128)(2,1)S(1)}, bf16[288,256]{1,0:T(8,128)(2,1)S(1)}, u32[]{:S(2)}, u32[]{:S(2)}) collective-permute-start(bf16[288,256]{1,0:T(8,128)(2,1)S(1)} %collective-permute-done.15.rest_5_), channel_id=1, source_target_pairs={{12,0},{13,1},{14,2},{15,3},{0,4},{1,5},{2,6},{3,7},{4,8},{5,9},{6... | collective-permute-start | bytes 442376 | tf_op jit(solution)/shard_map/ppermute | solution.py:80
  77.6 0.4 collective-permute-done.11.rest_1_
  78.1 2.9 %collective-permute-done.14.rest_4_ = bf16[288,256]{1,0:T(8,128)(2,1)S(1)} collective-permute-done((bf16[288,256]{1,0:T(8,128)(2,1)}, bf16[288,256]{1,0:T(8,128)(2,1)S(1)}, u32[]{:S(2)}, u32[]{:S(2)}) %collective-permute-start.14) | collective-permute-done | bytes 147488 | tf_op jit(solution)/shard_map/ppermute | solution.py:80
  81.1 1.0 copy-done.5
  82.2 0.9 copy-done.11
  83.1 0.7 copy-done.15
  83.8 6.4 %shard_map.136 = (bf16[256,1024]{1,0:T(8,128)(2,1)S(1)}, f32[16,1024]{1,0:T(8,128)S(1)}) custom-call(s32[13]{0:T(128)S(1)} %copy-done.15, bf16[256,1024]{1,0:T(8,128)(2,1)S(1)} %copy-done.5, bf16[288,256]{1,0:T(8,128)(2,1)S(1)} %copy-done.11, bf16[288,256]{1,0:T(8,128)(2,1)S(1)} %collective-permute-done.11.rest_1_, ...), custom_call_target="tpu_custom_call" | custom-call | tf_op jit(solution)/shard_map/pallas_call | solution.py:44
  90.1 0.6 copy-done.16
  90.8 1.6 %shard_map.137 = (bf16[80,128]{1,0:T(8,128)(2,1)S(1)}, bf16[80,128]{1,0:T(8,128)(2,1)S(1)}) custom-call(s32[13]{0:T(128)S(1)} %copy-done.16, s32[1]{0:T(128)} %collective-permute-done.oth, bf16[256,1024]{1,0:T(8,128)(2,1)S(1)} %get-tuple-element.28.ctx, f32[16,1024]{1,0:T(8,128)S(1)} %get-tuple-element.29.row_ctx, bf16[16,7,64,256]{3,2,1,0:T(8,128)(2,1)S(1)} %bitcast.12, ...), custom_call_target="tpu_custom_call" | custom-call | tf_op jit(solution)/shard_map/pallas_call | solution.py:44
  92.5 1.2 %collective-permute-done.18 = bf16[80,128]{1,0:T(8,128)(2,1)S(1)} collective-permute-done((bf16[80,128]{1,0:T(8,128)(2,1)S(1)}, bf16[80,128]{1,0:T(8,128)(2,1)S(1)}, u32[]{:S(2)}, u32[]{:S(2)}) %collective-permute-start.18) | collective-permute-done | bytes 20512 | tf_op jit(solution)/shard_map/ppermute | solution.py:427
  93.7 3.0 %collective-permute-start.19 = (bf16[80,128]{1,0:T(8,128)(2,1)S(1)}, bf16[80,128]{1,0:T(8,128)(2,1)S(1)}, u32[]{:S(2)}, u32[]{:S(2)}) collective-permute-start(bf16[80,128]{1,0:T(8,128)(2,1)S(1)} %add_convert_fusion.2.a), channel_id=1, source_target_pairs={{0,128},{128,0},{1,129},{129,1},{2,130},{130,2},{3,131},{131,3},{4... | collective-permute-start | bytes 61448 | tf_op jit(solution)/shard_map/ppermute | solution.py:430
  96.7 2.4 %collective-permute-done.19.b = bf16[80,128]{1,0:T(8,128)(2,1)S(1)} collective-permute-done((bf16[80,128]{1,0:T(8,128)(2,1)S(1)}, bf16[80,128]{1,0:T(8,128)(2,1)S(1)}, u32[]{:S(2)}, u32[]{:S(2)}) %collective-permute-start.19) | collective-permute-done | bytes 20512 | tf_op jit(solution)/shard_map/ppermute | solution.py:430
  99.1 2.0 %shard_map.138 = (bf16[128,4096]{1,0:T(8,128)(2,1)}, bf16[4,256]{1,0:T(4,128)(2,1)}) custom-call(s32[13]{0:T(128)S(1)} %copy-done.16, bf16[80,128]{1,0:T(8,128)(2,1)S(1)} %add_convert_fusion.2.a, bf16[80,128]{1,0:T(8,128)(2,1)S(1)} %collective-permute-done.19.b, bf16[16,7,64,256]{3,2,1,0:T(8,128)(2,1)S(1)} %bitcast.14, bf16[2,64,256]{2,1,0:T(8,128)(2,1)S(1)} %copy-done.7), custom_call_target="tpu_custom_call" | custom-call | tf_op jit(solution)/shard_map/pallas_call | solution.py:44
  (51 shorter events, 1.4 us)
Async XLA Ops:
  7.2 35.7 %copy-start.1 = (bf16[128,5120]{1,0:T(8,128)(2,1)S(1)}, bf16[128,5120]{1,0:T(8,128)(2,1)}, u32[]{:S(2)}) copy-start(bf16[128,5120]{1,0:T(8,128)(2,1)} %qkv.1) | copy-start | bytes 3932164
  7.2 50.6 %all-gather.3.cloned.1.call-start = ((), (), s32[]{:S(2)}) async-start(), calls=%async_computation | async-start | bytes 3899392 | tf_op jit(solution)/shard_map/all_gather | solution.py:449
  7.2 0.9 copy-start.6
  8.2 0.9 copy-start.12
  9.1 0.8 copy-start.13
  10.6 8.4 %collective-permute-start.4 = (bf16[2,192,256]{2,1,0:T(8,128)(2,1)}, bf16[2,192,256]{2,1,0:T(8,128)(2,1)S(1)}, u32[]{:S(2)}, u32[]{:S(2)}) collective-permute-start(bf16[2,192,256]{2,1,0:T(8,128)(2,1)} %bitcast.15), channel_id=1, source_target_pairs={{4,0},{5,1},{6,2},{7,3},{8,4},{9,5},{10,6},{11,7},{12,8},{13,9},{1... | collective-permute-start | bytes 589832 | tf_op jit(solution)/shard_map/ppermute | solution.py:438
  12.1 1.2 %copy-start.2 = (bf16[128,4096]{1,0:T(8,128)(2,1)S(1)}, bf16[128,4096]{1,0:T(8,128)(2,1)}, u32[]{:S(2)}) copy-start(bf16[128,4096]{1,0:T(8,128)(2,1)} %hid.1) | copy-start | bytes 3145732
  13.3 29.5 %copy-start.3 = (bf16[3,128,1024]{2,1,0:T(8,128)(2,1)S(1)}, bf16[3,128,1024]{2,1,0:T(8,128)(2,1)}, u32[]{:S(2)}) copy-start(bf16[3,128,1024]{2,1,0:T(8,128)(2,1)} %cache.1) | copy-start | bytes 2359300
  14.5 17.9 %collective-permute-start.1 = (bf16[144,1024]{1,0:T(8,128)(2,1)}, bf16[144,1024]{1,0:T(8,128)(2,1)S(1)}, u32[]{:S(2)}, u32[]{:S(2)}) collective-permute-start(bf16[144,1024]{1,0:T(8,128)(2,1)} %get-tuple-element.18), channel_id=1, source_target_pairs={{0,1},{1,0},{2,3},{3,2},{4,5},{5,4},{6,7},{7,6},{8,9},{9,8},{10,11... | collective-permute-start | bytes 884744 | tf_op jit(solution)/shard_map/ppermute | solution.py:427
  14.6 17.8 %collective-permute-start.2 = (bf16[144,1024]{1,0:T(8,128)(2,1)}, bf16[144,1024]{1,0:T(8,128)(2,1)S(1)}, u32[]{:S(2)}, u32[]{:S(2)}) collective-permute-start(bf16[144,1024]{1,0:T(8,128)(2,1)} %get-tuple-element.19), channel_id=1, source_target_pairs={{0,2},{1,3},{2,0},{3,1},{4,6},{5,7},{6,4},{7,5},{8,10},{9,11},{10,... | collective-permute-start | bytes 884744 | tf_op jit(solution)/shard_map/ppermute | solution.py:434
  16.2 20.8 %collective-permute-start.3 = (bf16[144,1024]{1,0:T(8,128)(2,1)}, bf16[144,1024]{1,0:T(8,128)(2,1)S(1)}, u32[]{:S(2)}, u32[]{:S(2)}) collective-permute-start(bf16[144,1024]{1,0:T(8,128)(2,1)} %get-tuple-element.20), channel_id=1, source_target_pairs={{0,3},{1,2},{2,1},{3,0},{4,7},{5,6},{6,5},{7,4},{8,11},{9,10},{10,... | collective-permute-start | bytes 884744 | tf_op jit(solution)/shard_map/ppermute | solution.py:462
  16.5 8.6 %collective-permute-start.5 = (bf16[2,192,256]{2,1,0:T(8,128)(2,1)}, bf16[2,192,256]{2,1,0:T(8,128)(2,1)}, u32[]{:S(2)}, u32[]{:S(2)}) collective-permute-start(bf16[2,192,256]{2,1,0:T(8,128)(2,1)} %bitcast.16), channel_id=1, source_target_pairs={{12,0},{13,1},{14,2},{15,3},{0,4},{1,5},{2,6},{3,7},{4,8},{5,9},{6... | collective-permute-start | bytes 589832 | tf_op jit(solution)/shard_map/ppermute | solution.py:438
  19.0 0.7 copy-start.9
  19.7 12.8 %collective-permute-start.6 = (bf16[2,192,256]{2,1,0:T(8,128)(2,1)}, bf16[2,192,256]{2,1,0:T(8,128)(2,1)}, u32[]{:S(2)}, u32[]{:S(2)}) collective-permute-start(bf16[2,192,256]{2,1,0:T(8,128)(2,1)} %bitcast.17), channel_id=1, source_target_pairs={{8,0},{9,1},{10,2},{11,3},{12,4},{13,5},{14,6},{15,7},{0,8},{1,9},... | collective-permute-start | bytes 589832 | tf_op jit(solution)/shard_map/ppermute | solution.py:438
  21.3 36.5 %copy-start.14 = (s32[13]{0:T(128)}, s32[13]{0:T(128)S(1)}, u32[]{:S(2)}) copy-start(s32[13]{0:T(128)S(1)} %concatenate.3.ids) | copy-start | bytes 160
  37.0 0.9 copy-start.8
  37.9 0.9 copy-start.10
  38.9 14.9 %copy-start.20 = (bf16[4,5120]{1,0:T(4,128)(2,1)S(1)}, bf16[4,5120]{1,0:T(4,128)(2,1)}, u32[]{:S(2)}) copy-start(bf16[4,5120]{1,0:T(4,128)(2,1)} %param.16) | copy-start | bytes 122884
  41.8 7.8 %collective-permute-start.7 = (bf16[416,128]{1,0:T(8,128)(2,1)S(1)}, bf16[416,128]{1,0:T(8,128)(2,1)S(1)}, u32[]{:S(2)}, u32[]{:S(2)}) collective-permute-start(bf16[416,128]{1,0:T(8,128)(2,1)S(1)} %get-tuple-element.22), channel_id=1, source_target_pairs={{0,2},{1,3},{2,0},{3,1},{4,6},{5,7},{6,4},{7,5},{8,10},{9,11},{10,... | collective-permute-start | bytes 319496 | tf_op jit(solution)/shard_map/ppermute | solution.py:434
  43.8 0.8 copy-start.4
  44.6 13.2 %collective-permute-start.10 = (bf16[128,2048]{1,0:T(8,128)(2,1)S(1)}, bf16[128,2048]{1,0:T(8,128)(2,1)S(1)}, u32[]{:S(2)}, u32[]{:S(2)}) collective-permute-start(bf16[128,2048]{1,0:T(8,128)(2,1)S(1)} %get-tuple-element.25), channel_id=1, source_target_pairs={{0,1},{1,0},{2,3},{3,2},{4,5},{5,4},{6,7},{7,6},{8,9},{9,8},{10,11... | collective-permute-start | bytes 1572872 | tf_op jit(solution)/shard_map/ppermute | solution.py:427
  49.7 1.4 %collective-permute-start.8 = (bf16[416,128]{1,0:T(8,128)(2,1)S(1)}, bf16[416,128]{1,0:T(8,128)(2,1)S(1)}, u32[]{:S(2)}, u32[]{:S(2)}) collective-permute-start(bf16[416,128]{1,0:T(8,128)(2,1)S(1)} %add_convert_fusion.1), channel_id=1, source_target_pairs={{0,1},{1,0},{2,3},{3,2},{4,5},{5,4},{6,7},{7,6},{8,9},{9,8},{10,11... | collective-permute-start | bytes 319496 | tf_op jit(solution)/shard_map/ppermute | solution.py:427
  51.1 6.7 %copy-start.18 = (bf16[416,128]{1,0:T(8,128)(2,1)}, bf16[416,128]{1,0:T(8,128)(2,1)S(1)}, u32[]{:S(2)}) copy-start(bf16[416,128]{1,0:T(8,128)(2,1)S(1)} %add_convert_fusion.mine) | copy-start | bytes 319492
  51.1 6.7 %collective-permute-start.9 = (bf16[416,128]{1,0:T(8,128)(2,1)S(1)}, bf16[416,128]{1,0:T(8,128)(2,1)S(1)}, u32[]{:S(2)}, u32[]{:S(2)}) collective-permute-start(bf16[416,128]{1,0:T(8,128)(2,1)S(1)} %add_convert_fusion.mine), channel_id=1, source_target_pairs={{0,128},{128,0},{1,129},{129,1},{2,130},{130,2},{3,131},{131,3},{4... | collective-permute-start | bytes 319496 | tf_op jit(solution)/shard_map/ppermute | solution.py:430
  53.7 1.2 %collective-permute-start = (s32[1]{0:T(128)}, s32[1]{0:T(128)}, u32[]{:S(2)}, u32[]{:S(2)}) collective-permute-start(s32[1]{0:T(128)} %param.14), channel_id=1, source_target_pairs={{0,1},{1,0},{2,3},{3,2},{4,5},{5,4},{6,7},{7,6},{8,9},{9,8},{10,11... | collective-permute-start | bytes 20 | tf_op jit(solution)/shard_map/ppermute | solution.py:427
  57.8 0.6 copy-start.19
  57.8 0.8 copy-start.17
  58.6 31.5 %copy-start = (bf16[112,64,256]{2,1,0:T(8,128)(2,1)S(1)}, bf16[112,64,256]{2,1,0:T(8,128)(2,1)}, u32[]{:S(2)}) copy-start(bf16[112,64,256]{2,1,0:T(8,128)(2,1)} %all-gather.3.cloned.1.call-done) | copy-start | bytes 11010052
  64.1 8.2 %collective-permute-start.12 = (bf16[288,256]{1,0:T(8,128)(2,1)}, bf16[288,256]{1,0:T(8,128)(2,1)S(1)}, u32[]{:S(2)}, u32[]{:S(2)}) collective-permute-start(bf16[288,256]{1,0:T(8,128)(2,1)} %get-tuple-element.27.rest_0_), channel_id=1, source_target_pairs={{4,0},{5,1},{6,2},{7,3},{8,4},{9,5},{10,6},{11,7},{12,8},{13,9},{1... | collective-permute-start | bytes 442376 | tf_op jit(solution)/shard_map/ppermute | solution.py:80
  64.1 9.3 %collective-permute-start.15 = (bf16[288,256]{1,0:T(8,128)(2,1)}, bf16[288,256]{1,0:T(8,128)(2,1)S(1)}, u32[]{:S(2)}, u32[]{:S(2)}) collective-permute-start(bf16[288,256]{1,0:T(8,128)(2,1)} %get-tuple-element.27.rest_0_), channel_id=1, source_target_pairs={{14,0},{15,1},{12,2},{13,3},{2,4},{3,5},{0,6},{1,7},{6,8},{7,9},{4... | collective-permute-start | bytes 442376 | tf_op jit(solution)/shard_map/ppermute | solution.py:80
  68.8 9.3 %collective-permute-start.11 = (bf16[288,256]{1,0:T(8,128)(2,1)}, bf16[288,256]{1,0:T(8,128)(2,1)S(1)}, u32[]{:S(2)}, u32[]{:S(2)}) collective-permute-start(bf16[288,256]{1,0:T(8,128)(2,1)} %get-tuple-element.27.rest_0_), channel_id=1, source_target_pairs={{2,0},{3,1},{0,2},{1,3},{6,4},{7,5},{4,6},{5,7},{10,8},{11,9},{8,1... | collective-permute-start | bytes 442376 | tf_op jit(solution)/shard_map/ppermute | solution.py:80
  70.0 8.1 %collective-permute-start.13 = (bf16[288,256]{1,0:T(8,128)(2,1)}, bf16[288,256]{1,0:T(8,128)(2,1)S(1)}, u32[]{:S(2)}, u32[]{:S(2)}) collective-permute-start(bf16[288,256]{1,0:T(8,128)(2,1)} %get-tuple-element.27.rest_0_), channel_id=1, source_target_pairs={{12,0},{13,1},{14,2},{15,3},{0,4},{1,5},{2,6},{3,7},{4,8},{5,9},{6... | collective-permute-start | bytes 442376 | tf_op jit(solution)/shard_map/ppermute | solution.py:80
  72.0 8.9 %collective-permute-start.14 = (bf16[288,256]{1,0:T(8,128)(2,1)}, bf16[288,256]{1,0:T(8,128)(2,1)S(1)}, u32[]{:S(2)}, u32[]{:S(2)}) collective-permute-start(bf16[288,256]{1,0:T(8,128)(2,1)} %get-tuple-element.27.rest_0_), channel_id=1, source_target_pairs={{6,0},{7,1},{4,2},{5,3},{10,4},{11,5},{8,6},{9,7},{14,8},{15,9},{1... | collective-permute-start | bytes 442376 | tf_op jit(solution)/shard_map/ppermute | solution.py:80
  72.3 8.9 %collective-permute-start.16 = (bf16[288,256]{1,0:T(8,128)(2,1)S(1)}, bf16[288,256]{1,0:T(8,128)(2,1)S(1)}, u32[]{:S(2)}, u32[]{:S(2)}) collective-permute-start(bf16[288,256]{1,0:T(8,128)(2,1)S(1)} %collective-permute-done.12.rest_2_), channel_id=1, source_target_pairs={{4,0},{5,1},{6,2},{7,3},{8,4},{9,5},{10,6},{11,7},{12,8},{13,9},{1... | collective-permute-start | bytes 442376 | tf_op jit(solution)/shard_map/ppermute | solution.py:80
  73.4 7.7 %collective-permute-start.17 = (bf16[288,256]{1,0:T(8,128)(2,1)S(1)}, bf16[288,256]{1,0:T(8,128)(2,1)S(1)}, u32[]{:S(2)}, u32[]{:S(2)}) collective-permute-start(bf16[288,256]{1,0:T(8,128)(2,1)S(1)} %collective-permute-done.15.rest_5_), channel_id=1, source_target_pairs={{12,0},{13,1},{14,2},{15,3},{0,4},{1,5},{2,6},{3,7},{4,8},{5,9},{6... | collective-permute-start | bytes 442376 | tf_op jit(solution)/shard_map/ppermute | solution.py:80
  81.1 1.0 copy-start.5
  82.2 0.9 copy-start.11
  83.1 0.7 copy-start.15
  90.1 0.7 copy-start.16
  90.8 8.3 %copy-start.7 = (bf16[2,64,256]{2,1,0:T(8,128)(2,1)S(1)}, bf16[2,64,256]{2,1,0:T(8,128)(2,1)}, u32[]{:S(2)}) copy-start(bf16[2,64,256]{2,1,0:T(8,128)(2,1)} %own_up.1) | copy-start | bytes 196612
  92.4 1.3 %collective-permute-start.18 = (bf16[80,128]{1,0:T(8,128)(2,1)S(1)}, bf16[80,128]{1,0:T(8,128)(2,1)S(1)}, u32[]{:S(2)}, u32[]{:S(2)}) collective-permute-start(bf16[80,128]{1,0:T(8,128)(2,1)S(1)} %get-tuple-element.31), channel_id=1, source_target_pairs={{0,1},{1,0},{2,3},{3,2},{4,5},{5,4},{6,7},{7,6},{8,9},{9,8},{10,11... | collective-permute-start | bytes 61448 | tf_op jit(solution)/shard_map/ppermute | solution.py:427
  93.7 5.4 %collective-permute-start.19 = (bf16[80,128]{1,0:T(8,128)(2,1)S(1)}, bf16[80,128]{1,0:T(8,128)(2,1)S(1)}, u32[]{:S(2)}, u32[]{:S(2)}) collective-permute-start(bf16[80,128]{1,0:T(8,128)(2,1)S(1)} %add_convert_fusion.2.a), channel_id=1, source_target_pairs={{0,128},{128,0},{1,129},{129,1},{2,130},{130,2},{3,131},{131,3},{4... | collective-permute-start | bytes 61448 | tf_op jit(solution)/shard_map/ppermute | solution.py:430
Sparse Core Ops, SparseCore 0:
  10.8 42.4 all-gather.2

commit v4 on v2

--- a/solution.py
+++ b/solution.py
@@ -89,37 +89,45 @@
     return [value, across, up, down, up_across, down_across, far, far_across]
 
 
-def pack_body(place, up, down, out_up, out):
+def pack_body(
+    place, adapter, hid, up, down, out_up, own, to_core, to_x, to_cross, weights, hid_in, up_in, mixed, tenant, sems
+):
+    x, core = lax.rem(place[0] // 2, 2), lax.rem(place[0], 2)
+    copies = []
+
+    def move(src, dst):
+        copies.append(pltpu.make_async_copy(src, dst, sems.at[len(copies)]))
+        copies[-1].start()
+        return copies[-1]
+
+    reads = [
+        move(hid, hid_in),
+        move(up, up_in),
+        move(down, mixed.at[3:5]),
+        move(out_up, mixed.at[5:7]),
+    ]
+    tenant[...] = jnp.full((ROWS, 4 * CHUNK), adapter[0].astype(F32)).astype(BF16)
+    reads[0].wait()
+    writes = []
+    for out, dx, dc in ((to_x, 1, 0), (to_cross, 1, 1), (to_core, 0, 1), (own, 0, 0)):
+        for y in range(4):
+            chunk = 4 * y + 2 * (x ^ dx) + (core ^ dc)
+            writes.append(move(hid_in.at[:, aligned(chunk, CHUNK)], out.at[:BLOCK, y * CHUNK : (y + 1) * CHUNK]))
+        writes.append(move(tenant, out.at[BLOCK:, :]))
+    for read in reads[1:]:
+        read.wait()
+
     def columns(main, tail, at):
         for t in range(2):
-            out[t] = up[t, :, main : main + CHUNK]
-            out[2, :, t * HEAD : (t + 1) * HEAD] = jnp.zeros((RANK, HEAD), BF16)
-            out[2, :, t * HEAD + at : t * HEAD + at + RANK] = up[t, :, tail : tail + RANK]
-
-    pl.when(lax.rem(place[0], 2) == 0)(lambda: columns(0, CHUNK, 0))
-    pl.when(lax.rem(place[0], 2) == 1)(lambda: columns(RANK, 0, RANK))
-    for t in range(2):
-        out[3 + t] = down[t]
-        out[5 + t] = out_up[t]
-
-
-def hidden_body(place, adapter, hid, own, to_core, to_x, to_cross, tenant, sems):
-    x, core = lax.rem(place[0] // 2, 2), lax.rem(place[0], 2)
-    tenant[...] = jnp.full((ROWS, 4 * CHUNK), adapter[0].astype(F32)).astype(BF16)
-    copies = []
-
-    def move(src, dst):
-        copies.append(pltpu.make_async_copy(src, dst, sems.at[len(copies)]))
-
-    for out, dx, dc in ((own, 0, 0), (to_core, 0, 1), (to_x, 1, 0), (to_cross, 1, 1)):
-        for y in range(4):
-            chunk = 4 * y + 2 * (x ^ dx) + (core ^ dc)
-            move(hid.at[:, aligned(chunk, CHUNK)], out.at[:BLOCK, y * CHUNK : (y + 1) * CHUNK])
-        move(tenant, out.at[BLOCK:, :])
-    for copy in copies:
-        copy.start()
-    for copy in copies:
-        copy.wait()
+            mixed[t] = up_in[t, :, main : main + CHUNK]
+            mixed[2, :, t * HEAD : (t + 1) * HEAD] = jnp.zeros((RANK, HEAD), BF16)
+            mixed[2, :, t * HEAD + at : t * HEAD + at + RANK] = up_in[t, :, tail : tail + RANK]
+
+    pl.when(core == 0)(lambda: columns(0, CHUNK, 0))
+    pl.when(core == 1)(lambda: columns(RANK, 0, RANK))
+    writes.append(move(mixed, weights))
+    for write in writes:
+        write.wait()
 
 
 CACHE_AT = (HEADS + 2) * HEAD
@@ -323,13 +331,13 @@
                 acc = acc + nn(weights, values[rows, :])
             ctx[:, aligned(j, HEAD)] = (acc[:, :HEAD] / acc[:, HEAD:]).astype(BF16)
 
-        def two_heads(i, carry):
-            scores = [head_scores(2 * i + e) for e in range(2)]
-            for e in range(2):
-                head_context(2 * i + e, scores[e])
+        def some_heads(i, carry):
+            scores = [head_scores(4 * i + e) for e in range(4)]
+            for e in range(4):
+                head_context(4 * i + e, scores[e])
             return carry
 
-        lax.fori_loop(0, HEADS // 2, two_heads, 0)
+        lax.fori_loop(0, HEADS // 4, some_heads, 0)
 
     for chips in range(2, CHIPS + 1, 2):
         pl.when(chip // 2 == chips // 2 - 1)(lambda chips=chips: branch(chips))
@@ -431,37 +439,33 @@
         return lax.ppermute(value, "blk", pairs)
 
     place = jnp.reshape(blk, (1,))
-    (weights,) = call(
+    hid, core_hid, x_hid, cross_hid, weights = call(
         pack_body,
-        [place],
-        [qkv_up, jnp.transpose(out_down, (0, 2, 1)), out_up],
-        [None] * 3,
-        [shape((7, RANK, CHUNK))],
-        limit=48,
+        [place, block_tenant],
+        [prompt_hidden, qkv_up, jnp.transpose(out_down, (0, 2, 1)), out_up],
+        [pl.BlockSpec(memory_space=pltpu.HBM)] * 4,
+        [shape((BLOCK + ROWS, 4 * CHUNK))] * 4 + [shape((7, RANK, CHUNK))],
+        [
+            pltpu.VMEM(prompt_hidden.shape, BF16),
+            pltpu.VMEM(qkv_up.shape, BF16),
+            pltpu.VMEM((7, RANK, CHUNK), BF16),
+            pltpu.VMEM((ROWS, 4 * CHUNK), BF16),
+            pltpu.SemaphoreType.DMA((25,)),
+        ],
+        63,
+        out_specs=[pl.BlockSpec(memory_space=pl.ANY)] * 5,
     )
     weights = lax.all_gather(weights, "blk")
-    arrived = from_row(down, 1)
-    downs = [down, arrived, from_row(down, 3), from_row(down, 2)]
-    hid, core_hid, x_hid, cross_hid = call(
-        hidden_body,
-        [place, block_tenant],
-        [prompt_hidden],
-        [pl.BlockSpec(memory_space=pl.ANY)],
-        [shape((BLOCK + ROWS, 4 * CHUNK))] * 4,
-        [pltpu.VMEM((ROWS, 4 * CHUNK), BF16), pltpu.SemaphoreType.DMA((20,))],
-        48,
-        out_specs=[pl.BlockSpec(memory_space=pl.ANY)] * 4,
-    )
     cross_hid = lax.ppermute(cross_hid, "blk", [(i, i ^ 3) for i in range(2 * CHIPS)])
     x_hid, core_hid = to_x(x_hid), to_core(core_hid)
+    downs = [down, from_row(down, 1), from_row(down, 3), from_row(down, 2)]
     base, base_send = call(
         base_body,
-        [lax.optimization_barrier((ids, arrived))[0]],
+        [lax.optimization_barrier((ids, x_hid))[0]],
         [prompt_qkv, row_cache],
-        [pl.BlockSpec(memory_space=pl.ANY)] * 2,
+        [pl.BlockSpec(memory_space=pltpu.HBM)] * 2,
         [shape((BLOCK, PACKED))] * 2,
         [pltpu.SemaphoreType.DMA((2 * (3 + 2 * (LIVE - 1)),))],
-        48,
         out_specs=[pl.BlockSpec(memory_space=pl.ANY)] * 2,
     )
     base_oth = to_core(base_send)

time: 104 us -> 98.5 us (0.947)
  the two profiles are of different devices: /device:TPU:248 before, /device:TPU:24 now
where the time goes in v4:
time: 98.5 us; the launch traced here: 98.2 us
  waiting for transfers between devices  33.7 us (34%)
  starting transfers between devices  24.8 us (25%)
  Pallas kernels  19.2 us (19%)
  between operations  14.9 us (15%)
  local copies, waits for them, and re-layouts  5.58 us (6%)
    pallas_call x7, Pallas kernels, call(): pl.pallas_call(body, grid_spec=pltpu.PrefetchScalarGridSpec(num_scalar_pr...  19.2 us
    ppermute x7, starting transfers between devices, get(): return lax.ppermute(value, 'blk', pairs)  10.7 us
    ppermute x3, waiting for transfers between devices, from_row(): return lax.ppermute(value, 'blk', pairs)  8.62 us
    ppermute x2, waiting for transfers between devices, to_role(): return lax.ppermute(value, 'role', [(0, 1), (1, 0)])  7.23 us
    ppermute x2, starting transfers between devices, to_role(): return lax.ppermute(value, 'role', [(0, 1), (1, 0)])  6.08 us
    ppermute x7, waiting for transfers between devices, get(): return lax.ppermute(value, 'blk', pairs)  5.82 us
    ppermute x2, waiting for transfers between devices, to_x(): return lax.ppermute(value, 'blk', [(i, i ^ 2) for i in range(2 * CHIPS)])  4.59 us
    unnamed x16, local copies, waits for them, and re-layouts  3.95 us
  transfers between devices with their start and end apart: 21, of which 14 were waited for; matrix products, arithmetic and copies ran while one was open for 2% of the time, Pallas kernels for 4%

profile of v4, /device:TPU:24, one launch (start us, length us, event | category | flops | bytes accessed | tf_op | source)
XLA Modules:
  0.0 98.2 jit_solution(1508820363322540125)
XLA Ops:
  7.2 0.0 all-gather.3.cloned.1.call-start
  7.9 2.5 %shard_map.131 = (bf16[144,1024]{1,0:T(8,128)(2,1)}, bf16[144,1024]{1,0:T(8,128)(2,1)}, bf16[144,1024]{1,0:T(8,128)(2,1)}, bf16[144,1024]{1,0:T(8,128)(2,1)}, bf16[7,64,256]{2,1,0:T(8,128)(2,1)}) custom-call(s32[1]{0:T(128)} %bitcast.5.place, s32[1]{0:T(128)S(6)} %copy.14.adapter, bf16[128,4096]{1,0:T(8,128)(2,1)} %hid.1, bf16[2,64,320]{2,1,0:T(8,128)(2,1)} %up.1, ...), custom_call_target="tpu_custom_call" | custom-call | tf_op jit(solution)/shard_map/pallas_call | solution.py:44
  10.5 0.0 copy-start.2
  10.5 0.0 all-gather.3.cloned.1.call-update
  10.5 0.8 collective-permute-start.4
  11.3 1.5 %collective-permute-start.2 = (bf16[144,1024]{1,0:T(8,128)(2,1)}, bf16[144,1024]{1,0:T(8,128)(2,1)S(1)}, u32[]{:S(2)}, u32[]{:S(2)}) collective-permute-start(bf16[144,1024]{1,0:T(8,128)(2,1)} %get-tuple-element.20), channel_id=1, source_target_pairs={{0,2},{1,3},{2,0},{3,1},{4,6},{5,7},{6,4},{7,5},{8,10},{9,11},{10,... | collective-permute-start | bytes 884744 | tf_op jit(solution)/shard_map/ppermute | solution.py:435
  12.8 0.6 collective-permute-start.3
  13.5 2.5 %collective-permute-start.5 = (bf16[2,192,256]{2,1,0:T(8,128)(2,1)}, bf16[2,192,256]{2,1,0:T(8,128)(2,1)}, u32[]{:S(2)}, u32[]{:S(2)}) collective-permute-start(bf16[2,192,256]{2,1,0:T(8,128)(2,1)} %bitcast.16), channel_id=1, source_target_pairs={{12,0},{13,1},{14,2},{15,3},{0,4},{1,5},{2,6},{3,7},{4,8},{5,9},{6... | collective-permute-start | bytes 589832 | tf_op jit(solution)/shard_map/ppermute | solution.py:439
  16.0 2.7 %collective-permute-done.4.w1 = bf16[2,192,256]{2,1,0:T(8,128)(2,1)S(1)} collective-permute-done((bf16[2,192,256]{2,1,0:T(8,128)(2,1)}, bf16[2,192,256]{2,1,0:T(8,128)(2,1)S(1)}, u32[]{:S(2)}, u32[]{:S(2)}) %collective-permute-start.4) | collective-permute-done | bytes 196640 | tf_op jit(solution)/shard_map/ppermute | solution.py:439
  18.6 0.0 collective-permute-start.6
  18.7 0.9 pad.8.row_hid
  19.5 0.8 concatenate.3.ids
  20.3 4.6 %collective-permute-done.5.w3 = bf16[2,192,256]{2,1,0:T(8,128)(2,1)} collective-permute-done((bf16[2,192,256]{2,1,0:T(8,128)(2,1)}, bf16[2,192,256]{2,1,0:T(8,128)(2,1)}, u32[]{:S(2)}, u32[]{:S(2)}) %collective-permute-start.5) | collective-permute-done | bytes 196640 | tf_op jit(solution)/shard_map/ppermute | solution.py:439
  24.9 1.4 %collective-permute-done.6.w2 = bf16[2,192,256]{2,1,0:T(8,128)(2,1)} collective-permute-done((bf16[2,192,256]{2,1,0:T(8,128)(2,1)}, bf16[2,192,256]{2,1,0:T(8,128)(2,1)}, u32[]{:S(2)}, u32[]{:S(2)}) %collective-permute-start.6) | collective-permute-done | bytes 196640 | tf_op jit(solution)/shard_map/ppermute | solution.py:439
  26.3 1.0 copy-done.4
  27.2 0.9 copy-done.6
  28.1 2.9 %shard_map.132 = (bf16[416,128]{1,0:T(8,128)(2,1)S(1)}, bf16[416,128]{1,0:T(8,128)(2,1)S(1)}) custom-call(s32[13]{0:T(128)S(1)} %concatenate.3.ids, bf16[144,1024]{1,0:T(8,128)(2,1)S(1)} %copy-done.4, bf16[144,1024]{1,0:T(8,128)(2,1)S(1)} %collective-permute-done.1.by_core, bf16[144,1024]{1,0:T(8,128)(2,1)S(1)} %collective-permute-done.2.by_x, ...), custom_call_target="tpu_custom_call" | custom-call | tf_op jit(solution)/shard_map/pallas_call | solution.py:44
  31.1 1.6 %collective-permute-start.7 = (bf16[416,128]{1,0:T(8,128)(2,1)S(1)}, bf16[416,128]{1,0:T(8,128)(2,1)S(1)}, u32[]{:S(2)}, u32[]{:S(2)}) collective-permute-start(bf16[416,128]{1,0:T(8,128)(2,1)S(1)} %get-tuple-element.23), channel_id=1, source_target_pairs={{0,2},{1,3},{2,0},{3,1},{4,6},{5,7},{6,4},{7,5},{8,10},{9,11},{10,... | collective-permute-start | bytes 319496 | tf_op jit(solution)/shard_map/ppermute | solution.py:435
  32.7 0.9 shard_map.133
  33.6 0.6 collective-permute-start.10
  34.2 4.6 %collective-permute-done.7 = bf16[416,128]{1,0:T(8,128)(2,1)S(1)} collective-permute-done((bf16[416,128]{1,0:T(8,128)(2,1)S(1)}, bf16[416,128]{1,0:T(8,128)(2,1)S(1)}, u32[]{:S(2)}, u32[]{:S(2)}) %collective-permute-start.7) | collective-permute-done | bytes 106528 | tf_op jit(solution)/shard_map/ppermute | solution.py:435
  38.8 0.3 collective-permute-start.8
  39.1 1.1 %collective-permute-done.8 = bf16[416,128]{1,0:T(8,128)(2,1)S(1)} collective-permute-done((bf16[416,128]{1,0:T(8,128)(2,1)S(1)}, bf16[416,128]{1,0:T(8,128)(2,1)S(1)}, u32[]{:S(2)}, u32[]{:S(2)}) %collective-permute-start.8) | collective-permute-done | bytes 106528 | tf_op jit(solution)/shard_map/ppermute | solution.py:428
  40.2 3.1 %collective-permute-start.9 = (bf16[416,128]{1,0:T(8,128)(2,1)S(1)}, bf16[416,128]{1,0:T(8,128)(2,1)S(1)}, u32[]{:S(2)}, u32[]{:S(2)}) collective-permute-start(bf16[416,128]{1,0:T(8,128)(2,1)S(1)} %add_convert_fusion.mine), channel_id=1, source_target_pairs={{0,128},{128,0},{1,129},{129,1},{2,130},{130,2},{3,131},{131,3},{4... | collective-permute-start | bytes 319496 | tf_op jit(solution)/shard_map/ppermute | solution.py:431
  43.3 1.2 %collective-permute-done.oth = s32[1]{0:T(128)} collective-permute-done((s32[1]{0:T(128)}, s32[1]{0:T(128)}, u32[]{:S(2)}, u32[]{:S(2)}) %collective-permute-start) | collective-permute-done | bytes 36 | tf_op jit(solution)/shard_map/ppermute | solution.py:428
  44.5 4.9 %collective-permute-done.9.theirs = bf16[416,128]{1,0:T(8,128)(2,1)S(1)} collective-permute-done((bf16[416,128]{1,0:T(8,128)(2,1)S(1)}, bf16[416,128]{1,0:T(8,128)(2,1)S(1)}, u32[]{:S(2)}, u32[]{:S(2)}) %collective-permute-start.9) | collective-permute-done | bytes 106528 | tf_op jit(solution)/shard_map/ppermute | solution.py:431
  49.4 3.9 %all-gather.3.cloned.1.call-done = bf16[112,64,256]{2,1,0:T(8,128)(2,1)} async-done(((bf16[7,64,256]{2,1,0:T(8,128)(2,1)}), bf16[112,64,256]{2,1,0:T(8,128)(2,1)}) %all-gather.3.cloned.1.call-update) | async-done | bytes 3670032 | tf_op jit(solution)/shard_map/all_gather | solution.py:458
  53.3 2.0 %copy-done = bf16[112,64,256]{2,1,0:T(8,128)(2,1)S(1)} copy-done((bf16[112,64,256]{2,1,0:T(8,128)(2,1)S(1)}, bf16[112,64,256]{2,1,0:T(8,128)(2,1)}, u32[]{:S(2)}) %copy-start) | copy-done | bytes 3670040
  55.4 2.8 %shard_map.134 = (bf16[256,1024]{1,0:T(8,128)(2,1)S(1)}, bf16[288,256]{1,0:T(8,128)(2,1)S(1)}) custom-call(s32[13]{0:T(128)S(1)} %concatenate.3.ids, s32[1]{0:T(128)} %collective-permute-done.oth, bf16[416,128]{1,0:T(8,128)(2,1)S(1)} %add_convert_fusion.mine, bf16[416,128]{1,0:T(8,128)(2,1)S(1)} %collective-permute-done.9.theirs, ...), custom_call_target="tpu_custom_call" | custom-call | tf_op jit(solution)/shard_map/pallas_call | solution.py:44
  58.2 1.2 %collective-permute-start.12 = (bf16[288,256]{1,0:T(8,128)(2,1)S(1)}, bf16[288,256]{1,0:T(8,128)(2,1)S(1)}, u32[]{:S(2)}, u32[]{:S(2)}) collective-permute-start(bf16[288,256]{1,0:T(8,128)(2,1)S(1)} %get-tuple-element.29.rest_0_), channel_id=1, source_target_pairs={{4,0},{5,1},{6,2},{7,3},{8,4},{9,5},{10,6},{11,7},{12,8},{13,9},{1... | collective-permute-start | bytes 442376 | tf_op jit(solution)/shard_map/ppermute | solution.py:80
  59.4 2.7 %collective-permute-start.15 = (bf16[288,256]{1,0:T(8,128)(2,1)S(1)}, bf16[288,256]{1,0:T(8,128)(2,1)S(1)}, u32[]{:S(2)}, u32[]{:S(2)}) collective-permute-start(bf16[288,256]{1,0:T(8,128)(2,1)S(1)} %get-tuple-element.29.rest_0_), channel_id=1, source_target_pairs={{14,0},{15,1},{12,2},{13,3},{2,4},{3,5},{0,6},{1,7},{6,8},{7,9},{4... | collective-permute-start | bytes 442376 | tf_op jit(solution)/shard_map/ppermute | solution.py:80
  62.0 0.8 collective-permute-start.11
  62.9 0.2 collective-permute-start.13
  63.1 2.4 %collective-permute-start.14 = (bf16[288,256]{1,0:T(8,128)(2,1)S(1)}, bf16[288,256]{1,0:T(8,128)(2,1)S(1)}, u32[]{:S(2)}, u32[]{:S(2)}) collective-permute-start(bf16[288,256]{1,0:T(8,128)(2,1)S(1)} %get-tuple-element.29.rest_0_), channel_id=1, source_target_pairs={{6,0},{7,1},{4,2},{5,3},{10,4},{11,5},{8,6},{9,7},{14,8},{15,9},{1... | collective-permute-start | bytes 442376 | tf_op jit(solution)/shard_map/ppermute | solution.py:80
  65.5 0.1 collective-permute-start.16
  65.6 1.4 %collective-permute-done.15.rest_5_ = bf16[288,256]{1,0:T(8,128)(2,1)S(1)} collective-permute-done((bf16[288,256]{1,0:T(8,128)(2,1)S(1)}, bf16[288,256]{1,0:T(8,128)(2,1)S(1)}, u32[]{:S(2)}, u32[]{:S(2)}) %collective-permute-start.15) | collective-permute-done | bytes 147488 | tf_op jit(solution)/shard_map/ppermute | solution.py:80
  67.0 3.3 %collective-permute-start.17 = (bf16[288,256]{1,0:T(8,128)(2,1)S(1)}, bf16[288,256]{1,0:T(8,128)(2,1)S(1)}, u32[]{:S(2)}, u32[]{:S(2)}) collective-permute-start(bf16[288,256]{1,0:T(8,128)(2,1)S(1)} %collective-permute-done.15.rest_5_), channel_id=1, source_target_pairs={{12,0},{13,1},{14,2},{15,3},{0,4},{1,5},{2,6},{3,7},{4,8},{5,9},{6... | collective-permute-start | bytes 442376 | tf_op jit(solution)/shard_map/ppermute | solution.py:80
  70.3 0.5 collective-permute-done.11.rest_1_
  70.8 1.8 %collective-permute-done.14.rest_4_ = bf16[288,256]{1,0:T(8,128)(2,1)S(1)} collective-permute-done((bf16[288,256]{1,0:T(8,128)(2,1)S(1)}, bf16[288,256]{1,0:T(8,128)(2,1)S(1)}, u32[]{:S(2)}, u32[]{:S(2)}) %collective-permute-start.14) | collective-permute-done | bytes 147488 | tf_op jit(solution)/shard_map/ppermute | solution.py:80
  72.6 2.1 %collective-permute-done.16.rest_6_ = bf16[288,256]{1,0:T(8,128)(2,1)S(1)} collective-permute-done((bf16[288,256]{1,0:T(8,128)(2,1)S(1)}, bf16[288,256]{1,0:T(8,128)(2,1)S(1)}, u32[]{:S(2)}, u32[]{:S(2)}) %collective-permute-start.16) | collective-permute-done | bytes 147488 | tf_op jit(solution)/shard_map/ppermute | solution.py:80
  74.7 6.4 %shard_map.135 = (bf16[256,1024]{1,0:T(8,128)(2,1)S(1)}, f32[16,1024]{1,0:T(8,128)S(1)}) custom-call(s32[13]{0:T(128)S(1)} %concatenate.3.ids, bf16[256,1024]{1,0:T(8,128)(2,1)S(1)} %get-tuple-element.28.q, bf16[288,256]{1,0:T(8,128)(2,1)S(1)} %get-tuple-element.29.rest_0_, bf16[288,256]{1,0:T(8,128)(2,1)S(1)} %collective-permute-done.11.rest_1_, ...), custom_call_target="tpu_custom_call" | custom-call | tf_op jit(solution)/shard_map/pallas_call | solution.py:44
  81.1 0.0 copy-start.5
  81.1 1.6 %shard_map.136 = (bf16[80,128]{1,0:T(8,128)(2,1)S(1)}, bf16[80,128]{1,0:T(8,128)(2,1)S(1)}) custom-call(s32[13]{0:T(128)S(1)} %concatenate.3.ids, s32[1]{0:T(128)} %collective-permute-done.oth, bf16[256,1024]{1,0:T(8,128)(2,1)S(1)} %get-tuple-element.30.ctx, f32[16,1024]{1,0:T(8,128)S(1)} %get-tuple-element.31.row_ctx, ...), custom_call_target="tpu_custom_call" | custom-call | tf_op jit(solution)/shard_map/pallas_call | solution.py:44
  82.7 0.1 collective-permute-start.18
  82.8 1.2 %collective-permute-done.18 = bf16[80,128]{1,0:T(8,128)(2,1)S(1)} collective-permute-done((bf16[80,128]{1,0:T(8,128)(2,1)S(1)}, bf16[80,128]{1,0:T(8,128)(2,1)S(1)}, u32[]{:S(2)}, u32[]{:S(2)}) %collective-permute-start.18) | collective-permute-done | bytes 20512 | tf_op jit(solution)/shard_map/ppermute | solution.py:428
  84.0 3.0 %collective-permute-start.19 = (bf16[80,128]{1,0:T(8,128)(2,1)S(1)}, bf16[80,128]{1,0:T(8,128)(2,1)S(1)}, u32[]{:S(2)}, u32[]{:S(2)}) collective-permute-start(bf16[80,128]{1,0:T(8,128)(2,1)S(1)} %add_convert_fusion.2.a), channel_id=1, source_target_pairs={{0,128},{128,0},{1,129},{129,1},{2,130},{130,2},{3,131},{131,3},{4... | collective-permute-start | bytes 61448 | tf_op jit(solution)/shard_map/ppermute | solution.py:431
  87.0 2.4 %collective-permute-done.19.b = bf16[80,128]{1,0:T(8,128)(2,1)S(1)} collective-permute-done((bf16[80,128]{1,0:T(8,128)(2,1)S(1)}, bf16[80,128]{1,0:T(8,128)(2,1)S(1)}, u32[]{:S(2)}, u32[]{:S(2)}) %collective-permute-start.19) | collective-permute-done | bytes 20512 | tf_op jit(solution)/shard_map/ppermute | solution.py:431
  89.4 2.0 %shard_map.137 = (bf16[128,4096]{1,0:T(8,128)(2,1)}, bf16[4,256]{1,0:T(4,128)(2,1)}) custom-call(s32[13]{0:T(128)S(1)} %concatenate.3.ids, bf16[80,128]{1,0:T(8,128)(2,1)S(1)} %add_convert_fusion.2.a, bf16[80,128]{1,0:T(8,128)(2,1)S(1)} %collective-permute-done.19.b, bf16[16,7,64,256]{3,2,1,0:T(8,128)(2,1)S(1)} %bitcast.14, bf16[2,64,256]{2,1,0:T(8,128)(2,1)S(1)} %copy-done.5), custom_call_target="tpu_custom_call" | custom-call | tf_op jit(solution)/shard_map/pallas_call | solution.py:44
  (24 shorter events, 0.1 us)
Async XLA Ops:
  7.2 25.5 %copy-start.3 = (bf16[3,128,1024]{2,1,0:T(8,128)(2,1)S(1)}, bf16[3,128,1024]{2,1,0:T(8,128)(2,1)}, u32[]{:S(2)}) copy-start(bf16[3,128,1024]{2,1,0:T(8,128)(2,1)} %cache.1) | copy-start | bytes 2359300
  7.2 36.1 %copy-start.7 = (bf16[4,5120]{1,0:T(4,128)(2,1)S(1)}, bf16[4,5120]{1,0:T(4,128)(2,1)}, u32[]{:S(2)}) copy-start(bf16[4,5120]{1,0:T(4,128)(2,1)} %param.16) | copy-start | bytes 122884
  7.2 46.1 %all-gather.3.cloned.1.call-start = ((), (), s32[]{:S(2)}) async-start(), calls=%async_computation | async-start | bytes 3899392 | tf_op jit(solution)/shard_map/all_gather | solution.py:458
  10.5 22.2 %copy-start.2 = (bf16[128,5120]{1,0:T(8,128)(2,1)S(1)}, bf16[128,5120]{1,0:T(8,128)(2,1)}, u32[]{:S(2)}) copy-start(bf16[128,5120]{1,0:T(8,128)(2,1)} %qkv.1) | copy-start | bytes 3932164
  10.5 8.1 %collective-permute-start.4 = (bf16[2,192,256]{2,1,0:T(8,128)(2,1)}, bf16[2,192,256]{2,1,0:T(8,128)(2,1)S(1)}, u32[]{:S(2)}, u32[]{:S(2)}) collective-permute-start(bf16[2,192,256]{2,1,0:T(8,128)(2,1)} %bitcast.15), channel_id=1, source_target_pairs={{4,0},{5,1},{6,2},{7,3},{8,4},{9,5},{10,6},{11,7},{12,8},{13,9},{1... | collective-permute-start | bytes 589832 | tf_op jit(solution)/shard_map/ppermute | solution.py:439
  11.3 14.9 %collective-permute-start.2 = (bf16[144,1024]{1,0:T(8,128)(2,1)}, bf16[144,1024]{1,0:T(8,128)(2,1)S(1)}, u32[]{:S(2)}, u32[]{:S(2)}) collective-permute-start(bf16[144,1024]{1,0:T(8,128)(2,1)} %get-tuple-element.20), channel_id=1, source_target_pairs={{0,2},{1,3},{2,0},{3,1},{4,6},{5,7},{6,4},{7,5},{8,10},{9,11},{10,... | collective-permute-start | bytes 884744 | tf_op jit(solution)/shard_map/ppermute | solution.py:435
  12.8 13.4 %collective-permute-start.1 = (bf16[144,1024]{1,0:T(8,128)(2,1)}, bf16[144,1024]{1,0:T(8,128)(2,1)S(1)}, u32[]{:S(2)}, u32[]{:S(2)}) collective-permute-start(bf16[144,1024]{1,0:T(8,128)(2,1)} %get-tuple-element.19), channel_id=1, source_target_pairs={{0,1},{1,0},{2,3},{3,2},{4,5},{5,4},{6,7},{7,6},{8,9},{9,8},{10,11... | collective-permute-start | bytes 884744 | tf_op jit(solution)/shard_map/ppermute | solution.py:428
  12.8 13.4 %collective-permute-start.3 = (bf16[144,1024]{1,0:T(8,128)(2,1)}, bf16[144,1024]{1,0:T(8,128)(2,1)S(1)}, u32[]{:S(2)}, u32[]{:S(2)}) collective-permute-start(bf16[144,1024]{1,0:T(8,128)(2,1)} %get-tuple-element.21), channel_id=1, source_target_pairs={{0,3},{1,2},{2,1},{3,0},{4,7},{5,6},{6,5},{7,4},{8,11},{9,10},{10,... | collective-permute-start | bytes 884744 | tf_op jit(solution)/shard_map/ppermute | solution.py:459
  13.5 11.4 %collective-permute-start.5 = (bf16[2,192,256]{2,1,0:T(8,128)(2,1)}, bf16[2,192,256]{2,1,0:T(8,128)(2,1)}, u32[]{:S(2)}, u32[]{:S(2)}) collective-permute-start(bf16[2,192,256]{2,1,0:T(8,128)(2,1)} %bitcast.16), channel_id=1, source_target_pairs={{12,0},{13,1},{14,2},{15,3},{0,4},{1,5},{2,6},{3,7},{4,8},{5,9},{6... | collective-permute-start | bytes 589832 | tf_op jit(solution)/shard_map/ppermute | solution.py:439
  18.6 7.6 %collective-permute-start.6 = (bf16[2,192,256]{2,1,0:T(8,128)(2,1)}, bf16[2,192,256]{2,1,0:T(8,128)(2,1)}, u32[]{:S(2)}, u32[]{:S(2)}) collective-permute-start(bf16[2,192,256]{2,1,0:T(8,128)(2,1)} %bitcast.17), channel_id=1, source_target_pairs={{8,0},{9,1},{10,2},{11,3},{12,4},{13,5},{14,6},{15,7},{0,8},{1,9},... | collective-permute-start | bytes 589832 | tf_op jit(solution)/shard_map/ppermute | solution.py:439
  26.2 1.0 copy-start.4
  27.2 0.9 copy-start.6
  31.1 7.7 %collective-permute-start.7 = (bf16[416,128]{1,0:T(8,128)(2,1)S(1)}, bf16[416,128]{1,0:T(8,128)(2,1)S(1)}, u32[]{:S(2)}, u32[]{:S(2)}) collective-permute-start(bf16[416,128]{1,0:T(8,128)(2,1)S(1)} %get-tuple-element.23), channel_id=1, source_target_pairs={{0,2},{1,3},{2,0},{3,1},{4,6},{5,7},{6,4},{7,5},{8,10},{9,11},{10,... | collective-permute-start | bytes 319496 | tf_op jit(solution)/shard_map/ppermute | solution.py:435
  33.6 15.8 %collective-permute-start.10 = (bf16[128,2048]{1,0:T(8,128)(2,1)S(1)}, bf16[128,2048]{1,0:T(8,128)(2,1)S(1)}, u32[]{:S(2)}, u32[]{:S(2)}) collective-permute-start(bf16[128,2048]{1,0:T(8,128)(2,1)S(1)} %get-tuple-element.26), channel_id=1, source_target_pairs={{0,1},{1,0},{2,3},{3,2},{4,5},{5,4},{6,7},{7,6},{8,9},{9,8},{10,11... | collective-permute-start | bytes 1572872 | tf_op jit(solution)/shard_map/ppermute | solution.py:428
  38.8 1.4 %collective-permute-start.8 = (bf16[416,128]{1,0:T(8,128)(2,1)S(1)}, bf16[416,128]{1,0:T(8,128)(2,1)S(1)}, u32[]{:S(2)}, u32[]{:S(2)}) collective-permute-start(bf16[416,128]{1,0:T(8,128)(2,1)S(1)} %add_convert_fusion.1), channel_id=1, source_target_pairs={{0,1},{1,0},{2,3},{3,2},{4,5},{5,4},{6,7},{7,6},{8,9},{9,8},{10,11... | collective-permute-start | bytes 319496 | tf_op jit(solution)/shard_map/ppermute | solution.py:428
  40.2 9.2 %collective-permute-start.9 = (bf16[416,128]{1,0:T(8,128)(2,1)S(1)}, bf16[416,128]{1,0:T(8,128)(2,1)S(1)}, u32[]{:S(2)}, u32[]{:S(2)}) collective-permute-start(bf16[416,128]{1,0:T(8,128)(2,1)S(1)} %add_convert_fusion.mine), channel_id=1, source_target_pairs={{0,128},{128,0},{1,129},{129,1},{2,130},{130,2},{3,131},{131,3},{4... | collective-permute-start | bytes 319496 | tf_op jit(solution)/shard_map/ppermute | solution.py:431
  43.3 1.2 %collective-permute-start = (s32[1]{0:T(128)}, s32[1]{0:T(128)}, u32[]{:S(2)}, u32[]{:S(2)}) collective-permute-start(s32[1]{0:T(128)} %param.14), channel_id=1, source_target_pairs={{0,1},{1,0},{2,3},{3,2},{4,5},{5,4},{6,7},{7,6},{8,9},{9,8},{10,11... | collective-permute-start | bytes 20 | tf_op jit(solution)/shard_map/ppermute | solution.py:428
  53.3 2.0 %copy-start = (bf16[112,64,256]{2,1,0:T(8,128)(2,1)S(1)}, bf16[112,64,256]{2,1,0:T(8,128)(2,1)}, u32[]{:S(2)}) copy-start(bf16[112,64,256]{2,1,0:T(8,128)(2,1)} %all-gather.3.cloned.1.call-done) | copy-start | bytes 11010052
  55.4 25.7 %copy-start.1 = (bf16[112,64,256]{2,1,0:T(8,128)(2,1)S(1)}, bf16[112,64,256]{2,1,0:T(8,128)(2,1)}, u32[]{:S(2)}) copy-start(bf16[112,64,256]{2,1,0:T(8,128)(2,1)} %all-gather.3.cloned.1.call-done) | copy-start | bytes 11010052
  58.2 7.4 %collective-permute-start.12 = (bf16[288,256]{1,0:T(8,128)(2,1)S(1)}, bf16[288,256]{1,0:T(8,128)(2,1)S(1)}, u32[]{:S(2)}, u32[]{:S(2)}) collective-permute-start(bf16[288,256]{1,0:T(8,128)(2,1)S(1)} %get-tuple-element.29.rest_0_), channel_id=1, source_target_pairs={{4,0},{5,1},{6,2},{7,3},{8,4},{9,5},{10,6},{11,7},{12,8},{13,9},{1... | collective-permute-start | bytes 442376 | tf_op jit(solution)/shard_map/ppermute | solution.py:80
  59.4 7.6 %collective-permute-start.15 = (bf16[288,256]{1,0:T(8,128)(2,1)S(1)}, bf16[288,256]{1,0:T(8,128)(2,1)S(1)}, u32[]{:S(2)}, u32[]{:S(2)}) collective-permute-start(bf16[288,256]{1,0:T(8,128)(2,1)S(1)} %get-tuple-element.29.rest_0_), channel_id=1, source_target_pairs={{14,0},{15,1},{12,2},{13,3},{2,4},{3,5},{0,6},{1,7},{6,8},{7,9},{4... | collective-permute-start | bytes 442376 | tf_op jit(solution)/shard_map/ppermute | solution.py:80
  62.0 8.7 %collective-permute-start.11 = (bf16[288,256]{1,0:T(8,128)(2,1)S(1)}, bf16[288,256]{1,0:T(8,128)(2,1)S(1)}, u32[]{:S(2)}, u32[]{:S(2)}) collective-permute-start(bf16[288,256]{1,0:T(8,128)(2,1)S(1)} %get-tuple-element.29.rest_0_), channel_id=1, source_target_pairs={{2,0},{3,1},{0,2},{1,3},{6,4},{7,5},{4,6},{5,7},{10,8},{11,9},{8,1... | collective-permute-start | bytes 442376 | tf_op jit(solution)/shard_map/ppermute | solution.py:80
  62.9 7.9 %collective-permute-start.13 = (bf16[288,256]{1,0:T(8,128)(2,1)S(1)}, bf16[288,256]{1,0:T(8,128)(2,1)S(1)}, u32[]{:S(2)}, u32[]{:S(2)}) collective-permute-start(bf16[288,256]{1,0:T(8,128)(2,1)S(1)} %get-tuple-element.29.rest_0_), channel_id=1, source_target_pairs={{12,0},{13,1},{14,2},{15,3},{0,4},{1,5},{2,6},{3,7},{4,8},{5,9},{6... | collective-permute-start | bytes 442376 | tf_op jit(solution)/shard_map/ppermute | solution.py:80
  63.1 9.5 %collective-permute-start.14 = (bf16[288,256]{1,0:T(8,128)(2,1)S(1)}, bf16[288,256]{1,0:T(8,128)(2,1)S(1)}, u32[]{:S(2)}, u32[]{:S(2)}) collective-permute-start(bf16[288,256]{1,0:T(8,128)(2,1)S(1)} %get-tuple-element.29.rest_0_), channel_id=1, source_target_pairs={{6,0},{7,1},{4,2},{5,3},{10,4},{11,5},{8,6},{9,7},{14,8},{15,9},{1... | collective-permute-start | bytes 442376 | tf_op jit(solution)/shard_map/ppermute | solution.py:80
  65.5 9.2 %collective-permute-start.16 = (bf16[288,256]{1,0:T(8,128)(2,1)S(1)}, bf16[288,256]{1,0:T(8,128)(2,1)S(1)}, u32[]{:S(2)}, u32[]{:S(2)}) collective-permute-start(bf16[288,256]{1,0:T(8,128)(2,1)S(1)} %collective-permute-done.12.rest_2_), channel_id=1, source_target_pairs={{4,0},{5,1},{6,2},{7,3},{8,4},{9,5},{10,6},{11,7},{12,8},{13,9},{1... | collective-permute-start | bytes 442376 | tf_op jit(solution)/shard_map/ppermute | solution.py:80
  67.0 7.7 %collective-permute-start.17 = (bf16[288,256]{1,0:T(8,128)(2,1)S(1)}, bf16[288,256]{1,0:T(8,128)(2,1)S(1)}, u32[]{:S(2)}, u32[]{:S(2)}) collective-permute-start(bf16[288,256]{1,0:T(8,128)(2,1)S(1)} %collective-permute-done.15.rest_5_), channel_id=1, source_target_pairs={{12,0},{13,1},{14,2},{15,3},{0,4},{1,5},{2,6},{3,7},{4,8},{5,9},{6... | collective-permute-start | bytes 442376 | tf_op jit(solution)/shard_map/ppermute | solution.py:80
  81.1 8.3 %copy-start.5 = (bf16[2,64,256]{2,1,0:T(8,128)(2,1)S(1)}, bf16[2,64,256]{2,1,0:T(8,128)(2,1)}, u32[]{:S(2)}) copy-start(bf16[2,64,256]{2,1,0:T(8,128)(2,1)} %own_up.1) | copy-start | bytes 196612
  82.7 1.3 %collective-permute-start.18 = (bf16[80,128]{1,0:T(8,128)(2,1)S(1)}, bf16[80,128]{1,0:T(8,128)(2,1)S(1)}, u32[]{:S(2)}, u32[]{:S(2)}) collective-permute-start(bf16[80,128]{1,0:T(8,128)(2,1)S(1)} %get-tuple-element.33), channel_id=1, source_target_pairs={{0,1},{1,0},{2,3},{3,2},{4,5},{5,4},{6,7},{7,6},{8,9},{9,8},{10,11... | collective-permute-start | bytes 61448 | tf_op jit(solution)/shard_map/ppermute | solution.py:428
  84.0 5.4 %collective-permute-start.19 = (bf16[80,128]{1,0:T(8,128)(2,1)S(1)}, bf16[80,128]{1,0:T(8,128)(2,1)S(1)}, u32[]{:S(2)}, u32[]{:S(2)}) collective-permute-start(bf16[80,128]{1,0:T(8,128)(2,1)S(1)} %add_convert_fusion.2.a), channel_id=1, source_target_pairs={{0,128},{128,0},{1,129},{129,1},{2,130},{130,2},{3,131},{131,3},{4... | collective-permute-start | bytes 61448 | tf_op jit(solution)/shard_map/ppermute | solution.py:431
Sparse Core Ops, SparseCore 0:
  10.6 42.6 all-gather.2

commit v5 on v4

--- a/solution.py
+++ b/solution.py
@@ -491,7 +491,7 @@
     q, kv = call(
         proj_body,
         [ids, oth],
-        [mine, theirs, base, base_oth] + [row_base] * 3 + [weights] * 3,
+        [mine, theirs, base, base_oth] + [row_base] * 3 + [weights[:, :3]] * 3,
         [None] * 4
         + row_columns
         + [spec((2 * CHIPS, 1, RANK, CHUNK), lambda s, i=i: (0, i, 0, 0)) for i in range(3)],

time: 98.5 us -> 100 us (1.015)
  starting transfers between devices: 24.8 us -> 26.7 us
  waiting for transfers between devices: 33.7 us -> 35.2 us
  local copies, waits for them, and re-layouts: 5.58 us -> 4.33 us
    ppermute x2, waiting for transfers between devices: 7.23 us -> 2.38 us  [to_role(): return lax.ppermute(value, 'role', [(0, 1), (1, 0)])]
    all_gather x1, waiting for transfers between devices: 3.9 us -> 7.04 us  [per_device(): weights = lax.all_gather(weights, 'blk')]
    ppermute x7, waiting for transfers between devices: 5.82 us -> 8.32 us  [get(): return lax.ppermute(value, 'blk', pairs)]
    ppermute x3, starting transfers between devices: 3.34 us -> 5.39 us  [from_row(): return lax.ppermute(value, 'blk', pairs)]
    ppermute x1, waiting for transfers between devices: 0.01 us -> 1.96 us  [per_device(): lax.ppermute(cross_hid, 'blk', [(i, i ^ 3) for i in range(2 * CHIPS)])]
    slice x0 -> x1, local copies, waits for them, and re-layouts: none -> 1.57 us  [per_device(): weights[:, :3]]
    unnamed x16 -> x24, local copies, waits for them, and re-layouts: 3.95 us -> 2.63 us
    ppermute x5, waiting for transfers between devices: 3.49 us -> 2.47 us  [to_core(): return lax.ppermute(value, 'blk', [(i, i ^ 1) for i in range(2 * CHIPS)])]
  transfers between devices with their start and end apart: 21 -> 21, of which waited for: 14 -> 11; matrix products, arithmetic and copies ran while one was open for 2% -> 2% of each run, Pallas kernels for 4% -> 4%
where the time goes in v5:
time: 100 us
  waiting for transfers between devices  35.2 us (35%)
  starting transfers between devices  26.7 us (27%)
  Pallas kernels  19 us (19%)
  between operations  14.9 us (15%)
  local copies, waits for them, and re-layouts  4.33 us (4%)
    pallas_call x7, Pallas kernels, call(): pl.pallas_call(body, grid_spec=pltpu.PrefetchScalarGridSpec(num_scalar_pr...  19 us
    ppermute x7, starting transfers between devices, get(): return lax.ppermute(value, 'blk', pairs)  11.1 us
    ppermute x3, waiting for transfers between devices, from_row(): return lax.ppermute(value, 'blk', pairs)  8.34 us
    ppermute x7, waiting for transfers between devices, get(): return lax.ppermute(value, 'blk', pairs)  8.32 us
    all_gather x1, waiting for transfers between devices, per_device(): weights = lax.all_gather(weights, 'blk')  7.04 us
    ppermute x2, starting transfers between devices, to_role(): return lax.ppermute(value, 'role', [(0, 1), (1, 0)])  5.51 us
    ppermute x3, starting transfers between devices, from_row(): return lax.ppermute(value, 'blk', pairs)  5.39 us
    ppermute x2, waiting for transfers between devices, to_x(): return lax.ppermute(value, 'blk', [(i, i ^ 2) for i in range(2 * CHIPS)])  4.63 us
  transfers between devices with their start and end apart: 21, of which 11 were waited for; matrix products, arithmetic and copies ran while one was open for 2% of the time, Pallas kernels for 4%

profile of v5, /device:TPU:24, one launch (start us, length us, event | category | flops | bytes accessed | tf_op | source)
XLA Modules:
  0.0 100.2 jit_solution(14021934207363884423)
XLA Ops:
  7.2 0.0 copy-start.5
  7.2 0.0 all-gather.3.cloned.1.call-start
  7.9 2.5 %shard_map.131 = (bf16[144,1024]{1,0:T(8,128)(2,1)}, bf16[144,1024]{1,0:T(8,128)(2,1)}, bf16[144,1024]{1,0:T(8,128)(2,1)}, bf16[144,1024]{1,0:T(8,128)(2,1)}, bf16[7,64,256]{2,1,0:T(8,128)(2,1)}) custom-call(s32[1]{0:T(128)} %bitcast.5.place, s32[1]{0:T(128)S(6)} %copy.14.adapter, bf16[128,4096]{1,0:T(8,128)(2,1)} %hid.1, bf16[2,64,320]{2,1,0:T(8,128)(2,1)} %up.1, ...), custom_call_target="tpu_custom_call" | custom-call | tf_op jit(solution)/shard_map/pallas_call | solution.py:44
  10.5 0.0 copy-start.1
  10.5 0.0 copy-start.2
  10.5 0.0 all-gather.3.cloned.1.call-update
  10.5 1.3 %collective-permute-start.6 = (bf16[2,192,256]{2,1,0:T(8,128)(2,1)}, bf16[2,192,256]{2,1,0:T(8,128)(2,1)S(1)}, u32[]{:S(2)}, u32[]{:S(2)}) collective-permute-start(bf16[2,192,256]{2,1,0:T(8,128)(2,1)} %bitcast.13), channel_id=1, source_target_pairs={{8,0},{9,1},{10,2},{11,3},{12,4},{13,5},{14,6},{15,7},{0,8},{1,9},... | collective-permute-start | bytes 589832 | tf_op jit(solution)/shard_map/ppermute | solution.py:439
  11.8 0.0 collective-permute-start.1
  11.8 1.5 %collective-permute-start.2 = (bf16[144,1024]{1,0:T(8,128)(2,1)}, bf16[144,1024]{1,0:T(8,128)(2,1)S(1)}, u32[]{:S(2)}, u32[]{:S(2)}) collective-permute-start(bf16[144,1024]{1,0:T(8,128)(2,1)} %get-tuple-element.20), channel_id=1, source_target_pairs={{0,2},{1,3},{2,0},{3,1},{4,6},{5,7},{6,4},{7,5},{8,10},{9,11},{10,... | collective-permute-start | bytes 884744 | tf_op jit(solution)/shard_map/ppermute | solution.py:435
  13.3 0.4 collective-permute-start.3
  13.7 2.2 %collective-permute-start.5 = (bf16[2,192,256]{2,1,0:T(8,128)(2,1)}, bf16[2,192,256]{2,1,0:T(8,128)(2,1)}, u32[]{:S(2)}, u32[]{:S(2)}) collective-permute-start(bf16[2,192,256]{2,1,0:T(8,128)(2,1)} %bitcast.14), channel_id=1, source_target_pairs={{12,0},{13,1},{14,2},{15,3},{0,4},{1,5},{2,6},{3,7},{4,8},{5,9},{6... | collective-permute-start | bytes 589832 | tf_op jit(solution)/shard_map/ppermute | solution.py:439
  15.9 3.1 %collective-permute-done.6.w2 = bf16[2,192,256]{2,1,0:T(8,128)(2,1)S(1)} collective-permute-done((bf16[2,192,256]{2,1,0:T(8,128)(2,1)}, bf16[2,192,256]{2,1,0:T(8,128)(2,1)S(1)}, u32[]{:S(2)}, u32[]{:S(2)}) %collective-permute-start.6) | collective-permute-done | bytes 196640 | tf_op jit(solution)/shard_map/ppermute | solution.py:439
  19.0 0.7 copy-done.6
  19.6 1.9 %collective-permute-start.4 = (bf16[2,192,256]{2,1,0:T(8,128)(2,1)}, bf16[2,192,256]{2,1,0:T(8,128)(2,1)}, u32[]{:S(2)}, u32[]{:S(2)}) collective-permute-start(bf16[2,192,256]{2,1,0:T(8,128)(2,1)} %bitcast.15), channel_id=1, source_target_pairs={{4,0},{5,1},{6,2},{7,3},{8,4},{9,5},{10,6},{11,7},{12,8},{13,9},{1... | collective-permute-start | bytes 589832 | tf_op jit(solution)/shard_map/ppermute | solution.py:439
  21.6 0.1 concatenate.3.ids
  21.7 0.0 collective-permute-done.5.w3
  21.7 5.3 %collective-permute-done.4.w1 = bf16[2,192,256]{2,1,0:T(8,128)(2,1)} collective-permute-done((bf16[2,192,256]{2,1,0:T(8,128)(2,1)}, bf16[2,192,256]{2,1,0:T(8,128)(2,1)}, u32[]{:S(2)}, u32[]{:S(2)}) %collective-permute-start.4) | collective-permute-done | bytes 196640 | tf_op jit(solution)/shard_map/ppermute | solution.py:439
  27.0 2.0 %collective-permute-done.3.by_cross = bf16[144,1024]{1,0:T(8,128)(2,1)S(1)} collective-permute-done((bf16[144,1024]{1,0:T(8,128)(2,1)}, bf16[144,1024]{1,0:T(8,128)(2,1)S(1)}, u32[]{:S(2)}, u32[]{:S(2)}) %collective-permute-start.3) | collective-permute-done | bytes 294944 | tf_op jit(solution)/shard_map/ppermute | solution.py:459
  28.9 1.0 copy-done.3
  29.9 0.9 copy-done.7
  30.8 3.0 %shard_map.132 = (bf16[416,128]{1,0:T(8,128)(2,1)S(1)}, bf16[416,128]{1,0:T(8,128)(2,1)S(1)}) custom-call(s32[13]{0:T(128)S(1)} %concatenate.3.ids, bf16[144,1024]{1,0:T(8,128)(2,1)S(1)} %copy-done.3, bf16[144,1024]{1,0:T(8,128)(2,1)S(1)} %collective-permute-done.1.by_core, bf16[144,1024]{1,0:T(8,128)(2,1)S(1)} %collective-permute-done.2.by_x, ...), custom_call_target="tpu_custom_call" | custom-call | tf_op jit(solution)/shard_map/pallas_call | solution.py:44
  33.8 0.0 copy-start.9
  33.8 1.3 %collective-permute-start.7 = (bf16[416,128]{1,0:T(8,128)(2,1)S(1)}, bf16[416,128]{1,0:T(8,128)(2,1)S(1)}, u32[]{:S(2)}, u32[]{:S(2)}) collective-permute-start(bf16[416,128]{1,0:T(8,128)(2,1)S(1)} %get-tuple-element.23), channel_id=1, source_target_pairs={{0,2},{1,3},{2,0},{3,1},{4,6},{5,7},{6,4},{7,5},{8,10},{9,11},{10,... | collective-permute-start | bytes 319496 | tf_op jit(solution)/shard_map/ppermute | solution.py:435
  35.1 0.9 shard_map.133
  36.0 1.3 %collective-permute-start.10 = (bf16[128,2048]{1,0:T(8,128)(2,1)S(1)}, bf16[128,2048]{1,0:T(8,128)(2,1)S(1)}, u32[]{:S(2)}, u32[]{:S(2)}) collective-permute-start(bf16[128,2048]{1,0:T(8,128)(2,1)S(1)} %get-tuple-element.26), channel_id=1, source_target_pairs={{0,1},{1,0},{2,3},{3,2},{4,5},{5,4},{6,7},{7,6},{8,9},{9,8},{10,11... | collective-permute-start | bytes 1572872 | tf_op jit(solution)/shard_map/ppermute | solution.py:428
  37.3 4.6 %collective-permute-done.7 = bf16[416,128]{1,0:T(8,128)(2,1)S(1)} collective-permute-done((bf16[416,128]{1,0:T(8,128)(2,1)S(1)}, bf16[416,128]{1,0:T(8,128)(2,1)S(1)}, u32[]{:S(2)}, u32[]{:S(2)}) %collective-permute-start.7) | collective-permute-done | bytes 106528 | tf_op jit(solution)/shard_map/ppermute | solution.py:435
  41.9 0.1 collective-permute-start.8
  42.0 1.3 %collective-permute-done.8 = bf16[416,128]{1,0:T(8,128)(2,1)S(1)} collective-permute-done((bf16[416,128]{1,0:T(8,128)(2,1)S(1)}, bf16[416,128]{1,0:T(8,128)(2,1)S(1)}, u32[]{:S(2)}, u32[]{:S(2)}) %collective-permute-start.8) | collective-permute-done | bytes 106528 | tf_op jit(solution)/shard_map/ppermute | solution.py:428
  43.4 2.5 %collective-permute-start.9 = (bf16[416,128]{1,0:T(8,128)(2,1)S(1)}, bf16[416,128]{1,0:T(8,128)(2,1)S(1)}, u32[]{:S(2)}, u32[]{:S(2)}) collective-permute-start(bf16[416,128]{1,0:T(8,128)(2,1)S(1)} %add_convert_fusion.mine), channel_id=1, source_target_pairs={{0,128},{128,0},{1,129},{129,1},{2,130},{130,2},{3,131},{131,3},{4... | collective-permute-start | bytes 319496 | tf_op jit(solution)/shard_map/ppermute | solution.py:431
  45.9 7.0 %all-gather.3.cloned.1.call-done = bf16[112,64,256]{2,1,0:T(8,128)(2,1)} async-done(((bf16[7,64,256]{2,1,0:T(8,128)(2,1)}), bf16[112,64,256]{2,1,0:T(8,128)(2,1)}) %all-gather.3.cloned.1.call-update) | async-done | bytes 3670032 | tf_op jit(solution)/shard_map/all_gather | solution.py:458
  52.9 1.6 %slice.4.up0.up1.tail = bf16[16,3,64,256]{3,2,1,0:T(8,128)(2,1)S(1)} slice(bf16[16,7,64,256]{3,2,1,0:T(8,128)(2,1)} %bitcast.9), slice={[0:16], [0:3], [0:64], [0:256]} | slice | bytes 3145728 | tf_op jit(solution)/shard_map/slice | solution.py:494
  54.6 2.7 %shard_map.134 = (bf16[256,1024]{1,0:T(8,128)(2,1)S(1)}, bf16[288,256]{1,0:T(8,128)(2,1)S(1)}) custom-call(s32[13]{0:T(128)S(1)} %concatenate.3.ids, s32[1]{0:T(128)} %collective-permute-done.oth, bf16[416,128]{1,0:T(8,128)(2,1)S(1)} %add_convert_fusion.mine, bf16[416,128]{1,0:T(8,128)(2,1)S(1)} %collective-permute-done.9.theirs, ...), custom_call_target="tpu_custom_call" | custom-call | tf_op jit(solution)/shard_map/pallas_call | solution.py:44
  57.3 3.0 %collective-permute-start.15 = (bf16[288,256]{1,0:T(8,128)(2,1)S(1)}, bf16[288,256]{1,0:T(8,128)(2,1)S(1)}, u32[]{:S(2)}, u32[]{:S(2)}) collective-permute-start(bf16[288,256]{1,0:T(8,128)(2,1)S(1)} %get-tuple-element.29.rest_0_), channel_id=1, source_target_pairs={{14,0},{15,1},{12,2},{13,3},{2,4},{3,5},{0,6},{1,7},{6,8},{7,9},{4... | collective-permute-start | bytes 442376 | tf_op jit(solution)/shard_map/ppermute | solution.py:80
  60.4 1.3 %collective-permute-start.14 = (bf16[288,256]{1,0:T(8,128)(2,1)S(1)}, bf16[288,256]{1,0:T(8,128)(2,1)S(1)}, u32[]{:S(2)}, u32[]{:S(2)}) collective-permute-start(bf16[288,256]{1,0:T(8,128)(2,1)S(1)} %get-tuple-element.29.rest_0_), channel_id=1, source_target_pairs={{6,0},{7,1},{4,2},{5,3},{10,4},{11,5},{8,6},{9,7},{14,8},{15,9},{1... | collective-permute-start | bytes 442376 | tf_op jit(solution)/shard_map/ppermute | solution.py:80
  61.6 2.2 %collective-permute-start.13 = (bf16[288,256]{1,0:T(8,128)(2,1)S(1)}, bf16[288,256]{1,0:T(8,128)(2,1)S(1)}, u32[]{:S(2)}, u32[]{:S(2)}) collective-permute-start(bf16[288,256]{1,0:T(8,128)(2,1)S(1)} %get-tuple-element.29.rest_0_), channel_id=1, source_target_pairs={{12,0},{13,1},{14,2},{15,3},{0,4},{1,5},{2,6},{3,7},{4,8},{5,9},{6... | collective-permute-start | bytes 442376 | tf_op jit(solution)/shard_map/ppermute | solution.py:80
  63.8 1.3 %collective-permute-start.11 = (bf16[288,256]{1,0:T(8,128)(2,1)S(1)}, bf16[288,256]{1,0:T(8,128)(2,1)S(1)}, u32[]{:S(2)}, u32[]{:S(2)}) collective-permute-start(bf16[288,256]{1,0:T(8,128)(2,1)S(1)} %get-tuple-element.29.rest_0_), channel_id=1, source_target_pairs={{2,0},{3,1},{0,2},{1,3},{6,4},{7,5},{4,6},{5,7},{10,8},{11,9},{8,1... | collective-permute-start | bytes 442376 | tf_op jit(solution)/shard_map/ppermute | solution.py:80
  65.1 3.4 %collective-permute-start.17 = (bf16[288,256]{1,0:T(8,128)(2,1)S(1)}, bf16[288,256]{1,0:T(8,128)(2,1)S(1)}, u32[]{:S(2)}, u32[]{:S(2)}) collective-permute-start(bf16[288,256]{1,0:T(8,128)(2,1)S(1)} %collective-permute-done.15.rest_5_), channel_id=1, source_target_pairs={{12,0},{13,1},{14,2},{15,3},{0,4},{1,5},{2,6},{3,7},{4,8},{5,9},{6... | collective-permute-start | bytes 442376 | tf_op jit(solution)/shard_map/ppermute | solution.py:80
  68.4 2.0 %collective-permute-done.12.rest_2_ = bf16[288,256]{1,0:T(8,128)(2,1)S(1)} collective-permute-done((bf16[288,256]{1,0:T(8,128)(2,1)S(1)}, bf16[288,256]{1,0:T(8,128)(2,1)S(1)}, u32[]{:S(2)}, u32[]{:S(2)}) %collective-permute-start.12) | collective-permute-done | bytes 147488 | tf_op jit(solution)/shard_map/ppermute | solution.py:80
  70.4 1.0 collective-permute-done.11.rest_1_
  71.4 5.4 %collective-permute-done.16.rest_6_ = bf16[288,256]{1,0:T(8,128)(2,1)S(1)} collective-permute-done((bf16[288,256]{1,0:T(8,128)(2,1)S(1)}, bf16[288,256]{1,0:T(8,128)(2,1)S(1)}, u32[]{:S(2)}, u32[]{:S(2)}) %collective-permute-start.16) | collective-permute-done | bytes 147488 | tf_op jit(solution)/shard_map/ppermute | solution.py:80
  76.7 6.3 %shard_map.135 = (bf16[256,1024]{1,0:T(8,128)(2,1)S(1)}, f32[16,1024]{1,0:T(8,128)S(1)}) custom-call(s32[13]{0:T(128)S(1)} %concatenate.3.ids, bf16[256,1024]{1,0:T(8,128)(2,1)S(1)} %get-tuple-element.28.q, bf16[288,256]{1,0:T(8,128)(2,1)S(1)} %get-tuple-element.29.rest_0_, bf16[288,256]{1,0:T(8,128)(2,1)S(1)} %collective-permute-done.11.rest_1_, ...), custom_call_target="tpu_custom_call" | custom-call | tf_op jit(solution)/shard_map/pallas_call | solution.py:44
  83.1 0.0 copy-start.4
  83.1 1.6 %shard_map.136 = (bf16[80,128]{1,0:T(8,128)(2,1)S(1)}, bf16[80,128]{1,0:T(8,128)(2,1)S(1)}) custom-call(s32[13]{0:T(128)S(1)} %concatenate.3.ids, s32[1]{0:T(128)} %collective-permute-done.oth, bf16[256,1024]{1,0:T(8,128)(2,1)S(1)} %get-tuple-element.30.ctx, f32[16,1024]{1,0:T(8,128)S(1)} %get-tuple-element.31.row_ctx, ...), custom_call_target="tpu_custom_call" | custom-call | tf_op jit(solution)/shard_map/pallas_call | solution.py:44
  84.7 0.1 collective-permute-start.18
  84.8 1.2 %collective-permute-done.18 = bf16[80,128]{1,0:T(8,128)(2,1)S(1)} collective-permute-done((bf16[80,128]{1,0:T(8,128)(2,1)S(1)}, bf16[80,128]{1,0:T(8,128)(2,1)S(1)}, u32[]{:S(2)}, u32[]{:S(2)}) %collective-permute-start.18) | collective-permute-done | bytes 20512 | tf_op jit(solution)/shard_map/ppermute | solution.py:428
  86.0 3.0 %collective-permute-start.19 = (bf16[80,128]{1,0:T(8,128)(2,1)S(1)}, bf16[80,128]{1,0:T(8,128)(2,1)S(1)}, u32[]{:S(2)}, u32[]{:S(2)}) collective-permute-start(bf16[80,128]{1,0:T(8,128)(2,1)S(1)} %add_convert_fusion.2.a), channel_id=1, source_target_pairs={{0,128},{128,0},{1,129},{129,1},{2,130},{130,2},{3,131},{131,3},{4... | collective-permute-start | bytes 61448 | tf_op jit(solution)/shard_map/ppermute | solution.py:431
  89.0 2.4 %collective-permute-done.19.b = bf16[80,128]{1,0:T(8,128)(2,1)S(1)} collective-permute-done((bf16[80,128]{1,0:T(8,128)(2,1)S(1)}, bf16[80,128]{1,0:T(8,128)(2,1)S(1)}, u32[]{:S(2)}, u32[]{:S(2)}) %collective-permute-start.19) | collective-permute-done | bytes 20512 | tf_op jit(solution)/shard_map/ppermute | solution.py:431
  91.3 2.0 %shard_map.137 = (bf16[128,4096]{1,0:T(8,128)(2,1)}, bf16[4,256]{1,0:T(4,128)(2,1)}) custom-call(s32[13]{0:T(128)S(1)} %concatenate.3.ids, bf16[80,128]{1,0:T(8,128)(2,1)S(1)} %add_convert_fusion.2.a, bf16[80,128]{1,0:T(8,128)(2,1)S(1)} %collective-permute-done.19.b, bf16[16,7,64,256]{3,2,1,0:T(8,128)(2,1)S(1)} %bitcast.12, bf16[2,64,256]{2,1,0:T(8,128)(2,1)S(1)} %copy-done.4), custom_call_target="tpu_custom_call" | custom-call | tf_op jit(solution)/shard_map/pallas_call | solution.py:44
  (33 shorter events, 0.2 us)
Async XLA Ops:
  7.2 21.7 %copy-start.5 = (bf16[2,256,192]{1,2,0:T(8,128)(2,1)S(1)}, bf16[2,256,192]{1,2,0:T(8,128)(2,1)}, u32[]{:S(2)}) copy-start(bf16[2,256,192]{1,2,0:T(8,128)(2,1)} %param.20) | copy-start | bytes 589828
  7.2 14.4 %copy-start.8 = (bf16[4,8192]{1,0:T(4,128)(2,1)S(1)}, bf16[4,8192]{1,0:T(4,128)(2,1)}, u32[]{:S(2)}) copy-start(bf16[4,8192]{1,0:T(4,128)(2,1)} %param.15) | copy-start | bytes 196612
  7.2 14.4 %copy-start.11 = (s32[3]{0:T(128)S(1)}, s32[3]{0:T(128)}, u32[]{:S(2)}) copy-start(s32[3]{0:T(128)} %param.19) | copy-start | bytes 40
  7.2 14.4 %copy-start.10 = (s32[4]{0:T(128)S(1)}, s32[4]{0:T(128)}, u32[]{:S(2)}) copy-start(s32[4]{0:T(128)} %param.17) | copy-start | bytes 52
  7.2 45.7 %all-gather.3.cloned.1.call-start = ((), (), s32[]{:S(2)}) async-start(), calls=%async_computation | async-start | bytes 3899392 | tf_op jit(solution)/shard_map/all_gather | solution.py:458
  10.5 24.6 %copy-start.1 = (bf16[128,5120]{1,0:T(8,128)(2,1)S(1)}, bf16[128,5120]{1,0:T(8,128)(2,1)}, u32[]{:S(2)}) copy-start(bf16[128,5120]{1,0:T(8,128)(2,1)} %qkv.1) | copy-start | bytes 3932164
  10.5 24.6 %copy-start.2 = (bf16[3,128,1024]{2,1,0:T(8,128)(2,1)S(1)}, bf16[3,128,1024]{2,1,0:T(8,128)(2,1)}, u32[]{:S(2)}) copy-start(bf16[3,128,1024]{2,1,0:T(8,128)(2,1)} %cache.1) | copy-start | bytes 2359300
  10.5 8.4 %collective-permute-start.6 = (bf16[2,192,256]{2,1,0:T(8,128)(2,1)}, bf16[2,192,256]{2,1,0:T(8,128)(2,1)S(1)}, u32[]{:S(2)}, u32[]{:S(2)}) collective-permute-start(bf16[2,192,256]{2,1,0:T(8,128)(2,1)} %bitcast.13), channel_id=1, source_target_pairs={{8,0},{9,1},{10,2},{11,3},{12,4},{13,5},{14,6},{15,7},{0,8},{1,9},... | collective-permute-start | bytes 589832 | tf_op jit(solution)/shard_map/ppermute | solution.py:439
  11.8 15.1 %collective-permute-start.1 = (bf16[144,1024]{1,0:T(8,128)(2,1)}, bf16[144,1024]{1,0:T(8,128)(2,1)S(1)}, u32[]{:S(2)}, u32[]{:S(2)}) collective-permute-start(bf16[144,1024]{1,0:T(8,128)(2,1)} %get-tuple-element.19), channel_id=1, source_target_pairs={{0,1},{1,0},{2,3},{3,2},{4,5},{5,4},{6,7},{7,6},{8,9},{9,8},{10,11... | collective-permute-start | bytes 884744 | tf_op jit(solution)/shard_map/ppermute | solution.py:428
  11.8 15.1 %collective-permute-start.2 = (bf16[144,1024]{1,0:T(8,128)(2,1)}, bf16[144,1024]{1,0:T(8,128)(2,1)S(1)}, u32[]{:S(2)}, u32[]{:S(2)}) collective-permute-start(bf16[144,1024]{1,0:T(8,128)(2,1)} %get-tuple-element.20), channel_id=1, source_target_pairs={{0,2},{1,3},{2,0},{3,1},{4,6},{5,7},{6,4},{7,5},{8,10},{9,11},{10,... | collective-permute-start | bytes 884744 | tf_op jit(solution)/shard_map/ppermute | solution.py:435
  13.3 15.6 %collective-permute-start.3 = (bf16[144,1024]{1,0:T(8,128)(2,1)}, bf16[144,1024]{1,0:T(8,128)(2,1)S(1)}, u32[]{:S(2)}, u32[]{:S(2)}) collective-permute-start(bf16[144,1024]{1,0:T(8,128)(2,1)} %get-tuple-element.21), channel_id=1, source_target_pairs={{0,3},{1,2},{2,1},{3,0},{4,7},{5,6},{6,5},{7,4},{8,11},{9,10},{10,... | collective-permute-start | bytes 884744 | tf_op jit(solution)/shard_map/ppermute | solution.py:459
  13.7 8.0 %collective-permute-start.5 = (bf16[2,192,256]{2,1,0:T(8,128)(2,1)}, bf16[2,192,256]{2,1,0:T(8,128)(2,1)}, u32[]{:S(2)}, u32[]{:S(2)}) collective-permute-start(bf16[2,192,256]{2,1,0:T(8,128)(2,1)} %bitcast.14), channel_id=1, source_target_pairs={{12,0},{13,1},{14,2},{15,3},{0,4},{1,5},{2,6},{3,7},{4,8},{5,9},{6... | collective-permute-start | bytes 589832 | tf_op jit(solution)/shard_map/ppermute | solution.py:439
  19.0 0.7 copy-start.6
  19.6 7.3 %collective-permute-start.4 = (bf16[2,192,256]{2,1,0:T(8,128)(2,1)}, bf16[2,192,256]{2,1,0:T(8,128)(2,1)}, u32[]{:S(2)}, u32[]{:S(2)}) collective-permute-start(bf16[2,192,256]{2,1,0:T(8,128)(2,1)} %bitcast.15), channel_id=1, source_target_pairs={{4,0},{5,1},{6,2},{7,3},{8,4},{9,5},{10,6},{11,7},{12,8},{13,9},{1... | collective-permute-start | bytes 589832 | tf_op jit(solution)/shard_map/ppermute | solution.py:439
  28.9 1.0 copy-start.3
  29.9 0.9 copy-start.7
  33.8 12.1 %copy-start.9 = (bf16[4,5120]{1,0:T(4,128)(2,1)S(1)}, bf16[4,5120]{1,0:T(4,128)(2,1)}, u32[]{:S(2)}) copy-start(bf16[4,5120]{1,0:T(4,128)(2,1)} %param.16) | copy-start | bytes 122884
  33.8 8.1 %collective-permute-start.7 = (bf16[416,128]{1,0:T(8,128)(2,1)S(1)}, bf16[416,128]{1,0:T(8,128)(2,1)S(1)}, u32[]{:S(2)}, u32[]{:S(2)}) collective-permute-start(bf16[416,128]{1,0:T(8,128)(2,1)S(1)} %get-tuple-element.23), channel_id=1, source_target_pairs={{0,2},{1,3},{2,0},{3,1},{4,6},{5,7},{6,4},{7,5},{8,10},{9,11},{10,... | collective-permute-start | bytes 319496 | tf_op jit(solution)/shard_map/ppermute | solution.py:435
  36.0 18.5 %collective-permute-start.10 = (bf16[128,2048]{1,0:T(8,128)(2,1)S(1)}, bf16[128,2048]{1,0:T(8,128)(2,1)S(1)}, u32[]{:S(2)}, u32[]{:S(2)}) collective-permute-start(bf16[128,2048]{1,0:T(8,128)(2,1)S(1)} %get-tuple-element.26), channel_id=1, source_target_pairs={{0,1},{1,0},{2,3},{3,2},{4,5},{5,4},{6,7},{7,6},{8,9},{9,8},{10,11... | collective-permute-start | bytes 1572872 | tf_op jit(solution)/shard_map/ppermute | solution.py:428
  41.9 1.4 %collective-permute-start.8 = (bf16[416,128]{1,0:T(8,128)(2,1)S(1)}, bf16[416,128]{1,0:T(8,128)(2,1)S(1)}, u32[]{:S(2)}, u32[]{:S(2)}) collective-permute-start(bf16[416,128]{1,0:T(8,128)(2,1)S(1)} %add_convert_fusion.1), channel_id=1, source_target_pairs={{0,1},{1,0},{2,3},{3,2},{4,5},{5,4},{6,7},{7,6},{8,9},{9,8},{10,11... | collective-permute-start | bytes 319496 | tf_op jit(solution)/shard_map/ppermute | solution.py:428
  43.4 11.2 %collective-permute-start.9 = (bf16[416,128]{1,0:T(8,128)(2,1)S(1)}, bf16[416,128]{1,0:T(8,128)(2,1)S(1)}, u32[]{:S(2)}, u32[]{:S(2)}) collective-permute-start(bf16[416,128]{1,0:T(8,128)(2,1)S(1)} %add_convert_fusion.mine), channel_id=1, source_target_pairs={{0,128},{128,0},{1,129},{129,1},{2,130},{130,2},{3,131},{131,3},{4... | collective-permute-start | bytes 319496 | tf_op jit(solution)/shard_map/ppermute | solution.py:431
  45.9 8.7 %collective-permute-start = (s32[1]{0:T(128)}, s32[1]{0:T(128)}, u32[]{:S(2)}, u32[]{:S(2)}) collective-permute-start(s32[1]{0:T(128)} %param.14), channel_id=1, source_target_pairs={{0,1},{1,0},{2,3},{3,2},{4,5},{5,4},{6,7},{7,6},{8,9},{9,8},{10,11... | collective-permute-start | bytes 20 | tf_op jit(solution)/shard_map/ppermute | solution.py:428
  54.6 28.5 %copy-start = (bf16[112,64,256]{2,1,0:T(8,128)(2,1)S(1)}, bf16[112,64,256]{2,1,0:T(8,128)(2,1)}, u32[]{:S(2)}) copy-start(bf16[112,64,256]{2,1,0:T(8,128)(2,1)} %all-gather.3.cloned.1.call-done) | copy-start | bytes 11010052
  57.3 7.8 %collective-permute-start.15 = (bf16[288,256]{1,0:T(8,128)(2,1)S(1)}, bf16[288,256]{1,0:T(8,128)(2,1)S(1)}, u32[]{:S(2)}, u32[]{:S(2)}) collective-permute-start(bf16[288,256]{1,0:T(8,128)(2,1)S(1)} %get-tuple-element.29.rest_0_), channel_id=1, source_target_pairs={{14,0},{15,1},{12,2},{13,3},{2,4},{3,5},{0,6},{1,7},{6,8},{7,9},{4... | collective-permute-start | bytes 442376 | tf_op jit(solution)/shard_map/ppermute | solution.py:80
  60.3 10.0 %collective-permute-start.12 = (bf16[288,256]{1,0:T(8,128)(2,1)S(1)}, bf16[288,256]{1,0:T(8,128)(2,1)S(1)}, u32[]{:S(2)}, u32[]{:S(2)}) collective-permute-start(bf16[288,256]{1,0:T(8,128)(2,1)S(1)} %get-tuple-element.29.rest_0_), channel_id=1, source_target_pairs={{4,0},{5,1},{6,2},{7,3},{8,4},{9,5},{10,6},{11,7},{12,8},{13,9},{1... | collective-permute-start | bytes 442376 | tf_op jit(solution)/shard_map/ppermute | solution.py:80
  60.4 10.0 %collective-permute-start.14 = (bf16[288,256]{1,0:T(8,128)(2,1)S(1)}, bf16[288,256]{1,0:T(8,128)(2,1)S(1)}, u32[]{:S(2)}, u32[]{:S(2)}) collective-permute-start(bf16[288,256]{1,0:T(8,128)(2,1)S(1)} %get-tuple-element.29.rest_0_), channel_id=1, source_target_pairs={{6,0},{7,1},{4,2},{5,3},{10,4},{11,5},{8,6},{9,7},{14,8},{15,9},{1... | collective-permute-start | bytes 442376 | tf_op jit(solution)/shard_map/ppermute | solution.py:80
  61.6 8.8 %collective-permute-start.13 = (bf16[288,256]{1,0:T(8,128)(2,1)S(1)}, bf16[288,256]{1,0:T(8,128)(2,1)S(1)}, u32[]{:S(2)}, u32[]{:S(2)}) collective-permute-start(bf16[288,256]{1,0:T(8,128)(2,1)S(1)} %get-tuple-element.29.rest_0_), channel_id=1, source_target_pairs={{12,0},{13,1},{14,2},{15,3},{0,4},{1,5},{2,6},{3,7},{4,8},{5,9},{6... | collective-permute-start | bytes 442376 | tf_op jit(solution)/shard_map/ppermute | solution.py:80
  63.8 7.6 %collective-permute-start.11 = (bf16[288,256]{1,0:T(8,128)(2,1)S(1)}, bf16[288,256]{1,0:T(8,128)(2,1)S(1)}, u32[]{:S(2)}, u32[]{:S(2)}) collective-permute-start(bf16[288,256]{1,0:T(8,128)(2,1)S(1)} %get-tuple-element.29.rest_0_), channel_id=1, source_target_pairs={{2,0},{3,1},{0,2},{1,3},{6,4},{7,5},{4,6},{5,7},{10,8},{11,9},{8,1... | collective-permute-start | bytes 442376 | tf_op jit(solution)/shard_map/ppermute | solution.py:80
  65.1 6.3 %collective-permute-start.17 = (bf16[288,256]{1,0:T(8,128)(2,1)S(1)}, bf16[288,256]{1,0:T(8,128)(2,1)S(1)}, u32[]{:S(2)}, u32[]{:S(2)}) collective-permute-start(bf16[288,256]{1,0:T(8,128)(2,1)S(1)} %collective-permute-done.15.rest_5_), channel_id=1, source_target_pairs={{12,0},{13,1},{14,2},{15,3},{0,4},{1,5},{2,6},{3,7},{4,8},{5,9},{6... | collective-permute-start | bytes 442376 | tf_op jit(solution)/shard_map/ppermute | solution.py:80
  70.4 6.4 %collective-permute-start.16 = (bf16[288,256]{1,0:T(8,128)(2,1)S(1)}, bf16[288,256]{1,0:T(8,128)(2,1)S(1)}, u32[]{:S(2)}, u32[]{:S(2)}) collective-permute-start(bf16[288,256]{1,0:T(8,128)(2,1)S(1)} %collective-permute-done.12.rest_2_), channel_id=1, source_target_pairs={{4,0},{5,1},{6,2},{7,3},{8,4},{9,5},{10,6},{11,7},{12,8},{13,9},{1... | collective-permute-start | bytes 442376 | tf_op jit(solution)/shard_map/ppermute | solution.py:80
  83.1 8.2 %copy-start.4 = (bf16[2,64,256]{2,1,0:T(8,128)(2,1)S(1)}, bf16[2,64,256]{2,1,0:T(8,128)(2,1)}, u32[]{:S(2)}) copy-start(bf16[2,64,256]{2,1,0:T(8,128)(2,1)} %own_up.1) | copy-start | bytes 196612
  84.7 1.3 %collective-permute-start.18 = (bf16[80,128]{1,0:T(8,128)(2,1)S(1)}, bf16[80,128]{1,0:T(8,128)(2,1)S(1)}, u32[]{:S(2)}, u32[]{:S(2)}) collective-permute-start(bf16[80,128]{1,0:T(8,128)(2,1)S(1)} %get-tuple-element.33), channel_id=1, source_target_pairs={{0,1},{1,0},{2,3},{3,2},{4,5},{5,4},{6,7},{7,6},{8,9},{9,8},{10,11... | collective-permute-start | bytes 61448 | tf_op jit(solution)/shard_map/ppermute | solution.py:428
  86.0 5.4 %collective-permute-start.19 = (bf16[80,128]{1,0:T(8,128)(2,1)S(1)}, bf16[80,128]{1,0:T(8,128)(2,1)S(1)}, u32[]{:S(2)}, u32[]{:S(2)}) collective-permute-start(bf16[80,128]{1,0:T(8,128)(2,1)S(1)} %add_convert_fusion.2.a), channel_id=1, source_target_pairs={{0,128},{128,0},{1,129},{129,1},{2,130},{130,2},{3,131},{131,3},{4... | collective-permute-start | bytes 61448 | tf_op jit(solution)/shard_map/ppermute | solution.py:431
Sparse Core Ops, SparseCore 0:
  10.6 42.2 all-gather.2

commit v6 on v4

--- a/solution.py
+++ b/solution.py
@@ -101,31 +101,30 @@
         return copies[-1]
 
     reads = [
-        move(hid, hid_in),
         move(up, up_in),
         move(down, mixed.at[3:5]),
         move(out_up, mixed.at[5:7]),
+        move(hid, hid_in),
     ]
     tenant[...] = jnp.full((ROWS, 4 * CHUNK), adapter[0].astype(F32)).astype(BF16)
-    reads[0].wait()
-    writes = []
+    for read in reads[:3]:
+        read.wait()
+
+    def columns(main, tail, at):
+        for t in range(2):
+            mixed[t] = up_in[t, :, main : main + CHUNK]
+            mixed[2, :, t * HEAD : (t + 1) * HEAD] = jnp.zeros((RANK, HEAD), BF16)
+            mixed[2, :, t * HEAD + at : t * HEAD + at + RANK] = up_in[t, :, tail : tail + RANK]
+
+    pl.when(core == 0)(lambda: columns(0, CHUNK, 0))
+    pl.when(core == 1)(lambda: columns(RANK, 0, RANK))
+    writes = [move(mixed, weights)]
+    reads[3].wait()
     for out, dx, dc in ((to_x, 1, 0), (to_cross, 1, 1), (to_core, 0, 1), (own, 0, 0)):
         for y in range(4):
             chunk = 4 * y + 2 * (x ^ dx) + (core ^ dc)
             writes.append(move(hid_in.at[:, aligned(chunk, CHUNK)], out.at[:BLOCK, y * CHUNK : (y + 1) * CHUNK]))
         writes.append(move(tenant, out.at[BLOCK:, :]))
-    for read in reads[1:]:
-        read.wait()
-
-    def columns(main, tail, at):
-        for t in range(2):
-            mixed[t] = up_in[t, :, main : main + CHUNK]
-            mixed[2, :, t * HEAD : (t + 1) * HEAD] = jnp.zeros((RANK, HEAD), BF16)
-            mixed[2, :, t * HEAD + at : t * HEAD + at + RANK] = up_in[t, :, tail : tail + RANK]
-
-    pl.when(core == 0)(lambda: columns(0, CHUNK, 0))
-    pl.when(core == 1)(lambda: columns(RANK, 0, RANK))
-    writes.append(move(mixed, weights))
     for write in writes:
         write.wait()
 

time: 98.5 us -> 98.6 us (level)
  no operation moved by 1% of the time
where the time goes in v6:
time: 98.6 us; the launch traced here: 98.3 us
  waiting for transfers between devices  33.6 us (34%)
  starting transfers between devices  24.9 us (25%)
  Pallas kernels  19.2 us (19%)
  between operations  14.9 us (15%)
  local copies, waits for them, and re-layouts  5.58 us (6%)
    pallas_call x7, Pallas kernels, call(): pl.pallas_call(body, grid_spec=pltpu.PrefetchScalarGridSpec(num_scalar_pr...  19.2 us
    ppermute x7, starting transfers between devices, get(): return lax.ppermute(value, 'blk', pairs)  10.7 us
    ppermute x3, waiting for transfers between devices, from_row(): return lax.ppermute(value, 'blk', pairs)  8.62 us
    ppermute x2, waiting for transfers between devices, to_role(): return lax.ppermute(value, 'role', [(0, 1), (1, 0)])  7.21 us
    ppermute x2, starting transfers between devices, to_role(): return lax.ppermute(value, 'role', [(0, 1), (1, 0)])  6.1 us
    ppermute x7, waiting for transfers between devices, get(): return lax.ppermute(value, 'blk', pairs)  5.8 us
    ppermute x2, waiting for transfers between devices, to_x(): return lax.ppermute(value, 'blk', [(i, i ^ 2) for i in range(2 * CHIPS)])  4.59 us
    unnamed x16, local copies, waits for them, and re-layouts  3.95 us
  transfers between devices with their start and end apart: 21, of which 14 were waited for; matrix products, arithmetic and copies ran while one was open for 2% of the time, Pallas kernels for 4%

profile of v6, /device:TPU:24, one launch (start us, length us, event | category | flops | bytes accessed | tf_op | source)
XLA Modules:
  0.0 98.3 jit_solution(13191703360628735723)
XLA Ops:
  7.2 0.0 all-gather.3.cloned.1.call-start
  7.9 2.6 %shard_map.131 = (bf16[144,1024]{1,0:T(8,128)(2,1)}, bf16[144,1024]{1,0:T(8,128)(2,1)}, bf16[144,1024]{1,0:T(8,128)(2,1)}, bf16[144,1024]{1,0:T(8,128)(2,1)}, bf16[7,64,256]{2,1,0:T(8,128)(2,1)}) custom-call(s32[1]{0:T(128)} %bitcast.5.place, s32[1]{0:T(128)S(6)} %copy.14.adapter, bf16[128,4096]{1,0:T(8,128)(2,1)} %hid.1, bf16[2,64,320]{2,1,0:T(8,128)(2,1)} %up.1, ...), custom_call_target="tpu_custom_call" | custom-call | tf_op jit(solution)/shard_map/pallas_call | solution.py:44
  10.5 0.0 copy-start.2
  10.5 0.0 all-gather.3.cloned.1.call-update
  10.6 0.8 collective-permute-start.4
  11.4 1.5 %collective-permute-start.2 = (bf16[144,1024]{1,0:T(8,128)(2,1)}, bf16[144,1024]{1,0:T(8,128)(2,1)S(1)}, u32[]{:S(2)}, u32[]{:S(2)}) collective-permute-start(bf16[144,1024]{1,0:T(8,128)(2,1)} %get-tuple-element.20), channel_id=1, source_target_pairs={{0,2},{1,3},{2,0},{3,1},{4,6},{5,7},{6,4},{7,5},{8,10},{9,11},{10,... | collective-permute-start | bytes 884744 | tf_op jit(solution)/shard_map/ppermute | solution.py:434
  12.9 0.6 collective-permute-start.3
  13.5 2.5 %collective-permute-start.5 = (bf16[2,192,256]{2,1,0:T(8,128)(2,1)}, bf16[2,192,256]{2,1,0:T(8,128)(2,1)}, u32[]{:S(2)}, u32[]{:S(2)}) collective-permute-start(bf16[2,192,256]{2,1,0:T(8,128)(2,1)} %bitcast.16), channel_id=1, source_target_pairs={{12,0},{13,1},{14,2},{15,3},{0,4},{1,5},{2,6},{3,7},{4,8},{5,9},{6... | collective-permute-start | bytes 589832 | tf_op jit(solution)/shard_map/ppermute | solution.py:438
  16.0 2.7 %collective-permute-done.4.w1 = bf16[2,192,256]{2,1,0:T(8,128)(2,1)S(1)} collective-permute-done((bf16[2,192,256]{2,1,0:T(8,128)(2,1)}, bf16[2,192,256]{2,1,0:T(8,128)(2,1)S(1)}, u32[]{:S(2)}, u32[]{:S(2)}) %collective-permute-start.4) | collective-permute-done | bytes 196640 | tf_op jit(solution)/shard_map/ppermute | solution.py:438
  18.7 0.0 collective-permute-start.6
  18.7 0.9 pad.8.row_hid
  19.6 0.8 concatenate.3.ids
  20.3 4.6 %collective-permute-done.5.w3 = bf16[2,192,256]{2,1,0:T(8,128)(2,1)} collective-permute-done((bf16[2,192,256]{2,1,0:T(8,128)(2,1)}, bf16[2,192,256]{2,1,0:T(8,128)(2,1)}, u32[]{:S(2)}, u32[]{:S(2)}) %collective-permute-start.5) | collective-permute-done | bytes 196640 | tf_op jit(solution)/shard_map/ppermute | solution.py:438
  24.9 1.4 %collective-permute-done.6.w2 = bf16[2,192,256]{2,1,0:T(8,128)(2,1)} collective-permute-done((bf16[2,192,256]{2,1,0:T(8,128)(2,1)}, bf16[2,192,256]{2,1,0:T(8,128)(2,1)}, u32[]{:S(2)}, u32[]{:S(2)}) %collective-permute-start.6) | collective-permute-done | bytes 196640 | tf_op jit(solution)/shard_map/ppermute | solution.py:438
  26.3 0.0 copy-start.4
  26.3 1.0 copy-done.4
  27.3 0.9 copy-done.6
  28.2 2.9 %shard_map.132 = (bf16[416,128]{1,0:T(8,128)(2,1)S(1)}, bf16[416,128]{1,0:T(8,128)(2,1)S(1)}) custom-call(s32[13]{0:T(128)S(1)} %concatenate.3.ids, bf16[144,1024]{1,0:T(8,128)(2,1)S(1)} %copy-done.4, bf16[144,1024]{1,0:T(8,128)(2,1)S(1)} %collective-permute-done.1.by_core, bf16[144,1024]{1,0:T(8,128)(2,1)S(1)} %collective-permute-done.2.by_x, ...), custom_call_target="tpu_custom_call" | custom-call | tf_op jit(solution)/shard_map/pallas_call | solution.py:44
  31.1 1.6 %collective-permute-start.7 = (bf16[416,128]{1,0:T(8,128)(2,1)S(1)}, bf16[416,128]{1,0:T(8,128)(2,1)S(1)}, u32[]{:S(2)}, u32[]{:S(2)}) collective-permute-start(bf16[416,128]{1,0:T(8,128)(2,1)S(1)} %get-tuple-element.23), channel_id=1, source_target_pairs={{0,2},{1,3},{2,0},{3,1},{4,6},{5,7},{6,4},{7,5},{8,10},{9,11},{10,... | collective-permute-start | bytes 319496 | tf_op jit(solution)/shard_map/ppermute | solution.py:434
  32.7 0.9 shard_map.133
  33.7 0.6 collective-permute-start.10
  34.2 4.6 %collective-permute-done.7 = bf16[416,128]{1,0:T(8,128)(2,1)S(1)} collective-permute-done((bf16[416,128]{1,0:T(8,128)(2,1)S(1)}, bf16[416,128]{1,0:T(8,128)(2,1)S(1)}, u32[]{:S(2)}, u32[]{:S(2)}) %collective-permute-start.7) | collective-permute-done | bytes 106528 | tf_op jit(solution)/shard_map/ppermute | solution.py:434
  38.9 0.3 collective-permute-start.8
  39.2 1.1 %collective-permute-done.8 = bf16[416,128]{1,0:T(8,128)(2,1)S(1)} collective-permute-done((bf16[416,128]{1,0:T(8,128)(2,1)S(1)}, bf16[416,128]{1,0:T(8,128)(2,1)S(1)}, u32[]{:S(2)}, u32[]{:S(2)}) %collective-permute-start.8) | collective-permute-done | bytes 106528 | tf_op jit(solution)/shard_map/ppermute | solution.py:427
  40.3 3.1 %collective-permute-start.9 = (bf16[416,128]{1,0:T(8,128)(2,1)S(1)}, bf16[416,128]{1,0:T(8,128)(2,1)S(1)}, u32[]{:S(2)}, u32[]{:S(2)}) collective-permute-start(bf16[416,128]{1,0:T(8,128)(2,1)S(1)} %add_convert_fusion.mine), channel_id=1, source_target_pairs={{0,128},{128,0},{1,129},{129,1},{2,130},{130,2},{3,131},{131,3},{4... | collective-permute-start | bytes 319496 | tf_op jit(solution)/shard_map/ppermute | solution.py:430
  43.4 1.2 %collective-permute-done.oth = s32[1]{0:T(128)} collective-permute-done((s32[1]{0:T(128)}, s32[1]{0:T(128)}, u32[]{:S(2)}, u32[]{:S(2)}) %collective-permute-start) | collective-permute-done | bytes 36 | tf_op jit(solution)/shard_map/ppermute | solution.py:427
  44.6 4.9 %collective-permute-done.9.theirs = bf16[416,128]{1,0:T(8,128)(2,1)S(1)} collective-permute-done((bf16[416,128]{1,0:T(8,128)(2,1)S(1)}, bf16[416,128]{1,0:T(8,128)(2,1)S(1)}, u32[]{:S(2)}, u32[]{:S(2)}) %collective-permute-start.9) | collective-permute-done | bytes 106528 | tf_op jit(solution)/shard_map/ppermute | solution.py:430
  49.5 3.9 %all-gather.3.cloned.1.call-done = bf16[112,64,256]{2,1,0:T(8,128)(2,1)} async-done(((bf16[7,64,256]{2,1,0:T(8,128)(2,1)}), bf16[112,64,256]{2,1,0:T(8,128)(2,1)}) %all-gather.3.cloned.1.call-update) | async-done | bytes 3670032 | tf_op jit(solution)/shard_map/all_gather | solution.py:457
  53.4 2.0 %copy-done = bf16[112,64,256]{2,1,0:T(8,128)(2,1)S(1)} copy-done((bf16[112,64,256]{2,1,0:T(8,128)(2,1)S(1)}, bf16[112,64,256]{2,1,0:T(8,128)(2,1)}, u32[]{:S(2)}) %copy-start) | copy-done | bytes 3670040
  55.4 2.8 %shard_map.134 = (bf16[256,1024]{1,0:T(8,128)(2,1)S(1)}, bf16[288,256]{1,0:T(8,128)(2,1)S(1)}) custom-call(s32[13]{0:T(128)S(1)} %concatenate.3.ids, s32[1]{0:T(128)} %collective-permute-done.oth, bf16[416,128]{1,0:T(8,128)(2,1)S(1)} %add_convert_fusion.mine, bf16[416,128]{1,0:T(8,128)(2,1)S(1)} %collective-permute-done.9.theirs, ...), custom_call_target="tpu_custom_call" | custom-call | tf_op jit(solution)/shard_map/pallas_call | solution.py:44
  58.2 1.2 %collective-permute-start.12 = (bf16[288,256]{1,0:T(8,128)(2,1)S(1)}, bf16[288,256]{1,0:T(8,128)(2,1)S(1)}, u32[]{:S(2)}, u32[]{:S(2)}) collective-permute-start(bf16[288,256]{1,0:T(8,128)(2,1)S(1)} %get-tuple-element.29.rest_0_), channel_id=1, source_target_pairs={{4,0},{5,1},{6,2},{7,3},{8,4},{9,5},{10,6},{11,7},{12,8},{13,9},{1... | collective-permute-start | bytes 442376 | tf_op jit(solution)/shard_map/ppermute | solution.py:80
  59.4 2.7 %collective-permute-start.15 = (bf16[288,256]{1,0:T(8,128)(2,1)S(1)}, bf16[288,256]{1,0:T(8,128)(2,1)S(1)}, u32[]{:S(2)}, u32[]{:S(2)}) collective-permute-start(bf16[288,256]{1,0:T(8,128)(2,1)S(1)} %get-tuple-element.29.rest_0_), channel_id=1, source_target_pairs={{14,0},{15,1},{12,2},{13,3},{2,4},{3,5},{0,6},{1,7},{6,8},{7,9},{4... | collective-permute-start | bytes 442376 | tf_op jit(solution)/shard_map/ppermute | solution.py:80
  62.1 0.8 collective-permute-start.11
  63.0 0.2 collective-permute-start.13
  63.1 2.5 %collective-permute-start.14 = (bf16[288,256]{1,0:T(8,128)(2,1)S(1)}, bf16[288,256]{1,0:T(8,128)(2,1)S(1)}, u32[]{:S(2)}, u32[]{:S(2)}) collective-permute-start(bf16[288,256]{1,0:T(8,128)(2,1)S(1)} %get-tuple-element.29.rest_0_), channel_id=1, source_target_pairs={{6,0},{7,1},{4,2},{5,3},{10,4},{11,5},{8,6},{9,7},{14,8},{15,9},{1... | collective-permute-start | bytes 442376 | tf_op jit(solution)/shard_map/ppermute | solution.py:80
  65.6 0.0 collective-permute-start.16
  65.6 1.4 %collective-permute-done.15.rest_5_ = bf16[288,256]{1,0:T(8,128)(2,1)S(1)} collective-permute-done((bf16[288,256]{1,0:T(8,128)(2,1)S(1)}, bf16[288,256]{1,0:T(8,128)(2,1)S(1)}, u32[]{:S(2)}, u32[]{:S(2)}) %collective-permute-start.15) | collective-permute-done | bytes 147488 | tf_op jit(solution)/shard_map/ppermute | solution.py:80
  67.1 3.3 %collective-permute-start.17 = (bf16[288,256]{1,0:T(8,128)(2,1)S(1)}, bf16[288,256]{1,0:T(8,128)(2,1)S(1)}, u32[]{:S(2)}, u32[]{:S(2)}) collective-permute-start(bf16[288,256]{1,0:T(8,128)(2,1)S(1)} %collective-permute-done.15.rest_5_), channel_id=1, source_target_pairs={{12,0},{13,1},{14,2},{15,3},{0,4},{1,5},{2,6},{3,7},{4,8},{5,9},{6... | collective-permute-start | bytes 442376 | tf_op jit(solution)/shard_map/ppermute | solution.py:80
  70.4 0.5 collective-permute-done.11.rest_1_
  70.9 1.8 %collective-permute-done.14.rest_4_ = bf16[288,256]{1,0:T(8,128)(2,1)S(1)} collective-permute-done((bf16[288,256]{1,0:T(8,128)(2,1)S(1)}, bf16[288,256]{1,0:T(8,128)(2,1)S(1)}, u32[]{:S(2)}, u32[]{:S(2)}) %collective-permute-start.14) | collective-permute-done | bytes 147488 | tf_op jit(solution)/shard_map/ppermute | solution.py:80
  72.6 2.1 %collective-permute-done.16.rest_6_ = bf16[288,256]{1,0:T(8,128)(2,1)S(1)} collective-permute-done((bf16[288,256]{1,0:T(8,128)(2,1)S(1)}, bf16[288,256]{1,0:T(8,128)(2,1)S(1)}, u32[]{:S(2)}, u32[]{:S(2)}) %collective-permute-start.16) | collective-permute-done | bytes 147488 | tf_op jit(solution)/shard_map/ppermute | solution.py:80
  74.8 6.4 %shard_map.135 = (bf16[256,1024]{1,0:T(8,128)(2,1)S(1)}, f32[16,1024]{1,0:T(8,128)S(1)}) custom-call(s32[13]{0:T(128)S(1)} %concatenate.3.ids, bf16[256,1024]{1,0:T(8,128)(2,1)S(1)} %get-tuple-element.28.q, bf16[288,256]{1,0:T(8,128)(2,1)S(1)} %get-tuple-element.29.rest_0_, bf16[288,256]{1,0:T(8,128)(2,1)S(1)} %collective-permute-done.11.rest_1_, ...), custom_call_target="tpu_custom_call" | custom-call | tf_op jit(solution)/shard_map/pallas_call | solution.py:44
  81.1 1.6 %shard_map.136 = (bf16[80,128]{1,0:T(8,128)(2,1)S(1)}, bf16[80,128]{1,0:T(8,128)(2,1)S(1)}) custom-call(s32[13]{0:T(128)S(1)} %concatenate.3.ids, s32[1]{0:T(128)} %collective-permute-done.oth, bf16[256,1024]{1,0:T(8,128)(2,1)S(1)} %get-tuple-element.30.ctx, f32[16,1024]{1,0:T(8,128)S(1)} %get-tuple-element.31.row_ctx, ...), custom_call_target="tpu_custom_call" | custom-call | tf_op jit(solution)/shard_map/pallas_call | solution.py:44
  82.8 0.1 collective-permute-start.18
  82.9 1.2 %collective-permute-done.18 = bf16[80,128]{1,0:T(8,128)(2,1)S(1)} collective-permute-done((bf16[80,128]{1,0:T(8,128)(2,1)S(1)}, bf16[80,128]{1,0:T(8,128)(2,1)S(1)}, u32[]{:S(2)}, u32[]{:S(2)}) %collective-permute-start.18) | collective-permute-done | bytes 20512 | tf_op jit(solution)/shard_map/ppermute | solution.py:427
  84.1 3.0 %collective-permute-start.19 = (bf16[80,128]{1,0:T(8,128)(2,1)S(1)}, bf16[80,128]{1,0:T(8,128)(2,1)S(1)}, u32[]{:S(2)}, u32[]{:S(2)}) collective-permute-start(bf16[80,128]{1,0:T(8,128)(2,1)S(1)} %add_convert_fusion.2.a), channel_id=1, source_target_pairs={{0,128},{128,0},{1,129},{129,1},{2,130},{130,2},{3,131},{131,3},{4... | collective-permute-start | bytes 61448 | tf_op jit(solution)/shard_map/ppermute | solution.py:430
  87.1 2.3 %collective-permute-done.19.b = bf16[80,128]{1,0:T(8,128)(2,1)S(1)} collective-permute-done((bf16[80,128]{1,0:T(8,128)(2,1)S(1)}, bf16[80,128]{1,0:T(8,128)(2,1)S(1)}, u32[]{:S(2)}, u32[]{:S(2)}) %collective-permute-start.19) | collective-permute-done | bytes 20512 | tf_op jit(solution)/shard_map/ppermute | solution.py:430
  89.4 2.0 %shard_map.137 = (bf16[128,4096]{1,0:T(8,128)(2,1)}, bf16[4,256]{1,0:T(4,128)(2,1)}) custom-call(s32[13]{0:T(128)S(1)} %concatenate.3.ids, bf16[80,128]{1,0:T(8,128)(2,1)S(1)} %add_convert_fusion.2.a, bf16[80,128]{1,0:T(8,128)(2,1)S(1)} %collective-permute-done.19.b, bf16[16,7,64,256]{3,2,1,0:T(8,128)(2,1)S(1)} %bitcast.14, bf16[2,64,256]{2,1,0:T(8,128)(2,1)S(1)} %copy-done.5), custom_call_target="tpu_custom_call" | custom-call | tf_op jit(solution)/shard_map/pallas_call | solution.py:44
  (24 shorter events, 0.1 us)
Async XLA Ops:
  7.2 25.6 %copy-start.3 = (bf16[3,128,1024]{2,1,0:T(8,128)(2,1)S(1)}, bf16[3,128,1024]{2,1,0:T(8,128)(2,1)}, u32[]{:S(2)}) copy-start(bf16[3,128,1024]{2,1,0:T(8,128)(2,1)} %cache.1) | copy-start | bytes 2359300
  7.2 36.2 %copy-start.7 = (bf16[4,5120]{1,0:T(4,128)(2,1)S(1)}, bf16[4,5120]{1,0:T(4,128)(2,1)}, u32[]{:S(2)}) copy-start(bf16[4,5120]{1,0:T(4,128)(2,1)} %param.16) | copy-start | bytes 122884
  7.2 46.2 %all-gather.3.cloned.1.call-start = ((), (), s32[]{:S(2)}) async-start(), calls=%async_computation | async-start | bytes 3899392 | tf_op jit(solution)/shard_map/all_gather | solution.py:457
  10.5 22.2 %copy-start.2 = (bf16[128,5120]{1,0:T(8,128)(2,1)S(1)}, bf16[128,5120]{1,0:T(8,128)(2,1)}, u32[]{:S(2)}) copy-start(bf16[128,5120]{1,0:T(8,128)(2,1)} %qkv.1) | copy-start | bytes 3932164
  10.6 8.1 %collective-permute-start.4 = (bf16[2,192,256]{2,1,0:T(8,128)(2,1)}, bf16[2,192,256]{2,1,0:T(8,128)(2,1)S(1)}, u32[]{:S(2)}, u32[]{:S(2)}) collective-permute-start(bf16[2,192,256]{2,1,0:T(8,128)(2,1)} %bitcast.15), channel_id=1, source_target_pairs={{4,0},{5,1},{6,2},{7,3},{8,4},{9,5},{10,6},{11,7},{12,8},{13,9},{1... | collective-permute-start | bytes 589832 | tf_op jit(solution)/shard_map/ppermute | solution.py:438
  11.4 14.9 %collective-permute-start.2 = (bf16[144,1024]{1,0:T(8,128)(2,1)}, bf16[144,1024]{1,0:T(8,128)(2,1)S(1)}, u32[]{:S(2)}, u32[]{:S(2)}) collective-permute-start(bf16[144,1024]{1,0:T(8,128)(2,1)} %get-tuple-element.20), channel_id=1, source_target_pairs={{0,2},{1,3},{2,0},{3,1},{4,6},{5,7},{6,4},{7,5},{8,10},{9,11},{10,... | collective-permute-start | bytes 884744 | tf_op jit(solution)/shard_map/ppermute | solution.py:434
  12.9 13.4 %collective-permute-start.1 = (bf16[144,1024]{1,0:T(8,128)(2,1)}, bf16[144,1024]{1,0:T(8,128)(2,1)S(1)}, u32[]{:S(2)}, u32[]{:S(2)}) collective-permute-start(bf16[144,1024]{1,0:T(8,128)(2,1)} %get-tuple-element.19), channel_id=1, source_target_pairs={{0,1},{1,0},{2,3},{3,2},{4,5},{5,4},{6,7},{7,6},{8,9},{9,8},{10,11... | collective-permute-start | bytes 884744 | tf_op jit(solution)/shard_map/ppermute | solution.py:427
  12.9 13.4 %collective-permute-start.3 = (bf16[144,1024]{1,0:T(8,128)(2,1)}, bf16[144,1024]{1,0:T(8,128)(2,1)S(1)}, u32[]{:S(2)}, u32[]{:S(2)}) collective-permute-start(bf16[144,1024]{1,0:T(8,128)(2,1)} %get-tuple-element.21), channel_id=1, source_target_pairs={{0,3},{1,2},{2,1},{3,0},{4,7},{5,6},{6,5},{7,4},{8,11},{9,10},{10,... | collective-permute-start | bytes 884744 | tf_op jit(solution)/shard_map/ppermute | solution.py:458
  13.5 11.4 %collective-permute-start.5 = (bf16[2,192,256]{2,1,0:T(8,128)(2,1)}, bf16[2,192,256]{2,1,0:T(8,128)(2,1)}, u32[]{:S(2)}, u32[]{:S(2)}) collective-permute-start(bf16[2,192,256]{2,1,0:T(8,128)(2,1)} %bitcast.16), channel_id=1, source_target_pairs={{12,0},{13,1},{14,2},{15,3},{0,4},{1,5},{2,6},{3,7},{4,8},{5,9},{6... | collective-permute-start | bytes 589832 | tf_op jit(solution)/shard_map/ppermute | solution.py:438
  18.7 7.6 %collective-permute-start.6 = (bf16[2,192,256]{2,1,0:T(8,128)(2,1)}, bf16[2,192,256]{2,1,0:T(8,128)(2,1)}, u32[]{:S(2)}, u32[]{:S(2)}) collective-permute-start(bf16[2,192,256]{2,1,0:T(8,128)(2,1)} %bitcast.17), channel_id=1, source_target_pairs={{8,0},{9,1},{10,2},{11,3},{12,4},{13,5},{14,6},{15,7},{0,8},{1,9},... | collective-permute-start | bytes 589832 | tf_op jit(solution)/shard_map/ppermute | solution.py:438
  26.3 1.0 copy-start.4
  27.3 0.9 copy-start.6
  31.1 7.7 %collective-permute-start.7 = (bf16[416,128]{1,0:T(8,128)(2,1)S(1)}, bf16[416,128]{1,0:T(8,128)(2,1)S(1)}, u32[]{:S(2)}, u32[]{:S(2)}) collective-permute-start(bf16[416,128]{1,0:T(8,128)(2,1)S(1)} %get-tuple-element.23), channel_id=1, source_target_pairs={{0,2},{1,3},{2,0},{3,1},{4,6},{5,7},{6,4},{7,5},{8,10},{9,11},{10,... | collective-permute-start | bytes 319496 | tf_op jit(solution)/shard_map/ppermute | solution.py:434
  33.7 15.8 %collective-permute-start.10 = (bf16[128,2048]{1,0:T(8,128)(2,1)S(1)}, bf16[128,2048]{1,0:T(8,128)(2,1)S(1)}, u32[]{:S(2)}, u32[]{:S(2)}) collective-permute-start(bf16[128,2048]{1,0:T(8,128)(2,1)S(1)} %get-tuple-element.26), channel_id=1, source_target_pairs={{0,1},{1,0},{2,3},{3,2},{4,5},{5,4},{6,7},{7,6},{8,9},{9,8},{10,11... | collective-permute-start | bytes 1572872 | tf_op jit(solution)/shard_map/ppermute | solution.py:427
  38.9 1.4 %collective-permute-start.8 = (bf16[416,128]{1,0:T(8,128)(2,1)S(1)}, bf16[416,128]{1,0:T(8,128)(2,1)S(1)}, u32[]{:S(2)}, u32[]{:S(2)}) collective-permute-start(bf16[416,128]{1,0:T(8,128)(2,1)S(1)} %add_convert_fusion.1), channel_id=1, source_target_pairs={{0,1},{1,0},{2,3},{3,2},{4,5},{5,4},{6,7},{7,6},{8,9},{9,8},{10,11... | collective-permute-start | bytes 319496 | tf_op jit(solution)/shard_map/ppermute | solution.py:427
  40.3 9.2 %collective-permute-start.9 = (bf16[416,128]{1,0:T(8,128)(2,1)S(1)}, bf16[416,128]{1,0:T(8,128)(2,1)S(1)}, u32[]{:S(2)}, u32[]{:S(2)}) collective-permute-start(bf16[416,128]{1,0:T(8,128)(2,1)S(1)} %add_convert_fusion.mine), channel_id=1, source_target_pairs={{0,128},{128,0},{1,129},{129,1},{2,130},{130,2},{3,131},{131,3},{4... | collective-permute-start | bytes 319496 | tf_op jit(solution)/shard_map/ppermute | solution.py:430
  43.4 1.2 %collective-permute-start = (s32[1]{0:T(128)}, s32[1]{0:T(128)}, u32[]{:S(2)}, u32[]{:S(2)}) collective-permute-start(s32[1]{0:T(128)} %param.14), channel_id=1, source_target_pairs={{0,1},{1,0},{2,3},{3,2},{4,5},{5,4},{6,7},{7,6},{8,9},{9,8},{10,11... | collective-permute-start | bytes 20 | tf_op jit(solution)/shard_map/ppermute | solution.py:427
  53.4 2.0 %copy-start = (bf16[112,64,256]{2,1,0:T(8,128)(2,1)S(1)}, bf16[112,64,256]{2,1,0:T(8,128)(2,1)}, u32[]{:S(2)}) copy-start(bf16[112,64,256]{2,1,0:T(8,128)(2,1)} %all-gather.3.cloned.1.call-done) | copy-start | bytes 11010052
  55.4 25.7 %copy-start.1 = (bf16[112,64,256]{2,1,0:T(8,128)(2,1)S(1)}, bf16[112,64,256]{2,1,0:T(8,128)(2,1)}, u32[]{:S(2)}) copy-start(bf16[112,64,256]{2,1,0:T(8,128)(2,1)} %all-gather.3.cloned.1.call-done) | copy-start | bytes 11010052
  58.2 7.4 %collective-permute-start.12 = (bf16[288,256]{1,0:T(8,128)(2,1)S(1)}, bf16[288,256]{1,0:T(8,128)(2,1)S(1)}, u32[]{:S(2)}, u32[]{:S(2)}) collective-permute-start(bf16[288,256]{1,0:T(8,128)(2,1)S(1)} %get-tuple-element.29.rest_0_), channel_id=1, source_target_pairs={{4,0},{5,1},{6,2},{7,3},{8,4},{9,5},{10,6},{11,7},{12,8},{13,9},{1... | collective-permute-start | bytes 442376 | tf_op jit(solution)/shard_map/ppermute | solution.py:80
  59.4 7.6 %collective-permute-start.15 = (bf16[288,256]{1,0:T(8,128)(2,1)S(1)}, bf16[288,256]{1,0:T(8,128)(2,1)S(1)}, u32[]{:S(2)}, u32[]{:S(2)}) collective-permute-start(bf16[288,256]{1,0:T(8,128)(2,1)S(1)} %get-tuple-element.29.rest_0_), channel_id=1, source_target_pairs={{14,0},{15,1},{12,2},{13,3},{2,4},{3,5},{0,6},{1,7},{6,8},{7,9},{4... | collective-permute-start | bytes 442376 | tf_op jit(solution)/shard_map/ppermute | solution.py:80
  62.1 8.7 %collective-permute-start.11 = (bf16[288,256]{1,0:T(8,128)(2,1)S(1)}, bf16[288,256]{1,0:T(8,128)(2,1)S(1)}, u32[]{:S(2)}, u32[]{:S(2)}) collective-permute-start(bf16[288,256]{1,0:T(8,128)(2,1)S(1)} %get-tuple-element.29.rest_0_), channel_id=1, source_target_pairs={{2,0},{3,1},{0,2},{1,3},{6,4},{7,5},{4,6},{5,7},{10,8},{11,9},{8,1... | collective-permute-start | bytes 442376 | tf_op jit(solution)/shard_map/ppermute | solution.py:80
  63.0 7.9 %collective-permute-start.13 = (bf16[288,256]{1,0:T(8,128)(2,1)S(1)}, bf16[288,256]{1,0:T(8,128)(2,1)S(1)}, u32[]{:S(2)}, u32[]{:S(2)}) collective-permute-start(bf16[288,256]{1,0:T(8,128)(2,1)S(1)} %get-tuple-element.29.rest_0_), channel_id=1, source_target_pairs={{12,0},{13,1},{14,2},{15,3},{0,4},{1,5},{2,6},{3,7},{4,8},{5,9},{6... | collective-permute-start | bytes 442376 | tf_op jit(solution)/shard_map/ppermute | solution.py:80
  63.1 9.5 %collective-permute-start.14 = (bf16[288,256]{1,0:T(8,128)(2,1)S(1)}, bf16[288,256]{1,0:T(8,128)(2,1)S(1)}, u32[]{:S(2)}, u32[]{:S(2)}) collective-permute-start(bf16[288,256]{1,0:T(8,128)(2,1)S(1)} %get-tuple-element.29.rest_0_), channel_id=1, source_target_pairs={{6,0},{7,1},{4,2},{5,3},{10,4},{11,5},{8,6},{9,7},{14,8},{15,9},{1... | collective-permute-start | bytes 442376 | tf_op jit(solution)/shard_map/ppermute | solution.py:80
  65.6 9.2 %collective-permute-start.16 = (bf16[288,256]{1,0:T(8,128)(2,1)S(1)}, bf16[288,256]{1,0:T(8,128)(2,1)S(1)}, u32[]{:S(2)}, u32[]{:S(2)}) collective-permute-start(bf16[288,256]{1,0:T(8,128)(2,1)S(1)} %collective-permute-done.12.rest_2_), channel_id=1, source_target_pairs={{4,0},{5,1},{6,2},{7,3},{8,4},{9,5},{10,6},{11,7},{12,8},{13,9},{1... | collective-permute-start | bytes 442376 | tf_op jit(solution)/shard_map/ppermute | solution.py:80
  67.1 7.7 %collective-permute-start.17 = (bf16[288,256]{1,0:T(8,128)(2,1)S(1)}, bf16[288,256]{1,0:T(8,128)(2,1)S(1)}, u32[]{:S(2)}, u32[]{:S(2)}) collective-permute-start(bf16[288,256]{1,0:T(8,128)(2,1)S(1)} %collective-permute-done.15.rest_5_), channel_id=1, source_target_pairs={{12,0},{13,1},{14,2},{15,3},{0,4},{1,5},{2,6},{3,7},{4,8},{5,9},{6... | collective-permute-start | bytes 442376 | tf_op jit(solution)/shard_map/ppermute | solution.py:80
  81.1 8.3 %copy-start.5 = (bf16[2,64,256]{2,1,0:T(8,128)(2,1)S(1)}, bf16[2,64,256]{2,1,0:T(8,128)(2,1)}, u32[]{:S(2)}) copy-start(bf16[2,64,256]{2,1,0:T(8,128)(2,1)} %own_up.1) | copy-start | bytes 196612
  82.8 1.3 %collective-permute-start.18 = (bf16[80,128]{1,0:T(8,128)(2,1)S(1)}, bf16[80,128]{1,0:T(8,128)(2,1)S(1)}, u32[]{:S(2)}, u32[]{:S(2)}) collective-permute-start(bf16[80,128]{1,0:T(8,128)(2,1)S(1)} %get-tuple-element.33), channel_id=1, source_target_pairs={{0,1},{1,0},{2,3},{3,2},{4,5},{5,4},{6,7},{7,6},{8,9},{9,8},{10,11... | collective-permute-start | bytes 61448 | tf_op jit(solution)/shard_map/ppermute | solution.py:427
  84.1 5.4 %collective-permute-start.19 = (bf16[80,128]{1,0:T(8,128)(2,1)S(1)}, bf16[80,128]{1,0:T(8,128)(2,1)S(1)}, u32[]{:S(2)}, u32[]{:S(2)}) collective-permute-start(bf16[80,128]{1,0:T(8,128)(2,1)S(1)} %add_convert_fusion.2.a), channel_id=1, source_target_pairs={{0,128},{128,0},{1,129},{129,1},{2,130},{130,2},{3,131},{131,3},{4... | collective-permute-start | bytes 61448 | tf_op jit(solution)/shard_map/ppermute | solution.py:430
Sparse Core Ops, SparseCore 0:
  10.7 42.6 all-gather.2
